TPU v7x, 32 devices: a whole 2x2x4 slice. The times are simulated.
32 devices in a mesh: rows: 16 (over z, y, x), rep: 2 (over core).
Axes of the slice: x: 2, y: 2, z: 4, core: 2. Of those that a mesh axis runs over, the one named last changes fastest.
Arguments:
- features: bfloat16 [4096, 128], P('rows'), may hold values from -6 to 6
- weight: bfloat16 [128, 256], replicated, may hold values from -0.5 to 0.5
- bias: float32 [256], replicated, may hold values from -3 to 3
- block_count: int32 [2, 64], P('rep', 'rows'), may hold values from 1 to 16, as said below
- block_cols: int32 [2, 64, 16], P('rep', 'rows'), may hold values from 0 to 31, as said below
- block_vals: bfloat16 [2, 64, 16, 4096], P('rep', 'rows'), may hold values from -0.375 to 0.375
- cotangent: bfloat16 [4096, 256], P(('rows', 'rep')), may hold values from -0.1875 to 0.1875
Outputs:
- activated: bfloat16 [4096, 256], P(('rows', 'rep'))
- weight_grad: float32 [128, 256], P(None, 'rows')
- bias_grad: float32 [256], P('rows')
Inputs may be any that keep to these rules, and one draw needn't show every extreme that they name: `block_count`: every draw has a block row with exactly 16 blocks in each half; counts are skewed by node range. `block_cols`: the column blocks of one block row and half are all different; slots at or beyond the count are ignored. Within one half, all column blocks c named by the block rows of one index of rows that share c // 2 are the same block.
All inputs are finite; a program needn't handle non-finite values.
Results may differ from a plain program's by a relative error of at most 0.0085.
Values may be sent and summed in bfloat16 or wider, within the bound.
No kernel may reach another device: no remote copies, remote signals or barrier semaphores. Data moves between devices by JAX's collectives and lax.ppermute only.
A program may use at most 64 MiB of HBM per device.

v0:
```python
import jax
import jax.numpy as jnp
from jax import lax
from jax.sharding import PartitionSpec as P

group_width = 8


def aggregate(feat_blocks, counts, cols, tiles):
    nblocks = counts.shape[0]
    width = feat_blocks.shape[2]
    turns = (jnp.max(counts) + group_width - 1) // group_width

    def step(turn, acc):
        start = turn * group_width
        cols_now = lax.dynamic_slice_in_dim(cols, start, group_width, 1)
        tiles_now = lax.dynamic_slice_in_dim(tiles, start, group_width, 1).reshape(
            nblocks, group_width, 64, 64
        )
        slot_ids = start + jnp.arange(group_width, dtype=jnp.int32)
        keep = slot_ids[None, :] < counts[:, None]
        tiles_now = jnp.where(keep[:, :, None, None], tiles_now, jnp.zeros_like(tiles_now))
        gathered = feat_blocks[cols_now]
        return acc + jnp.einsum(
            "bkij,bkjf->bif", tiles_now, gathered, preferred_element_type=jnp.float32
        )

    start_acc = jnp.zeros((nblocks, 64, width), jnp.float32)
    return lax.fori_loop(0, turns, step, start_acc)


def body(features, weight, bias, block_count, block_cols, block_vals, cotangent):
    node_rows = features.shape[0]
    width = features.shape[1]
    half_blocks = node_rows // 128
    slots = block_cols.shape[2]
    side = lax.axis_index("rep")
    owners_all = lax.axis_size("rows")
    counts = block_count[0]
    cols = block_cols[0]
    owners = cols // half_blocks
    within = cols % half_blocks
    active = jnp.arange(slots, dtype=jnp.int32)[None, :] < counts[:, None]
    matches = (
        owners[:, :, None] == jnp.arange(owners_all, dtype=jnp.int32)[None, None, :]
    ) & active[:, :, None]
    wanted = jnp.max(jnp.where(matches, within[:, :, None], -1), axis=(0, 1))
    requested = lax.all_to_all(wanted, "rows", split_axis=0, concat_axis=0, tiled=True)
    own_blocks = features.reshape(2 * half_blocks, 64, width)
    picked = own_blocks[side * half_blocks + jnp.maximum(requested, 0)]
    picked = jnp.where((requested >= 0)[:, None, None], picked, jnp.zeros_like(picked))
    fetched = lax.all_to_all(picked, "rows", split_axis=0, concat_axis=0, tiled=True)
    partial_sum = aggregate(fetched, counts, owners, block_vals[0])
    partial_sum = partial_sum.reshape(node_rows, width)
    aggregated = lax.psum_scatter(partial_sum, "rep", scatter_dimension=0, tiled=True).astype(
        jnp.bfloat16
    )
    pre = jnp.dot(aggregated, weight, preferred_element_type=jnp.float32) + bias
    activated = jax.nn.silu(pre).astype(jnp.bfloat16)
    sig = jax.nn.sigmoid(pre)
    delta = (cotangent.astype(jnp.float32) * sig * (1.0 + pre * (1.0 - sig))).astype(jnp.bfloat16)
    weight_term = jnp.einsum("nf,no->fo", aggregated, delta, preferred_element_type=jnp.float32)
    bias_term = jnp.sum(delta.astype(jnp.float32), axis=0)
    weight_part, bias_part = (
        lax.psum_scatter(weight_term, "rows", scatter_dimension=1, tiled=True),
        lax.psum_scatter(bias_term, "rows", scatter_dimension=0, tiled=True),
    )
    weight_grad, bias_grad = lax.psum((weight_part, bias_part), "rep")
    return (activated, weight_grad, bias_grad)


def solution(mesh):
    placed = (
        P("rows", None),
        P(),
        P(),
        P("rep", "rows"),
        P("rep", "rows", None),
        P("rep", "rows", None, None),
        P(("rows", "rep"), None),
    )
    return jax.shard_map(
        body,
        mesh=mesh,
        in_specs=placed,
        out_specs=(P(("rows", "rep"), None), P(None, "rows"), P("rows")),
        check_vma=False,
    )
```

profile of v0, /device:TPU:0, one launch (start us, length us, event | category | flops | bytes accessed | tf_op | source)
XLA Modules:
  0.0 138.7 jit_solution(5454632545059774460)
XLA Ops:
  7.2 0.0 copy-start
  7.2 0.0 copy-start.8
  7.2 0.0 copy-start.4
  7.2 0.7 copy-done.8
  7.9 0.1 iota_compare_fusion.1
  7.9 0.0 copy-done.4
  8.0 0.1 select_reduce_fusion
  8.1 0.7 copy.12
  8.8 8.3 %all-to-all-start = ((s32[16,1,1]{2,1,0:T(1,128)}), s32[16,1,1]{2,1,0:T(1,128)S(1)}, u32[]{:S(2)}, u32[]{:S(2)}) async-start(s32[16,1,1]{2,1,0:T(1,128)} %copy.12), calls=%async_computation | async-start | bytes 16384 | tf_op jit(solution)/shard_map/all_to_all | solution.py:48
  17.1 7.2 %all-to-all-done = s32[16,1,1]{2,1,0:T(1,128)S(1)} async-done(((s32[16,1,1]{2,1,0:T(1,128)}), s32[16,1,1]{2,1,0:T(1,128)S(1)}, u32[]{:S(2)}, u32[]{:S(2)}) %all-to-all-start) | async-done | bytes 96 | tf_op jit(solution)/shard_map/all_to_all | solution.py:48
  24.3 0.4 add_reduce_fusion
  24.7 0.0 copy-done
  24.7 0.6 gather_fusion.1
  25.3 0.4 compare_reduce_fusion
  25.7 0.0 copy-start.1
  25.7 0.8 broadcast_select_fusion
  26.5 3.5 %all-to-all-start.1 = ((bf16[16,64,128]{2,1,0:T(8,128)(2,1)}), bf16[16,64,128]{2,1,0:T(8,128)(2,1)S(1)}, u32[]{:S(2)}, u32[]{:S(2)}) async-start(bf16[16,64,128]{2,1,0:T(8,128)(2,1)} %broadcast_select_fusion), calls=%async_computation.1 | async-start | bytes 524288 | tf_op jit(solution)/shard_map/all_to_all | solution.py:52
  30.0 0.0 reduce-scatter.3.cloned.1.call-start
  30.0 0.6 reduce_max.18
  31.4 7.1 %all-to-all-done.1 = bf16[16,64,128]{2,1,0:T(8,128)(2,1)S(1)} async-done(((bf16[16,64,128]{2,1,0:T(8,128)(2,1)}), bf16[16,64,128]{2,1,0:T(8,128)(2,1)S(1)}, u32[]{:S(2)}, u32[]{:S(2)}) %all-to-all-start.1) | async-done | bytes 262176 | tf_op jit(solution)/shard_map/all_to_all | solution.py:52
  38.5 0.0 copy-done.1
  38.5 0.0 copy-start.7
  38.5 3.7 %while.10 = (s32[]{:T(128)}, f32[4,64,128]{2,1,0:T(8,128)S(1)}, s32[]{:T(128)}, s32[1,4]{1,0:T(1,128)S(1)}, bf16[4,16,4096]{2,1,0:T(8,128)(2,1)S(1)}, /*index=5*...) while((s32[]{:T(128)}, f32[4,64,128]{2,1,0:T(8,128)S(1)}, ...), condition=%wide.region_3.4_spmd, body=%wide.region_2.3_spmd.sunk | while | flops 33719436 | bytes 3150903 | solution.py:29
  38.5 0.1 broadcast_compare_fusion.3
  38.6 0.1 compare_select_fusion.3
  38.7 0.1 reshape.182
  38.8 0.5 reshape.183
  39.3 0.6 gather_fusion
  40.0 0.4 fusion.20
  40.4 0.1 broadcast_compare_fusion.3
  40.5 0.1 compare_select_fusion.3
  40.5 0.1 reshape.182
  40.7 0.5 reshape.183
  41.2 0.6 gather_fusion
  41.9 0.4 fusion.20
  42.2 0.0 copy-start.2
  42.2 0.0 copy-start.5
  42.3 0.0 copy-start.6
  42.3 0.6 copy-done.2
  42.9 0.0 reduce-scatter.3.cloned.1.call-update
  42.9 0.0 reduce-scatter.5.cloned.1.call-start
  42.9 5.7 %reduce-scatter.3.cloned.1.call-done = f32[128,128]{1,0:T(8,128)} async-done(((f32[256,128]{1,0:T(8,128)}), f32[128,128]{1,0:T(8,128)}) %reduce-scatter.3.cloned.1.call-update) | async-done | bytes 65552 | tf_op jit(solution)/shard_map/reduce_scatter | solution.py:55
  48.7 0.0 copy-done.7
  48.7 0.0 copy-done.5
  48.7 0.0 copy-done.6
  48.7 0.0 copy-start.3
  48.7 1.7 %convert_reduce_fusion = (f32[256]{0:T(256)S(1)}, bf16[128,256]{1,0:T(8,128)(2,1)S(1)}, bf16[128,256]{1,0:T(8,128)(2,1)}) fusion(bf16[128,256]{1,0:T(8,128)(2,1)S(1)} %copy-done.5, f32[256]{0:T(256)S(1)} %copy-done.7, bf16[128,256]{1,0:T(8,128)(2,1)S(1)} %copy-done.6, f32[128,128]{1,0:T(8,128)} %reduce-scatter.3.cloned.1.call-done), kind=kOutput, calls=%fused_computation.15 | convolution fusion | flops 8896256 | bytes 329728 | tf_op jit(solution)/shard_map/dot_general | solution.py:58
  50.4 0.0 copy-done.3
  50.4 0.9 fusion.6
  51.3 0.0 reduce-scatter.5.cloned.1.call-update
  51.3 0.0 copy-start.9
  51.3 0.6 copy-done.9
  52.0 0.6 dynamic-slice
  53.2 41.9 %all-reduce = f32[256]{0:T(256)S(1)} all-reduce(f32[256]{0:T(256)S(1)} %get-tuple-element.58), channel_id=4, replica_groups=mesh['rows'=16,'rep'=2] {'rows'}, use_global_device_ids=true, to_apply=%region_8.9.clone | all-reduce | flops 256 | bytes 2048
  95.1 0.1 dynamic-slice.1
  95.2 33.4 %reduce-scatter.5.cloned.1.call-done = f32[128,16]{0,1:T(8,128)} async-done(((f32[128,256]{0,1:T(8,128)}), f32[128,16]{0,1:T(8,128)}) %reduce-scatter.5.cloned.1.call-update) | async-done | bytes 8208 | tf_op jit(solution)/shard_map/reduce_scatter | solution.py:65
  128.6 3.2 %all-reduce.1 = (f32[128,16]{0,1:T(8,128)}, f32[16]{0:T(128)}) all-reduce(f32[128,16]{0,1:T(8,128)} %reduce-scatter.5.cloned.1.call-done, f32[16]{0:T(128)S(1)} %dynamic-slice.1), channel_id=1, replica_groups=mesh['rows'=16,'rep'=2] {'rep'}, use_global_device_ids=true, to_apply=%region_6.7 | all-reduce | flops 2064 | bytes 16512 | tf_op jit(solution)/shard_map/psum | solution.py:68
  (10 shorter events, 0.1 us)
Async XLA Ops:
  7.2 17.5 %copy-start = (bf16[256,128]{1,0:T(8,128)(2,1)S(1)}, bf16[256,128]{1,0:T(8,128)(2,1)}, u32[]{:S(2)}) copy-start(bf16[256,128]{1,0:T(8,128)(2,1)} %param.9) | copy-start | bytes 196612
  7.2 0.7 copy-start.8
  7.2 0.8 copy-start.4
  8.8 15.5 %all-to-all-start = ((s32[16,1,1]{2,1,0:T(1,128)}), s32[16,1,1]{2,1,0:T(1,128)S(1)}, u32[]{:S(2)}, u32[]{:S(2)}) async-start(s32[16,1,1]{2,1,0:T(1,128)} %copy.12), calls=%async_computation | async-start | bytes 16384 | tf_op jit(solution)/shard_map/all_to_all | solution.py:48
  25.7 12.8 %copy-start.1 = (bf16[1,4,16,4096]{3,2,1,0:T(8,128)(2,1)S(1)}, bf16[1,4,16,4096]{3,2,1,0:T(8,128)(2,1)}, u32[]{:S(2)}) copy-start(bf16[1,4,16,4096]{3,2,1,0:T(8,128)(2,1)} %param.14) | copy-start | bytes 1572868
  26.5 12.0 %all-to-all-start.1 = ((bf16[16,64,128]{2,1,0:T(8,128)(2,1)}), bf16[16,64,128]{2,1,0:T(8,128)(2,1)S(1)}, u32[]{:S(2)}, u32[]{:S(2)}) async-start(bf16[16,64,128]{2,1,0:T(8,128)(2,1)} %broadcast_select_fusion), calls=%async_computation.1 | async-start | bytes 524288 | tf_op jit(solution)/shard_map/all_to_all | solution.py:52
  30.0 18.7 %reduce-scatter.3.cloned.1.call-start = ((), (), s32[]{:S(2)}) async-start(), calls=%async_computation.4 | async-start | bytes 196608 | tf_op jit(solution)/shard_map/reduce_scatter | solution.py:55
  38.5 10.2 %copy-start.7 = (f32[256]{0:T(256)S(1)}, f32[256]{0:T(256)}, u32[]{:S(2)}) copy-start(f32[256]{0:T(256)} %param.11) | copy-start | bytes 3076
  42.2 0.6 copy-start.2
  42.2 6.4 %copy-start.5 = (bf16[128,256]{1,0:T(8,128)(2,1)S(1)}, bf16[128,256]{1,0:T(8,128)(2,1)}, u32[]{:S(2)}) copy-start(bf16[128,256]{1,0:T(8,128)(2,1)} %param.15) | copy-start | bytes 196612
  42.3 6.4 %copy-start.6 = (bf16[128,256]{1,0:T(8,128)(2,1)S(1)}, bf16[128,256]{1,0:T(8,128)(2,1)}, u32[]{:S(2)}) copy-start(bf16[128,256]{1,0:T(8,128)(2,1)} %param.10) | copy-start | bytes 196612
  42.9 85.7 %reduce-scatter.5.cloned.1.call-start = ((), (), s32[]{:S(2)}) async-start(), calls=%async_computation.5 | async-start | bytes 139264 | tf_op jit(solution)/shard_map/reduce_scatter | solution.py:65
  48.7 1.8 %copy-start.3 = (f32[128,128]{1,0:T(8,128)S(1)}, f32[128,128]{1,0:T(8,128)}, u32[]{:S(2)}) copy-start(f32[128,128]{1,0:T(8,128)} %reduce-scatter.3.cloned.1.call-done) | copy-start | bytes 196612
  51.3 0.7 copy-start.9
Sparse Core Ops, SparseCore 0:
  43.0 5.5 reduce-scatter.2
  51.4 77.1 reduce-scatter.4
where the time goes:
time: 138 us; the launch traced here: 139 us
  waiting for transfers between devices  53.5 us (39%)
  blocking collectives  45.1 us (33%)
  between operations  15.5 us (11%)
  starting transfers between devices  11.9 us (9%)
  local copies, waits for them, and re-layouts  6.49 us (5%)
  matrix products  3.32 us (2%)
  other arithmetic  2.7 us (2%)
    unnamed x1, blocking collectives  41.9 us
    reduce_scatter x1, waiting for transfers between devices, body(): lax.psum_scatter(weight_term, 'rows', scatter_dimension=1, tiled=True)  33.4 us
    all_to_all x1, starting transfers between devices, body(): lax.all_to_all(wanted, 'rows', split_axis=0, concat_axis=0, tiled=True)  8.31 us
    all_to_all x1, waiting for transfers between devices, body(): lax.all_to_all(wanted, 'rows', split_axis=0, concat_axis=0, tiled=True)  7.19 us
    all_to_all x1, waiting for transfers between devices, body(): lax.all_to_all(picked, 'rows', split_axis=0, concat_axis=0, tiled=True)  7.12 us
    reduce_scatter x1, waiting for transfers between devices, body(): lax.psum_scatter(partial_sum, 'rep', scatter_dimension=0, tiled=True)  5.71 us
    all_to_all x1, starting transfers between devices, body(): lax.all_to_all(picked, 'rows', split_axis=0, concat_axis=0, tiled=True)  3.53 us
    psum x1, blocking collectives, body(): weight_grad, bias_grad = lax.psum((weight_part, bias_part), 'rep')  3.19 us
  transfers between devices with their start and end apart: 4, of which 4 were waited for; matrix products, arithmetic and copies ran while one was open for 1% of the time, Pallas kernels for 0%

commit v1 on v0

v1 whole, which is shorter than its diff:
```python
import functools

import jax
import jax.numpy as jnp
from jax import lax
from jax.experimental import pallas as pl
from jax.experimental.pallas import tpu as pltpu
from jax.sharding import PartitionSpec as P

BOTH = ("rows", "rep")
VMEM = pl.BlockSpec(memory_space=pltpu.VMEM)
SMEM = pl.BlockSpec(memory_space=pltpu.SMEM)


def digit_groups(owners):
    top = owners.bit_length() - 1
    groups = []
    while top > 0:
        take = min(2, top)
        top -= take
        groups.append((top, 1 << take))
    return groups


def swap_to(value, mask, owners):
    pairs = [(i, i ^ (2 * mask + 1)) for i in range(2 * owners)]
    return lax.ppermute(value, BOTH, pairs)


def place_kernel(counts, place, vals, dense, rows):
    nblk, slots = vals.shape[0], vals.shape[1]
    wide = vals.shape[2] // 128
    dense[...] = jnp.zeros_like(dense)
    low = lax.broadcasted_iota(jnp.int32, (wide, 128), 1) < 64
    for r in range(nblk):
        for i in range(wide):
            rows[r, i * slots : (i + 1) * slots, :] = vals[r, :, i * 128 : (i + 1) * 128].astype(jnp.float32)
        for k in range(slots):

            @pl.when(k < counts[0, r])
            def _():
                here = place[r, k]
                at = here // 2
                left = here % 2 == 0
                two = rows[r, pl.ds(k, wide, stride=slots), :]
                turned = pltpu.roll(two, 64, 1)
                first = jnp.where(left, two, turned)
                second = jnp.where(left, turned, two)
                mine = low == left
                even = jnp.where(mine, first, 0.0).astype(jnp.bfloat16)
                odd = jnp.where(mine, second, 0.0).astype(jnp.bfloat16)
                dense[at, pl.ds(r * wide, wide), :] = even
                dense[at, pl.ds((nblk + r) * wide, wide), :] = odd


def place_blocks(counts, place, vals, owners):
    nblk, slots, flat = vals.shape
    wide = flat // 128
    return pl.pallas_call(
        place_kernel,
        out_shape=jax.ShapeDtypeStruct((owners, 2 * nblk * wide, 128), jnp.bfloat16),
        in_specs=[SMEM, SMEM, VMEM],
        out_specs=VMEM,
        scratch_shapes=[pltpu.VMEM((nblk, wide * slots, 128), jnp.float32)],
        name="place",
    )(counts, place, vals)


def sum_kernel(dense, feats, out):
    owners, rows, _ = dense.shape
    acc = jnp.zeros((rows, 128), jnp.float32)

    def two(q, acc):
        left = jnp.concatenate([dense[2 * q], dense[2 * q + 1]], axis=1)
        right = feats[pl.ds(pl.multiple_of(q * 256, 256), 256), :]
        return acc + jnp.dot(left, right, preferred_element_type=jnp.float32)

    if owners <= 16:
        for q in range(owners // 2):
            acc = two(q, acc)
    else:
        acc = lax.fori_loop(0, owners // 2, two, acc)
    nblk = rows // 64
    for p in range(2):
        for r in range(nblk):
            out[pl.ds(r * 64 + p, 32, stride=2), :] = acc[(p * nblk + r) * 32 : (p * nblk + r + 1) * 32]


def sum_blocks(dense, feats):
    return pl.pallas_call(
        sum_kernel,
        out_shape=jax.ShapeDtypeStruct((dense.shape[1], 128), jnp.float32),
        in_specs=[VMEM, VMEM],
        out_specs=VMEM,
        name="block_sum",
    )(dense, feats)


def layer_kernel(side, mine, other, weight, bias, cot_mine, cot_other, act, parts, value):
    half = cot_mine.shape[0]
    owners, chunk, _ = parts.shape
    share = 256 // owners
    aggregated = (mine[...] + other[...]).astype(jnp.bfloat16)
    pre = jnp.dot(aggregated, weight[...], preferred_element_type=jnp.float32) + bias[...]
    sig = 1.0 / (1.0 + jnp.exp(-pre))
    value[...] = pre * sig
    act[...] = value[pl.ds(pl.multiple_of(side[0] * half, half), half), :].astype(jnp.bfloat16)
    first = side[0] == 0
    cot_a = cot_mine[...].astype(jnp.float32)
    cot_b = cot_other[...].astype(jnp.float32)
    cot = jnp.concatenate([jnp.where(first, cot_a, cot_b), jnp.where(first, cot_b, cot_a)], axis=0)
    delta = (cot * sig * (1.0 + pre * (1.0 - sig))).astype(jnp.bfloat16)
    grad = lax.dot_general(delta, aggregated, (((0,), (0,)), ((), ())), preferred_element_type=jnp.float32)
    total = jnp.sum(delta.astype(jnp.float32), axis=0, keepdims=True)
    tail = jnp.concatenate(
        [total[:, :128], total[:, 128:], jnp.zeros((chunk - share - 2, 128), jnp.float32)], axis=0
    )
    for r in range(owners):
        parts[r] = jnp.concatenate([grad[r * share : (r + 1) * share], tail], axis=0)


def layer(side, mine, other, weight, bias, cot_mine, cot_other, owners):
    nodes = mine.shape[0]
    half, wide = cot_mine.shape
    chunk = -(-(wide // owners + 2) // 8) * 8
    return pl.pallas_call(
        layer_kernel,
        out_shape=(
            jax.ShapeDtypeStruct((half, wide), jnp.bfloat16),
            jax.ShapeDtypeStruct((owners, chunk, 128), jnp.float32),
        ),
        in_specs=[SMEM] + [VMEM] * 6,
        out_specs=(VMEM, VMEM),
        scratch_shapes=[pltpu.VMEM((nodes, wide), jnp.float32)],
        name="layer",
    )(side, mine, other, weight, bias, cot_mine, cot_other)


def finish_kernel(row, got, weight_grad, bias_grad):
    share = weight_grad.shape[0]
    total = jnp.sum(got[...], axis=0)
    weight_grad[...] = total[:share]
    flat = jnp.concatenate([total[share : share + 1], total[share + 1 : share + 2]], axis=1)
    flat = jnp.broadcast_to(flat, (8, 256))
    flat = pltpu.roll(flat, lax.rem(256 - row[0] * share, 256), 1)
    bias_grad[...] = flat[:1, :share]


def finish(row, got):
    share = 256 // got.shape[0]
    return pl.pallas_call(
        finish_kernel,
        out_shape=(
            jax.ShapeDtypeStruct((share, 128), jnp.float32),
            jax.ShapeDtypeStruct((1, share), jnp.float32),
        ),
        in_specs=[SMEM, VMEM],
        out_specs=(VMEM, VMEM),
        name="finish",
    )(row, got)


def body(features, weight, bias, block_count, block_cols, block_vals, cotangent):
    side = lax.axis_index("rep")
    row = lax.axis_index("rows")
    owners = lax.axis_size("rows")
    groups = digit_groups(owners)
    half_rows = features.shape[0] // 2

    cols = block_cols[0]
    apart = (cols // 2) ^ row
    place = jnp.zeros_like(cols)
    stride = 1
    for shift, radix in groups:
        place = place + ((apart >> shift) & (radix - 1)) * stride
        stride *= radix
    place = place * 2 + cols % 2

    flip = (len(groups) - 1) & 1
    keep = lax.dynamic_slice_in_dim(features, (side ^ flip) * half_rows, half_rows, 0)
    give = lax.dynamic_slice_in_dim(features, (1 - side ^ flip) * half_rows, half_rows, 0)
    shift, radix = groups[0]
    held = jnp.concatenate([keep] + [swap_to(give, s << shift, owners) for s in range(1, radix)])
    cot_other = swap_to(cotangent, 0, owners)
    for shift, radix in groups[1:]:
        held = jnp.concatenate([swap_to(held, s << shift, owners) for s in range(radix)])

    dense = place_blocks(block_count, place, block_vals[0], owners)
    mine = sum_blocks(dense, held)
    other = swap_to(mine, 0, owners)
    side_arr = side.reshape(1).astype(jnp.int32)
    activated, parts = layer(
        side_arr, mine, other, weight, bias.reshape(1, -1), cotangent, cot_other, owners
    )
    got = lax.all_to_all(parts, "rows", split_axis=0, concat_axis=0, tiled=True)
    weight_grad, bias_grad = finish(row.reshape(1).astype(jnp.int32), got)
    return activated, weight_grad.T, bias_grad.reshape(-1)


def solution(mesh):
    placed = (
        P("rows", None),
        P(),
        P(),
        P("rep", "rows"),
        P("rep", "rows", None),
        P("rep", "rows", None, None),
        P(BOTH, None),
    )
    return jax.shard_map(
        body,
        mesh=mesh,
        in_specs=placed,
        out_specs=(P(BOTH, None), P(None, "rows"), P("rows")),
        check_vma=False,
    )
```

time: 138 us -> 46 us (0.33)
  waiting for transfers between devices: 53.5 us -> 6.61 us
  blocking collectives: 45.1 us -> 13.1 us
  between operations: 15.5 us -> 0.68 us
  Pallas kernels: 0 us -> 13.1 us
  local copies, waits for them, and re-layouts: 6.49 us -> 1.44 us
  matrix products: 3.32 us -> 0 us
  starting transfers between devices: 11.9 us -> 9.23 us
    unnamed x1 -> x0, blocking collectives: 41.9 us -> none
    reduce_scatter x2 -> x0, waiting for transfers between devices: 39.1 us -> none  [the longest x1 33.4 us: body(): lax.psum_scatter(weight_term, 'rows', scatter_dimension=1, tiled=True)]
    all_to_all x2 -> x0, waiting for transfers between devices: 14.3 us -> none  [the longest x1 7.19 us: body(): lax.all_to_all(wanted, 'rows', split_axis=0, concat_axis=0, tiled=True)]
    all_to_all x0 -> x1, blocking collectives: none -> 13.1 us  [body(): got = lax.all_to_all(parts, 'rows', split_axis=0, concat_axis=0, tiled=True)]
    pallas_call x0 -> x4, Pallas kernels: none -> 13.1 us  [the longest x1 6.87 us: place_blocks(): pl.pallas_call(place_kernel, out_shape=jax.ShapeDtypeStruct((owners, 2 *...]
    all_to_all x2 -> x0, starting transfers between devices: 11.8 us -> none  [the longest x1 8.31 us: body(): lax.all_to_all(wanted, 'rows', split_axis=0, concat_axis=0, tiled=True)]
    ppermute x0 -> x9, starting transfers between devices: none -> 9.23 us  [swap_to(): return lax.ppermute(value, BOTH, pairs)]
    ppermute x0 -> x9, waiting for transfers between devices: none -> 6.61 us  [swap_to(): return lax.ppermute(value, BOTH, pairs)]
  transfers between devices with their start and end apart: 4 -> 9, of which waited for: 4 -> 4; matrix products, arithmetic and copies ran while one was open for 1% -> 1% of each run, Pallas kernels for 0% -> 15%
where the time goes in v1:
time: 46 us; the launch traced here: 45.6 us
  Pallas kernels  13.1 us (28%)
  blocking collectives  13.1 us (28%)
  starting transfers between devices  9.23 us (20%)
  waiting for transfers between devices  6.61 us (14%)
  other arithmetic  1.47 us (3%)
  local copies, waits for them, and re-layouts  1.44 us (3%)
  between operations  0.68 us (1%)
    all_to_all x1, blocking collectives, body(): got = lax.all_to_all(parts, 'rows', split_axis=0, concat_axis=0, tiled=True)  13.1 us
    ppermute x9, starting transfers between devices, swap_to(): return lax.ppermute(value, BOTH, pairs)  9.23 us
    pallas_call x1, Pallas kernels, place_blocks(): pl.pallas_call(place_kernel, out_shape=jax.ShapeDtypeStruct((owners, 2 *...  6.87 us
    ppermute x9, waiting for transfers between devices, swap_to(): return lax.ppermute(value, BOTH, pairs)  6.61 us
    pallas_call x1, Pallas kernels, sum_blocks(): pl.pallas_call(sum_kernel, out_shape=jax.ShapeDtypeStruct((dense.shape[1]...  2.45 us
    pallas_call x1, Pallas kernels, layer(): pl.pallas_call(layer_kernel, out_shape=(jax.ShapeDtypeStruct((half, wide)...  2.22 us
    pallas_call x1, Pallas kernels, finish(): pl.pallas_call(finish_kernel, out_shape=(jax.ShapeDtypeStruct((share, 128...  1.55 us
  transfers between devices with their start and end apart: 9, of which 4 were waited for; matrix products, arithmetic and copies ran while one was open for 1% of the time, Pallas kernels for 15%

profile of v1, /device:TPU:0, one launch (start us, length us, event | category | flops | bytes accessed | tf_op | source)
XLA Modules:
  0.0 45.6 jit_solution(7584688419713057880)
XLA Ops:
  0.6 0.8 %constant_dynamic-slice_fusion.1 = (bf16[128,128]{1,0:T(8,128)(2,1)S(1)}, bf16[128,128]{1,0:T(8,128)(2,1)S(1)}) fusion(bf16[256,128]{1,0:T(8,128)(2,1)} %param.7, s32[]{:T(128)S(6)} %select_n.20, s32[]{:T(128)S(6)} %select_n.21), kind=kLoop, calls=%fused_computation.15 | loop fusion | bytes 131080 | tf_op jit(solution)/shard_map/dynamic_slice | solution.py:180
  1.4 2.5 %collective-permute-start = (bf16[128,128]{1,0:T(8,128)(2,1)S(1)}, bf16[128,128]{1,0:T(8,128)(2,1)S(1)}, u32[]{:S(2)}, u32[]{:S(2)}) collective-permute-start(bf16[128,128]{1,0:T(8,128)(2,1)S(1)} %get-tuple-element.12), channel_id=1, source_target_pairs={{0,9},{1,8},{2,11},{3,10},{4,13},{5,12},{6,15},{7,14},{8,1},{9,0},... | collective-permute-start | bytes 98312 | tf_op jit(solution)/shard_map/ppermute | solution.py:27
  3.9 2.9 %collective-permute-start.1 = (bf16[128,128]{1,0:T(8,128)(2,1)S(1)}, bf16[128,128]{1,0:T(8,128)(2,1)S(1)}, u32[]{:S(2)}, u32[]{:S(2)}) collective-permute-start(bf16[128,128]{1,0:T(8,128)(2,1)S(1)} %get-tuple-element.12), channel_id=1, source_target_pairs={{0,17},{1,16},{2,19},{3,18},{4,21},{5,20},{6,23},{7,22},{8,25},{9,... | collective-permute-start | bytes 98312 | tf_op jit(solution)/shard_map/ppermute | solution.py:27
  6.8 0.0 collective-permute-start.2
  6.8 0.0 collective-permute-done
  6.8 1.6 %collective-permute-done.1 = bf16[128,128]{1,0:T(8,128)(2,1)S(1)} collective-permute-done((bf16[128,128]{1,0:T(8,128)(2,1)S(1)}, bf16[128,128]{1,0:T(8,128)(2,1)S(1)}, u32[]{:S(2)}, u32[]{:S(2)}) %collective-permute-start.1) | collective-permute-done | bytes 32800 | tf_op jit(solution)/shard_map/ppermute | solution.py:27
  8.4 3.9 %collective-permute-done.2 = bf16[128,128]{1,0:T(8,128)(2,1)S(1)} collective-permute-done((bf16[128,128]{1,0:T(8,128)(2,1)S(1)}, bf16[128,128]{1,0:T(8,128)(2,1)S(1)}, u32[]{:S(2)}, u32[]{:S(2)}) %collective-permute-start.2) | collective-permute-done | bytes 32800 | tf_op jit(solution)/shard_map/ppermute | solution.py:27
  12.2 0.0 copy-start.3
  12.3 0.2 collective-permute-start.3
  12.4 1.5 %collective-permute-start.4 = (bf16[512,128]{1,0:T(8,128)(2,1)S(1)}, bf16[512,128]{1,0:T(8,128)(2,1)S(1)}, u32[]{:S(2)}, u32[]{:S(2)}) collective-permute-start(bf16[512,128]{1,0:T(8,128)(2,1)S(1)} %pad_maximum_fusion.1), channel_id=1, source_target_pairs={{0,3},{1,2},{2,1},{3,0},{4,7},{5,6},{6,5},{7,4},{8,11},{9,10},{10,... | collective-permute-start | bytes 393224 | tf_op jit(solution)/shard_map/ppermute | solution.py:27
  13.9 1.3 %collective-permute-start.5 = (bf16[512,128]{1,0:T(8,128)(2,1)S(1)}, bf16[512,128]{1,0:T(8,128)(2,1)S(1)}, u32[]{:S(2)}, u32[]{:S(2)}) collective-permute-start(bf16[512,128]{1,0:T(8,128)(2,1)S(1)} %pad_maximum_fusion.1), channel_id=1, source_target_pairs={{0,5},{1,4},{2,7},{3,6},{4,1},{5,0},{6,3},{7,2},{8,13},{9,12},{10,... | collective-permute-start | bytes 393224 | tf_op jit(solution)/shard_map/ppermute | solution.py:27
  15.2 0.4 collective-permute-start.6
  15.6 0.0 copy-done.3
  15.6 0.6 %fusion.1.place = s32[4,16]{1,0:T(4,128)} fusion(s32[1,4,16]{2,1,0:T(4,128)S(1)} %copy-done.3, s32[]{:T(128)} %axis_index.25), kind=kLoop, calls=%fused_computation.8 | loop fusion | flops 1792 | bytes 516 | tf_op jit(solution)/shard_map/add | solution.py:177
  16.2 6.9 %place.1.dense = bf16[16,256,128]{2,1,0:T(8,128)(2,1)} custom-call(s32[1,4]{1,0:T(1,128)} %counts.1, s32[4,16]{1,0:T(4,128)} %fusion.1.place, bf16[4,16,4096]{2,1,0:T(8,128)(2,1)} %bitcast.22), custom_call_target="tpu_custom_call" | custom-call | tf_op jit(solution)/shard_map/place/pallas_call | solution.py:59
  23.1 0.0 collective-permute-done.3
  23.1 0.0 collective-permute-done.4
  23.1 0.0 collective-permute-done.5
  23.1 0.0 collective-permute-done.6
  23.1 0.9 %pad_maximum_fusion.feats = bf16[2048,128]{1,0:T(8,128)(2,1)} fusion(bf16[512,128]{1,0:T(8,128)(2,1)S(1)} %collective-permute-done.6, bf16[512,128]{1,0:T(8,128)(2,1)S(1)} %collective-permute-done.5, bf16[512,128]{1,0:T(8,128)(2,1)S(1)} %collective-permute-done.4, bf16[512,128]{1,0:T(8,128)(2,1)S(1)} %collective-permute-done.3), kind=kLoop, calls=%fused_computation | loop fusion | flops 2097152 | bytes 1048576 | tf_op jit(solution)/shard_map/concatenate | solution.py:186
  24.0 0.0 copy-start.1
  24.0 2.5 %block_sum.1.mine = f32[256,128]{1,0:T(8,128)} custom-call(bf16[16,256,128]{2,1,0:T(8,128)(2,1)} %place.1.dense, bf16[2048,128]{1,0:T(8,128)(2,1)} %pad_maximum_fusion.feats), custom_call_target="tpu_custom_call" | custom-call | tf_op jit(solution)/shard_map/block_sum/pallas_call | solution.py:90
  26.5 0.0 collective-permute-start.7
  26.5 0.0 copy-done.1
  26.5 0.5 %collective-permute-start.8 = (bf16[128,256]{1,0:T(8,128)(2,1)S(1)}, bf16[128,256]{1,0:T(8,128)(2,1)S(1)}, u32[]{:S(2)}, u32[]{:S(2)}) collective-permute-start(bf16[128,256]{1,0:T(8,128)(2,1)S(1)} %copy-done.1), channel_id=1, source_target_pairs={{0,1},{1,0},{2,3},{3,2},{4,5},{5,4},{6,7},{7,6},{8,9},{9,8},{10,11... | collective-permute-start | bytes 196616 | tf_op jit(solution)/shard_map/ppermute | solution.py:27
  27.0 0.9 %collective-permute-done.8.cot_other = bf16[128,256]{1,0:T(8,128)(2,1)S(1)} collective-permute-done((bf16[128,256]{1,0:T(8,128)(2,1)S(1)}, bf16[128,256]{1,0:T(8,128)(2,1)S(1)}, u32[]{:S(2)}, u32[]{:S(2)}) %collective-permute-start.8) | collective-permute-done | bytes 65568 | tf_op jit(solution)/shard_map/ppermute | solution.py:27
  27.9 0.0 copy-start.2
  27.9 0.2 collective-permute-done.7.other
  28.1 0.0 copy-start
  28.1 0.4 copy-done.2
  28.5 0.3 copy-done
  28.8 2.2 %layer.1 = (bf16[128,256]{1,0:T(8,128)(2,1)}, f32[16,24,128]{2,1,0:T(8,128)}) custom-call(s32[1]{0:T(128)} %bitcast.side, f32[256,128]{1,0:T(8,128)} %block_sum.1.mine, f32[256,128]{1,0:T(8,128)} %copy-done, bf16[128,256]{1,0:T(8,128)(2,1)} %weight.1, f32[1,256]{1,0:T(1,128)} %bitcast.23, bf16[128,256]{1,0:T(8,128)(2,1)} %cot_mine.1, bf16[128,256]{1,0:T(8,128)(2,1)} %copy-done.2), custom_call_target="tpu_custom_call" | custom-call | tf_op jit(solution)/shard_map/layer/pallas_call | solution.py:126
  31.0 13.1 %all_to_all.5.got = f32[16,24,128]{2,1,0:T(8,128)} all-to-all(f32[16,24,128]{2,1,0:T(8,128)} %get-tuple-element.8), channel_id=1, replica_groups=mesh['rows'=16,'rep'=2] {'rows'}, dimensions={0} | all-to-all | bytes 393216 | tf_op jit(solution)/shard_map/all_to_all | solution.py:195
  44.1 1.5 %finish.1 = (f32[16,128]{1,0:T(8,128)}, f32[1,16]{1,0:T(1,128)}) custom-call(s32[1]{0:T(128)} %bitcast.4.row, f32[16,24,128]{2,1,0:T(8,128)} %all_to_all.5.got), custom_call_target="tpu_custom_call" | custom-call | tf_op jit(solution)/shard_map/finish/pallas_call | solution.py:151
  (1 shorter events, 0.0 us)
Async XLA Ops:
  1.4 5.3 %collective-permute-start = (bf16[128,128]{1,0:T(8,128)(2,1)S(1)}, bf16[128,128]{1,0:T(8,128)(2,1)S(1)}, u32[]{:S(2)}, u32[]{:S(2)}) collective-permute-start(bf16[128,128]{1,0:T(8,128)(2,1)S(1)} %get-tuple-element.12), channel_id=1, source_target_pairs={{0,9},{1,8},{2,11},{3,10},{4,13},{5,12},{6,15},{7,14},{8,1},{9,0},... | collective-permute-start | bytes 98312 | tf_op jit(solution)/shard_map/ppermute | solution.py:27
  3.9 4.5 %collective-permute-start.1 = (bf16[128,128]{1,0:T(8,128)(2,1)S(1)}, bf16[128,128]{1,0:T(8,128)(2,1)S(1)}, u32[]{:S(2)}, u32[]{:S(2)}) collective-permute-start(bf16[128,128]{1,0:T(8,128)(2,1)S(1)} %get-tuple-element.12), channel_id=1, source_target_pairs={{0,17},{1,16},{2,19},{3,18},{4,21},{5,20},{6,23},{7,22},{8,25},{9,... | collective-permute-start | bytes 98312 | tf_op jit(solution)/shard_map/ppermute | solution.py:27
  6.8 5.5 %collective-permute-start.2 = (bf16[128,128]{1,0:T(8,128)(2,1)S(1)}, bf16[128,128]{1,0:T(8,128)(2,1)S(1)}, u32[]{:S(2)}, u32[]{:S(2)}) collective-permute-start(bf16[128,128]{1,0:T(8,128)(2,1)S(1)} %get-tuple-element.12), channel_id=1, source_target_pairs={{0,25},{1,24},{2,27},{3,26},{4,29},{5,28},{6,31},{7,30},{8,17},{9,... | collective-permute-start | bytes 98312 | tf_op jit(solution)/shard_map/ppermute | solution.py:27
  12.2 3.4 %copy-start.3 = (s32[1,4,16]{2,1,0:T(4,128)S(1)}, s32[1,4,16]{2,1,0:T(4,128)}, u32[]{:S(2)}) copy-start(s32[1,4,16]{2,1,0:T(4,128)} %param.11) | copy-start | bytes 772
  12.3 10.9 %collective-permute-start.3 = (bf16[512,128]{1,0:T(8,128)(2,1)S(1)}, bf16[512,128]{1,0:T(8,128)(2,1)S(1)}, u32[]{:S(2)}, u32[]{:S(2)}) collective-permute-start(bf16[512,128]{1,0:T(8,128)(2,1)S(1)} %pad_maximum_fusion.1), channel_id=1, source_target_pairs={{0,1},{1,0},{2,3},{3,2},{4,5},{5,4},{6,7},{7,6},{8,9},{9,8},{10,11... | collective-permute-start | bytes 393224 | tf_op jit(solution)/shard_map/ppermute | solution.py:27
  12.4 10.7 %collective-permute-start.4 = (bf16[512,128]{1,0:T(8,128)(2,1)S(1)}, bf16[512,128]{1,0:T(8,128)(2,1)S(1)}, u32[]{:S(2)}, u32[]{:S(2)}) collective-permute-start(bf16[512,128]{1,0:T(8,128)(2,1)S(1)} %pad_maximum_fusion.1), channel_id=1, source_target_pairs={{0,3},{1,2},{2,1},{3,0},{4,7},{5,6},{6,5},{7,4},{8,11},{9,10},{10,... | collective-permute-start | bytes 393224 | tf_op jit(solution)/shard_map/ppermute | solution.py:27
  13.9 9.2 %collective-permute-start.5 = (bf16[512,128]{1,0:T(8,128)(2,1)S(1)}, bf16[512,128]{1,0:T(8,128)(2,1)S(1)}, u32[]{:S(2)}, u32[]{:S(2)}) collective-permute-start(bf16[512,128]{1,0:T(8,128)(2,1)S(1)} %pad_maximum_fusion.1), channel_id=1, source_target_pairs={{0,5},{1,4},{2,7},{3,6},{4,1},{5,0},{6,3},{7,2},{8,13},{9,12},{10,... | collective-permute-start | bytes 393224 | tf_op jit(solution)/shard_map/ppermute | solution.py:27
  15.2 7.9 %collective-permute-start.6 = (bf16[512,128]{1,0:T(8,128)(2,1)S(1)}, bf16[512,128]{1,0:T(8,128)(2,1)S(1)}, u32[]{:S(2)}, u32[]{:S(2)}) collective-permute-start(bf16[512,128]{1,0:T(8,128)(2,1)S(1)} %pad_maximum_fusion.1), channel_id=1, source_target_pairs={{0,7},{1,6},{2,5},{3,4},{4,3},{5,2},{6,1},{7,0},{8,15},{9,14},{10,... | collective-permute-start | bytes 393224 | tf_op jit(solution)/shard_map/ppermute | solution.py:27
  24.0 2.5 %copy-start.1 = (bf16[128,256]{1,0:T(8,128)(2,1)S(1)}, bf16[128,256]{1,0:T(8,128)(2,1)}, u32[]{:S(2)}) copy-start(bf16[128,256]{1,0:T(8,128)(2,1)} %cot_mine.1) | copy-start | bytes 196612
  26.5 1.7 %collective-permute-start.7 = (f32[256,128]{1,0:T(8,128)}, f32[256,128]{1,0:T(8,128)S(1)}, u32[]{:S(2)}, u32[]{:S(2)}) collective-permute-start(f32[256,128]{1,0:T(8,128)} %block_sum.1.mine), channel_id=1, source_target_pairs={{0,1},{1,0},{2,3},{3,2},{4,5},{5,4},{6,7},{7,6},{8,9},{9,8},{10,11... | collective-permute-start | bytes 393224 | tf_op jit(solution)/shard_map/ppermute | solution.py:27
  26.5 1.4 %collective-permute-start.8 = (bf16[128,256]{1,0:T(8,128)(2,1)S(1)}, bf16[128,256]{1,0:T(8,128)(2,1)S(1)}, u32[]{:S(2)}, u32[]{:S(2)}) collective-permute-start(bf16[128,256]{1,0:T(8,128)(2,1)S(1)} %copy-done.1), channel_id=1, source_target_pairs={{0,1},{1,0},{2,3},{3,2},{4,5},{5,4},{6,7},{7,6},{8,9},{9,8},{10,11... | collective-permute-start | bytes 196616 | tf_op jit(solution)/shard_map/ppermute | solution.py:27
  27.9 0.6 %copy-start.2 = (bf16[128,256]{1,0:T(8,128)(2,1)}, bf16[128,256]{1,0:T(8,128)(2,1)S(1)}, u32[]{:S(2)}) copy-start(bf16[128,256]{1,0:T(8,128)(2,1)S(1)} %collective-permute-done.8.cot_other) | copy-start | bytes 196612
  28.1 0.6 %copy-start = (f32[256,128]{1,0:T(8,128)}, f32[256,128]{1,0:T(8,128)S(1)}, u32[]{:S(2)}) copy-start(f32[256,128]{1,0:T(8,128)S(1)} %collective-permute-done.7.other) | copy-start | bytes 393220

commit v2 on v1

--- a/solution.py
+++ b/solution.py
@@ -1,3 +1,5 @@
+import functools
+
 import functools
 
 import jax
@@ -27,73 +29,109 @@
     return lax.ppermute(value, BOTH, pairs)
 
 
-def place_kernel(counts, place, vals, dense, rows):
-    nblk, slots = vals.shape[0], vals.shape[1]
-    wide = vals.shape[2] // 128
-    dense[...] = jnp.zeros_like(dense)
-    low = lax.broadcasted_iota(jnp.int32, (wide, 128), 1) < 64
+def limit(owners):
+    return pltpu.CompilerParams(vmem_limit_bytes=(8 if owners <= 16 else 48) << 20)
+
+
+def place_kernel(groups, row, counts, cols, vals, dense):
+    nblk, slots, flat = vals.shape
+    owners = dense.shape[0]
+    wide = flat // 128
+    deep = 16 * slots
+    lane = lax.broadcasted_iota(jnp.int32, (slots, deep), 1)
+    slot = lax.broadcasted_iota(jnp.int32, (slots, deep), 0)
+    spread = (lane % slots == slot).astype(jnp.bfloat16)
+    named = jnp.dot(cols[...].astype(jnp.bfloat16), spread, preferred_element_type=jnp.float32)
+    named = named.astype(jnp.int32)
+    apart = (named >> 1) ^ row[0]
+    place = jnp.zeros_like(apart)
+    stride = 1
+    for shift, radix in groups:
+        place = place + ((apart >> shift) & (radix - 1)) * stride
+        stride *= radix
+    side = named & 1
+    lane = lax.broadcasted_iota(jnp.int32, (1, deep), 1)
+    at = lax.broadcasted_iota(jnp.int32, (256, deep), 0)
+    same = at % 16 == lax.broadcasted_iota(jnp.int32, (256, deep), 1) // slots
+    low = lax.broadcasted_iota(jnp.int32, (slots, 128), 1) < 64
     for r in range(nblk):
-        for i in range(wide):
-            rows[r, i * slots : (i + 1) * slots, :] = vals[r, :, i * 128 : (i + 1) * 128].astype(jnp.float32)
-        for k in range(slots):
-
-            @pl.when(k < counts[0, r])
-            def _():
-                here = place[r, k]
-                at = here // 2
-                left = here % 2 == 0
-                two = rows[r, pl.ds(k, wide, stride=slots), :]
+        used = lane % slots < counts[0, r]
+        to_first = jnp.where(used & (side[r : r + 1] == 0), place[r : r + 1], -1)
+        to_second = jnp.where(used & (side[r : r + 1] == 1), place[r : r + 1], -1)
+        rights = []
+        for g in range(wide // 16):
+            top, bottom = [], []
+            for i in range(g * 16, g * 16 + 16):
+                two = vals[r, :, i * 128 : (i + 1) * 128].astype(jnp.float32)
                 turned = pltpu.roll(two, 64, 1)
-                first = jnp.where(left, two, turned)
-                second = jnp.where(left, turned, two)
-                mine = low == left
-                even = jnp.where(mine, first, 0.0).astype(jnp.bfloat16)
-                odd = jnp.where(mine, second, 0.0).astype(jnp.bfloat16)
-                dense[at, pl.ds(r * wide, wide), :] = even
-                dense[at, pl.ds((nblk + r) * wide, wide), :] = odd
-
-
-def place_blocks(counts, place, vals, owners):
+                top.append(jnp.concatenate([jnp.where(low, two, 0.0), jnp.where(low, turned, 0.0)], axis=1).astype(jnp.bfloat16))
+                bottom.append(jnp.concatenate([jnp.where(low, 0.0, turned), jnp.where(low, 0.0, two)], axis=1).astype(jnp.bfloat16))
+            rights.append(jnp.concatenate(top + bottom, axis=0))
+
+        def put(q):
+            here = at // 16 + q * 16
+            pick = jnp.concatenate([same & (here == to_first), same & (here == to_second)], axis=1)
+            pick = pick.astype(jnp.bfloat16)
+            for g, right in enumerate(rights):
+                moved = jnp.dot(pick, right, preferred_element_type=jnp.float32).astype(jnp.bfloat16)
+                moved = moved.reshape(16, 16, 256)
+                start = r * wide + g * 16
+                dense[pl.ds(q * 16, 16), start : start + 16, :] = moved[:, :, :128]
+                start += nblk * wide
+                dense[pl.ds(q * 16, 16), start : start + 16, :] = moved[:, :, 128:]
+
+        if owners <= 16:
+            put(0)
+        else:
+            pl.loop(0, owners // 16)(put)
+
+
+def place_blocks(row, counts, cols, vals, owners):
     nblk, slots, flat = vals.shape
     wide = flat // 128
     return pl.pallas_call(
-        place_kernel,
+        functools.partial(place_kernel, digit_groups(owners)),
         out_shape=jax.ShapeDtypeStruct((owners, 2 * nblk * wide, 128), jnp.bfloat16),
-        in_specs=[SMEM, SMEM, VMEM],
+        in_specs=[SMEM, SMEM, VMEM, VMEM],
         out_specs=VMEM,
-        scratch_shapes=[pltpu.VMEM((nblk, wide * slots, 128), jnp.float32)],
+        compiler_params=limit(owners),
         name="place",
-    )(counts, place, vals)
-
-
-def sum_kernel(dense, feats, out):
+    )(row, counts, cols, vals)
+
+
+def sum_kernel(dense, *refs):
+    pieces, out = refs[:-1], refs[-1]
     owners, rows, _ = dense.shape
+    each = owners // len(pieces)
     acc = jnp.zeros((rows, 128), jnp.float32)
-
-    def two(q, acc):
-        left = jnp.concatenate([dense[2 * q], dense[2 * q + 1]], axis=1)
-        right = feats[pl.ds(pl.multiple_of(q * 256, 256), 256), :]
-        return acc + jnp.dot(left, right, preferred_element_type=jnp.float32)
-
-    if owners <= 16:
-        for q in range(owners // 2):
-            acc = two(q, acc)
-    else:
-        acc = lax.fori_loop(0, owners // 2, two, acc)
+    for s, feats in enumerate(pieces):
+
+        def two(q, acc):
+            at = s * each + 2 * q
+            left = jnp.concatenate([dense[at], dense[at + 1]], axis=1)
+            right = feats[pl.ds(pl.multiple_of(q * 256, 256), 256), :]
+            return acc + jnp.dot(left, right, preferred_element_type=jnp.float32)
+
+        if each <= 16:
+            for q in range(each // 2):
+                acc = two(q, acc)
+        else:
+            acc = lax.fori_loop(0, each // 2, two, acc)
     nblk = rows // 64
     for p in range(2):
         for r in range(nblk):
             out[pl.ds(r * 64 + p, 32, stride=2), :] = acc[(p * nblk + r) * 32 : (p * nblk + r + 1) * 32]
 
 
-def sum_blocks(dense, feats):
+def sum_blocks(dense, pieces):
     return pl.pallas_call(
         sum_kernel,
         out_shape=jax.ShapeDtypeStruct((dense.shape[1], 128), jnp.float32),
-        in_specs=[VMEM, VMEM],
+        in_specs=[VMEM] * (1 + len(pieces)),
         out_specs=VMEM,
+        compiler_params=limit(dense.shape[0]),
         name="block_sum",
-    )(dense, feats)
+    )(dense, *pieces)
 
 
 def layer_kernel(side, mine, other, weight, bias, cot_mine, cot_other, act, parts, value):
@@ -132,6 +170,7 @@
         in_specs=[SMEM] + [VMEM] * 6,
         out_specs=(VMEM, VMEM),
         scratch_shapes=[pltpu.VMEM((nodes, wide), jnp.float32)],
+        compiler_params=limit(owners),
         name="layer",
     )(side, mine, other, weight, bias, cot_mine, cot_other)
 
@@ -156,6 +195,7 @@
         ),
         in_specs=[SMEM, VMEM],
         out_specs=(VMEM, VMEM),
+        compiler_params=limit(got.shape[0]),
         name="finish",
     )(row, got)
 
@@ -167,33 +207,27 @@
     groups = digit_groups(owners)
     half_rows = features.shape[0] // 2
 
-    cols = block_cols[0]
-    apart = (cols // 2) ^ row
-    place = jnp.zeros_like(cols)
-    stride = 1
-    for shift, radix in groups:
-        place = place + ((apart >> shift) & (radix - 1)) * stride
-        stride *= radix
-    place = place * 2 + cols % 2
+    row_arr = row.reshape(1).astype(jnp.int32)
+    dense = place_blocks(row_arr, block_count, block_cols[0], block_vals[0], owners)
 
     flip = (len(groups) - 1) & 1
     keep = lax.dynamic_slice_in_dim(features, (side ^ flip) * half_rows, half_rows, 0)
     give = lax.dynamic_slice_in_dim(features, (1 - side ^ flip) * half_rows, half_rows, 0)
     shift, radix = groups[0]
-    held = jnp.concatenate([keep] + [swap_to(give, s << shift, owners) for s in range(1, radix)])
+    pieces = [keep] + [swap_to(give, s << shift, owners) for s in range(1, radix)]
     cot_other = swap_to(cotangent, 0, owners)
     for shift, radix in groups[1:]:
-        held = jnp.concatenate([swap_to(held, s << shift, owners) for s in range(radix)])
-
-    dense = place_blocks(block_count, place, block_vals[0], owners)
-    mine = sum_blocks(dense, held)
+        held, dense, cot_other = lax.optimization_barrier((jnp.concatenate(pieces), dense, cot_other))
+        pieces = [swap_to(held, s << shift, owners) for s in range(radix)]
+
+    mine = sum_blocks(dense, pieces)
     other = swap_to(mine, 0, owners)
     side_arr = side.reshape(1).astype(jnp.int32)
     activated, parts = layer(
         side_arr, mine, other, weight, bias.reshape(1, -1), cotangent, cot_other, owners
     )
     got = lax.all_to_all(parts, "rows", split_axis=0, concat_axis=0, tiled=True)
-    weight_grad, bias_grad = finish(row.reshape(1).astype(jnp.int32), got)
+    weight_grad, bias_grad = finish(row_arr, got)
     return activated, weight_grad.T, bias_grad.reshape(-1)
 
 

time: 46 us -> 38.9 us (0.85)
  Pallas kernels: 13.1 us -> 3.35 us
  local copies, waits for them, and re-layouts: 1.44 us -> 3.22 us
  other arithmetic: 1.47 us -> 0.01 us
  blocking collectives: 13.1 us -> 14.4 us
  waiting for transfers between devices: 6.61 us -> 7.88 us
    pallas_call x1, Pallas kernels: 6.87 us -> 1.37 us  [place_blocks(): pl.pallas_call(functools.partial(place_kernel, digit_groups(owners)), out...]
    pallas_call x1, Pallas kernels: 2.45 us -> 0.43 us  [sum_blocks(): pl.pallas_call(sum_kernel, out_shape=jax.ShapeDtypeStruct((dense.shape[1]...]
    unnamed x8 -> x12, local copies, waits for them, and re-layouts: 0.66 us -> 2.41 us
    all_to_all x1, blocking collectives: 13.1 us -> 14.4 us  [body(): got = lax.all_to_all(parts, 'rows', split_axis=0, concat_axis=0, tiled=True)]
    pallas_call x1, Pallas kernels: 2.22 us -> 0.92 us  [layer(): pl.pallas_call(layer_kernel, out_shape=(jax.ShapeDtypeStruct((half, wide)...]
    ppermute x9, waiting for transfers between devices: 6.61 us -> 7.88 us  [swap_to(): return lax.ppermute(value, BOTH, pairs)]
    pallas_call x1, Pallas kernels: 1.55 us -> 0.62 us  [finish(): pl.pallas_call(finish_kernel, out_shape=(jax.ShapeDtypeStruct((share, 128...]
    concatenate x2 -> x1, other arithmetic: 0.87 us -> 0.01 us  [body(): jnp.concatenate(pieces)]
  transfers between devices with their start and end apart: 9 -> 9, of which waited for: 4 -> 4; matrix products, arithmetic and copies ran while one was open for 1% -> 0% of each run, Pallas kernels for 15% -> 4%
where the time goes in v2:
time: 38.9 us; the launch traced here: 38.6 us
  blocking collectives  14.4 us (37%)
  starting transfers between devices  9 us (23%)
  waiting for transfers between devices  7.88 us (20%)
  Pallas kernels  3.35 us (9%)
  local copies, waits for them, and re-layouts  3.22 us (8%)
  between operations  0.72 us (2%)
    all_to_all x1, blocking collectives, body(): got = lax.all_to_all(parts, 'rows', split_axis=0, concat_axis=0, tiled=True)  14.4 us
    ppermute x9, starting transfers between devices, swap_to(): return lax.ppermute(value, BOTH, pairs)  9 us
    ppermute x9, waiting for transfers between devices, swap_to(): return lax.ppermute(value, BOTH, pairs)  7.88 us
    unnamed x12, local copies, waits for them, and re-layouts  2.41 us
    pallas_call x1, Pallas kernels, place_blocks(): pl.pallas_call(functools.partial(place_kernel, digit_groups(owners)), out...  1.37 us
    pallas_call x1, Pallas kernels, layer(): pl.pallas_call(layer_kernel, out_shape=(jax.ShapeDtypeStruct((half, wide)...  0.92 us
    dynamic_slice x1, local copies, waits for them, and re-layouts, body(): lax.dynamic_slice_in_dim(features, (side ^ flip) * half_rows, half_rows, 0)  0.82 us
  transfers between devices with their start and end apart: 9, of which 4 were waited for; matrix products, arithmetic and copies ran while one was open for 0% of the time, Pallas kernels for 4%

profile of v2, /device:TPU:0, one launch (start us, length us, event | category | flops | bytes accessed | tf_op | source)
XLA Modules:
  0.0 38.6 jit_solution(930450802097600109)
XLA Ops:
  0.6 0.0 copy-start.2
  0.7 0.8 %constant_dynamic-slice_fusion.1 = (bf16[128,128]{1,0:T(8,128)(2,1)S(1)}, bf16[128,128]{1,0:T(8,128)(2,1)S(1)}) fusion(bf16[256,128]{1,0:T(8,128)(2,1)} %param.7, s32[]{:T(128)S(6)} %select_n.6, s32[]{:T(128)S(6)} %select_n.7), kind=kLoop, calls=%fused_computation.2 | loop fusion | bytes 131080 | tf_op jit(solution)/shard_map/dynamic_slice | solution.py:214
  1.5 4.5 %collective-permute-start.2 = (bf16[128,128]{1,0:T(8,128)(2,1)S(1)}, bf16[128,128]{1,0:T(8,128)(2,1)S(1)}, u32[]{:S(2)}, u32[]{:S(2)}) collective-permute-start(bf16[128,128]{1,0:T(8,128)(2,1)S(1)} %get-tuple-element.18), channel_id=1, source_target_pairs={{0,25},{1,24},{2,27},{3,26},{4,29},{5,28},{6,31},{7,30},{8,17},{9,... | collective-permute-start | bytes 98312 | tf_op jit(solution)/shard_map/ppermute | solution.py:29
  6.0 0.0 collective-permute-start.1
  6.0 0.9 %collective-permute-start = (bf16[128,128]{1,0:T(8,128)(2,1)S(1)}, bf16[128,128]{1,0:T(8,128)(2,1)S(1)}, u32[]{:S(2)}, u32[]{:S(2)}) collective-permute-start(bf16[128,128]{1,0:T(8,128)(2,1)S(1)} %get-tuple-element.18), channel_id=1, source_target_pairs={{0,9},{1,8},{2,11},{3,10},{4,13},{5,12},{6,15},{7,14},{8,1},{9,0},... | collective-permute-start | bytes 98312 | tf_op jit(solution)/shard_map/ppermute | solution.py:29
  6.9 0.0 copy-done.2
  6.9 0.0 collective-permute-start.3
  6.9 0.0 copy-start.3
  6.9 0.0 copy-start.5
  6.9 0.7 %copy-done.3 = s32[1,4,16]{2,1,0:T(4,128)S(1)} copy-done((s32[1,4,16]{2,1,0:T(4,128)S(1)}, s32[1,4,16]{2,1,0:T(4,128)}, u32[]{:S(2)}) %copy-start.3) | copy-done | bytes 280
  7.6 0.0 copy-done.5
  7.6 0.0 copy-start
  7.6 1.0 %copy-done = bf16[1,4,16,4096]{3,2,1,0:T(8,128)(2,1)S(1)} copy-done((bf16[1,4,16,4096]{3,2,1,0:T(8,128)(2,1)S(1)}, bf16[1,4,16,4096]{3,2,1,0:T(8,128)(2,1)}, u32[]{:S(2)}) %copy-start) | copy-done | bytes 524312
  8.6 1.4 %place.1.dense = bf16[16,256,128]{2,1,0:T(8,128)(2,1)S(1)} custom-call(s32[1]{0:T(128)} %bitcast.1.row, s32[1,4]{1,0:T(1,128)S(1)} %copy-done.5, s32[4,16]{1,0:T(4,128)S(1)} %bitcast.8, bf16[4,16,4096]{2,1,0:T(8,128)(2,1)S(1)} %bitcast.7), custom_call_target="tpu_custom_call" | custom-call | tf_op jit(solution)/shard_map/place/pallas_call | solution.py:92
  10.0 0.0 collective-permute-done.2
  10.0 0.5 %collective-permute-done.1 = bf16[128,128]{1,0:T(8,128)(2,1)S(1)} collective-permute-done((bf16[128,128]{1,0:T(8,128)(2,1)S(1)}, bf16[128,128]{1,0:T(8,128)(2,1)S(1)}, u32[]{:S(2)}, u32[]{:S(2)}) %collective-permute-start.1) | collective-permute-done | bytes 32800 | tf_op jit(solution)/shard_map/ppermute | solution.py:29
  10.5 0.0 collective-permute-done
  10.5 0.0 copy-start.1
  10.5 0.0 collective-permute-done.3.cot_other
  10.5 2.5 %collective-permute-start.7 = (bf16[512,128]{1,0:T(8,128)(2,1)S(1)}, bf16[512,128]{1,0:T(8,128)(2,1)S(1)}, u32[]{:S(2)}, u32[]{:S(2)}) collective-permute-start(bf16[512,128]{1,0:T(8,128)(2,1)S(1)} %pad_maximum_fusion), channel_id=1, source_target_pairs={{0,7},{1,6},{2,5},{3,4},{4,3},{5,2},{6,1},{7,0},{8,15},{9,14},{10,... | collective-permute-start | bytes 393224 | tf_op jit(solution)/shard_map/ppermute | solution.py:29
  13.0 0.3 collective-permute-start.6
  13.3 0.5 %collective-permute-start.5 = (bf16[512,128]{1,0:T(8,128)(2,1)S(1)}, bf16[512,128]{1,0:T(8,128)(2,1)S(1)}, u32[]{:S(2)}, u32[]{:S(2)}) collective-permute-start(bf16[512,128]{1,0:T(8,128)(2,1)S(1)} %pad_maximum_fusion), channel_id=1, source_target_pairs={{0,3},{1,2},{2,1},{3,0},{4,7},{5,6},{6,5},{7,4},{8,11},{9,10},{10,... | collective-permute-start | bytes 393224 | tf_op jit(solution)/shard_map/ppermute | solution.py:29
  13.8 0.2 collective-permute-start.4
  14.0 3.0 %collective-permute-done.7.refs_3_ = bf16[512,128]{1,0:T(8,128)(2,1)S(1)} collective-permute-done((bf16[512,128]{1,0:T(8,128)(2,1)S(1)}, bf16[512,128]{1,0:T(8,128)(2,1)S(1)}, u32[]{:S(2)}, u32[]{:S(2)}) %collective-permute-start.7) | collective-permute-done | bytes 131104 | tf_op jit(solution)/shard_map/ppermute | solution.py:29
  16.9 3.2 %collective-permute-done.6.refs_2_ = bf16[512,128]{1,0:T(8,128)(2,1)S(1)} collective-permute-done((bf16[512,128]{1,0:T(8,128)(2,1)S(1)}, bf16[512,128]{1,0:T(8,128)(2,1)S(1)}, u32[]{:S(2)}, u32[]{:S(2)}) %collective-permute-start.6) | collective-permute-done | bytes 131104 | tf_op jit(solution)/shard_map/ppermute | solution.py:29
  20.1 0.0 collective-permute-done.5.refs_1_
  20.1 0.0 collective-permute-done.4.refs_0_
  20.1 0.4 %block_sum.1.mine = f32[256,128]{1,0:T(8,128)S(1)} custom-call(bf16[16,256,128]{2,1,0:T(8,128)(2,1)S(1)} %place.1.dense, bf16[512,128]{1,0:T(8,128)(2,1)S(1)} %collective-permute-done.4.refs_0_, bf16[512,128]{1,0:T(8,128)(2,1)S(1)} %collective-permute-done.5.refs_1_, bf16[512,128]{1,0:T(8,128)(2,1)S(1)} %collective-permute-done.6.refs_2_, ...), custom_call_target="tpu_custom_call" | custom-call | tf_op jit(solution)/shard_map/block_sum/pallas_call | solution.py:127
  20.5 0.2 collective-permute-start.8
  20.7 1.2 %collective-permute-done.8.other = f32[256,128]{1,0:T(8,128)S(1)} collective-permute-done((f32[256,128]{1,0:T(8,128)S(1)}, f32[256,128]{1,0:T(8,128)S(1)}, u32[]{:S(2)}, u32[]{:S(2)}) %collective-permute-start.8) | collective-permute-done | bytes 131104 | tf_op jit(solution)/shard_map/ppermute | solution.py:29
  22.0 0.0 copy-start.4
  22.0 0.0 copy-done.1
  22.0 0.7 %copy-done.4 = f32[256]{0:T(256)S(1)} copy-done((f32[256]{0:T(256)S(1)}, f32[256]{0:T(256)}, u32[]{:S(2)}) %copy-start.4) | copy-done | bytes 1048
  22.6 0.9 %layer.1 = (bf16[128,256]{1,0:T(8,128)(2,1)}, f32[16,24,128]{2,1,0:T(8,128)S(1)}) custom-call(s32[1]{0:T(128)} %bitcast.side, f32[256,128]{1,0:T(8,128)S(1)} %block_sum.1.mine, f32[256,128]{1,0:T(8,128)S(1)} %collective-permute-done.8.other, bf16[128,256]{1,0:T(8,128)(2,1)S(1)} %copy-done.1, f32[1,256]{1,0:T(1,128)S(1)} %bitcast.9, ...), custom_call_target="tpu_custom_call" | custom-call | tf_op jit(solution)/shard_map/layer/pallas_call | solution.py:164
  23.6 14.4 %all_to_all.5.got = f32[16,24,128]{2,1,0:T(8,128)S(1)} all-to-all(f32[16,24,128]{2,1,0:T(8,128)S(1)} %get-tuple-element.14), channel_id=1, replica_groups=mesh['rows'=16,'rep'=2] {'rows'}, dimensions={0} | all-to-all | bytes 393216 | tf_op jit(solution)/shard_map/all_to_all | solution.py:229
  38.0 0.6 %finish.1 = (f32[16,128]{1,0:T(8,128)}, f32[1,16]{1,0:T(1,128)}) custom-call(s32[1]{0:T(128)} %bitcast.1.row, f32[16,24,128]{2,1,0:T(8,128)S(1)} %all_to_all.5.got), custom_call_target="tpu_custom_call" | custom-call | tf_op jit(solution)/shard_map/finish/pallas_call | solution.py:190
  (1 shorter events, 0.0 us)
Async XLA Ops:
  0.6 6.2 %copy-start.2 = (bf16[128,256]{1,0:T(8,128)(2,1)S(1)}, bf16[128,256]{1,0:T(8,128)(2,1)}, u32[]{:S(2)}) copy-start(bf16[128,256]{1,0:T(8,128)(2,1)} %cot_mine.1) | copy-start | bytes 196612
  1.5 8.5 %collective-permute-start.2 = (bf16[128,128]{1,0:T(8,128)(2,1)S(1)}, bf16[128,128]{1,0:T(8,128)(2,1)S(1)}, u32[]{:S(2)}, u32[]{:S(2)}) collective-permute-start(bf16[128,128]{1,0:T(8,128)(2,1)S(1)} %get-tuple-element.18), channel_id=1, source_target_pairs={{0,25},{1,24},{2,27},{3,26},{4,29},{5,28},{6,31},{7,30},{8,17},{9,... | collective-permute-start | bytes 98312 | tf_op jit(solution)/shard_map/ppermute | solution.py:29
  6.0 4.5 %collective-permute-start.1 = (bf16[128,128]{1,0:T(8,128)(2,1)S(1)}, bf16[128,128]{1,0:T(8,128)(2,1)S(1)}, u32[]{:S(2)}, u32[]{:S(2)}) collective-permute-start(bf16[128,128]{1,0:T(8,128)(2,1)S(1)} %get-tuple-element.18), channel_id=1, source_target_pairs={{0,17},{1,16},{2,19},{3,18},{4,21},{5,20},{6,23},{7,22},{8,25},{9,... | collective-permute-start | bytes 98312 | tf_op jit(solution)/shard_map/ppermute | solution.py:29
  6.0 4.5 %collective-permute-start = (bf16[128,128]{1,0:T(8,128)(2,1)S(1)}, bf16[128,128]{1,0:T(8,128)(2,1)S(1)}, u32[]{:S(2)}, u32[]{:S(2)}) collective-permute-start(bf16[128,128]{1,0:T(8,128)(2,1)S(1)} %get-tuple-element.18), channel_id=1, source_target_pairs={{0,9},{1,8},{2,11},{3,10},{4,13},{5,12},{6,15},{7,14},{8,1},{9,0},... | collective-permute-start | bytes 98312 | tf_op jit(solution)/shard_map/ppermute | solution.py:29
  6.9 3.7 %collective-permute-start.3 = (bf16[128,256]{1,0:T(8,128)(2,1)S(1)}, bf16[128,256]{1,0:T(8,128)(2,1)S(1)}, u32[]{:S(2)}, u32[]{:S(2)}) collective-permute-start(bf16[128,256]{1,0:T(8,128)(2,1)S(1)} %copy-done.2), channel_id=1, source_target_pairs={{0,1},{1,0},{2,3},{3,2},{4,5},{5,4},{6,7},{7,6},{8,9},{9,8},{10,11... | collective-permute-start | bytes 196616 | tf_op jit(solution)/shard_map/ppermute | solution.py:29
  6.9 0.7 %copy-start.3 = (s32[1,4,16]{2,1,0:T(4,128)S(1)}, s32[1,4,16]{2,1,0:T(4,128)}, u32[]{:S(2)}) copy-start(s32[1,4,16]{2,1,0:T(4,128)} %param.11) | copy-start | bytes 772
  6.9 0.7 %copy-start.5 = (s32[1,4]{1,0:T(1,128)S(1)}, s32[1,4]{1,0:T(1,128)}, u32[]{:S(2)}) copy-start(s32[1,4]{1,0:T(1,128)} %counts.1) | copy-start | bytes 52
  7.6 1.0 %copy-start = (bf16[1,4,16,4096]{3,2,1,0:T(8,128)(2,1)S(1)}, bf16[1,4,16,4096]{3,2,1,0:T(8,128)(2,1)}, u32[]{:S(2)}) copy-start(bf16[1,4,16,4096]{3,2,1,0:T(8,128)(2,1)} %param.12) | copy-start | bytes 1572868
  10.5 11.4 %copy-start.1 = (bf16[128,256]{1,0:T(8,128)(2,1)S(1)}, bf16[128,256]{1,0:T(8,128)(2,1)}, u32[]{:S(2)}) copy-start(bf16[128,256]{1,0:T(8,128)(2,1)} %weight.1) | copy-start | bytes 196612
  10.5 6.4 %collective-permute-start.7 = (bf16[512,128]{1,0:T(8,128)(2,1)S(1)}, bf16[512,128]{1,0:T(8,128)(2,1)S(1)}, u32[]{:S(2)}, u32[]{:S(2)}) collective-permute-start(bf16[512,128]{1,0:T(8,128)(2,1)S(1)} %pad_maximum_fusion), channel_id=1, source_target_pairs={{0,7},{1,6},{2,5},{3,4},{4,3},{5,2},{6,1},{7,0},{8,15},{9,14},{10,... | collective-permute-start | bytes 393224 | tf_op jit(solution)/shard_map/ppermute | solution.py:29
  13.0 7.1 %collective-permute-start.6 = (bf16[512,128]{1,0:T(8,128)(2,1)S(1)}, bf16[512,128]{1,0:T(8,128)(2,1)S(1)}, u32[]{:S(2)}, u32[]{:S(2)}) collective-permute-start(bf16[512,128]{1,0:T(8,128)(2,1)S(1)} %pad_maximum_fusion), channel_id=1, source_target_pairs={{0,5},{1,4},{2,7},{3,6},{4,1},{5,0},{6,3},{7,2},{8,13},{9,12},{10,... | collective-permute-start | bytes 393224 | tf_op jit(solution)/shard_map/ppermute | solution.py:29
  13.3 6.8 %collective-permute-start.5 = (bf16[512,128]{1,0:T(8,128)(2,1)S(1)}, bf16[512,128]{1,0:T(8,128)(2,1)S(1)}, u32[]{:S(2)}, u32[]{:S(2)}) collective-permute-start(bf16[512,128]{1,0:T(8,128)(2,1)S(1)} %pad_maximum_fusion), channel_id=1, source_target_pairs={{0,3},{1,2},{2,1},{3,0},{4,7},{5,6},{6,5},{7,4},{8,11},{9,10},{10,... | collective-permute-start | bytes 393224 | tf_op jit(solution)/shard_map/ppermute | solution.py:29
  13.8 6.3 %collective-permute-start.4 = (bf16[512,128]{1,0:T(8,128)(2,1)S(1)}, bf16[512,128]{1,0:T(8,128)(2,1)S(1)}, u32[]{:S(2)}, u32[]{:S(2)}) collective-permute-start(bf16[512,128]{1,0:T(8,128)(2,1)S(1)} %pad_maximum_fusion), channel_id=1, source_target_pairs={{0,1},{1,0},{2,3},{3,2},{4,5},{5,4},{6,7},{7,6},{8,9},{9,8},{10,11... | collective-permute-start | bytes 393224 | tf_op jit(solution)/shard_map/ppermute | solution.py:29
  20.5 1.4 %collective-permute-start.8 = (f32[256,128]{1,0:T(8,128)S(1)}, f32[256,128]{1,0:T(8,128)S(1)}, u32[]{:S(2)}, u32[]{:S(2)}) collective-permute-start(f32[256,128]{1,0:T(8,128)S(1)} %block_sum.1.mine), channel_id=1, source_target_pairs={{0,1},{1,0},{2,3},{3,2},{4,5},{5,4},{6,7},{7,6},{8,9},{9,8},{10,11... | collective-permute-start | bytes 393224 | tf_op jit(solution)/shard_map/ppermute | solution.py:29
  22.0 0.7 %copy-start.4 = (f32[256]{0:T(256)S(1)}, f32[256]{0:T(256)}, u32[]{:S(2)}) copy-start(f32[256]{0:T(256)} %param.9) | copy-start | bytes 3076

commit v3 on v2

--- a/solution.py
+++ b/solution.py
@@ -24,8 +24,8 @@
     return groups
 
 
-def swap_to(value, mask, owners):
-    pairs = [(i, i ^ (2 * mask + 1)) for i in range(2 * owners)]
+def across(value, mask, owners, swap):
+    pairs = [(i, i ^ (2 * mask + swap)) for i in range(2 * owners)]
     return lax.ppermute(value, BOTH, pairs)
 
 
@@ -33,9 +33,12 @@
     return pltpu.CompilerParams(vmem_limit_bytes=(8 if owners <= 16 else 48) << 20)
 
 
-def place_kernel(groups, row, counts, cols, vals, dense):
+def place_kernel(groups, index, counts, cols, vals, cot, weight, bias, dense, cot_out, weight_out, bias_out):
     nblk, slots, flat = vals.shape
     owners = dense.shape[0]
+    cot_out[...] = cot[...]
+    weight_out[...] = weight[...]
+    bias_out[...] = bias[...]
     wide = flat // 128
     deep = 16 * slots
     lane = lax.broadcasted_iota(jnp.int32, (slots, deep), 1)
@@ -43,7 +46,7 @@
     spread = (lane % slots == slot).astype(jnp.bfloat16)
     named = jnp.dot(cols[...].astype(jnp.bfloat16), spread, preferred_element_type=jnp.float32)
     named = named.astype(jnp.int32)
-    apart = (named >> 1) ^ row[0]
+    apart = (named >> 1) ^ (index[0] >> 1)
     place = jnp.zeros_like(apart)
     stride = 1
     for shift, radix in groups:
@@ -86,17 +89,22 @@
             pl.loop(0, owners // 16)(put)
 
 
-def place_blocks(row, counts, cols, vals, owners):
+def place_blocks(index, counts, cols, vals, cot, weight, bias, owners):
     nblk, slots, flat = vals.shape
     wide = flat // 128
     return pl.pallas_call(
         functools.partial(place_kernel, digit_groups(owners)),
-        out_shape=jax.ShapeDtypeStruct((owners, 2 * nblk * wide, 128), jnp.bfloat16),
-        in_specs=[SMEM, SMEM, VMEM, VMEM],
-        out_specs=VMEM,
+        out_shape=(
+            jax.ShapeDtypeStruct((owners, 2 * nblk * wide, 128), jnp.bfloat16),
+            jax.ShapeDtypeStruct(cot.shape, cot.dtype),
+            jax.ShapeDtypeStruct(weight.shape, weight.dtype),
+            jax.ShapeDtypeStruct(bias.shape, bias.dtype),
+        ),
+        in_specs=[SMEM, SMEM] + [VMEM] * 5,
+        out_specs=(VMEM,) * 4,
         compiler_params=limit(owners),
         name="place",
-    )(row, counts, cols, vals)
+    )(index, counts, cols, vals, cot, weight, bias)
 
 
 def sum_kernel(dense, *refs):
@@ -134,16 +142,17 @@
     )(dense, *pieces)
 
 
-def layer_kernel(side, mine, other, weight, bias, cot_mine, cot_other, act, parts, value):
+def layer_kernel(index, mine, other, weight, bias, cot_mine, cot_other, act, parts, value):
     half = cot_mine.shape[0]
+    side = index[0] & 1
     owners, chunk, _ = parts.shape
     share = 256 // owners
     aggregated = (mine[...] + other[...]).astype(jnp.bfloat16)
     pre = jnp.dot(aggregated, weight[...], preferred_element_type=jnp.float32) + bias[...]
     sig = 1.0 / (1.0 + jnp.exp(-pre))
     value[...] = pre * sig
-    act[...] = value[pl.ds(pl.multiple_of(side[0] * half, half), half), :].astype(jnp.bfloat16)
-    first = side[0] == 0
+    act[...] = value[pl.ds(pl.multiple_of(side * half, half), half), :].astype(jnp.bfloat16)
+    first = side == 0
     cot_a = cot_mine[...].astype(jnp.float32)
     cot_b = cot_other[...].astype(jnp.float32)
     cot = jnp.concatenate([jnp.where(first, cot_a, cot_b), jnp.where(first, cot_b, cot_a)], axis=0)
@@ -157,7 +166,7 @@
         parts[r] = jnp.concatenate([grad[r * share : (r + 1) * share], tail], axis=0)
 
 
-def layer(side, mine, other, weight, bias, cot_mine, cot_other, owners):
+def layer(index, mine, other, weight, bias, cot_mine, cot_other, owners):
     nodes = mine.shape[0]
     half, wide = cot_mine.shape
     chunk = -(-(wide // owners + 2) // 8) * 8
@@ -172,20 +181,20 @@
         scratch_shapes=[pltpu.VMEM((nodes, wide), jnp.float32)],
         compiler_params=limit(owners),
         name="layer",
-    )(side, mine, other, weight, bias, cot_mine, cot_other)
-
-
-def finish_kernel(row, got, weight_grad, bias_grad):
+    )(index, mine, other, weight, bias, cot_mine, cot_other)
+
+
+def finish_kernel(index, got, weight_grad, bias_grad):
     share = weight_grad.shape[0]
     total = jnp.sum(got[...], axis=0)
     weight_grad[...] = total[:share]
     flat = jnp.concatenate([total[share : share + 1], total[share + 1 : share + 2]], axis=1)
     flat = jnp.broadcast_to(flat, (8, 256))
-    flat = pltpu.roll(flat, lax.rem(256 - row[0] * share, 256), 1)
+    flat = pltpu.roll(flat, lax.rem(256 - (index[0] >> 1) * share, 256), 1)
     bias_grad[...] = flat[:1, :share]
 
 
-def finish(row, got):
+def finish(index, got):
     share = 256 // got.shape[0]
     return pl.pallas_call(
         finish_kernel,
@@ -197,37 +206,36 @@
         out_specs=(VMEM, VMEM),
         compiler_params=limit(got.shape[0]),
         name="finish",
-    )(row, got)
+    )(index, got)
 
 
 def body(features, weight, bias, block_count, block_cols, block_vals, cotangent):
     side = lax.axis_index("rep")
-    row = lax.axis_index("rows")
     owners = lax.axis_size("rows")
     groups = digit_groups(owners)
     half_rows = features.shape[0] // 2
 
-    row_arr = row.reshape(1).astype(jnp.int32)
-    dense = place_blocks(row_arr, block_count, block_cols[0], block_vals[0], owners)
-
-    flip = (len(groups) - 1) & 1
-    keep = lax.dynamic_slice_in_dim(features, (side ^ flip) * half_rows, half_rows, 0)
-    give = lax.dynamic_slice_in_dim(features, (1 - side ^ flip) * half_rows, half_rows, 0)
+    keep = lax.dynamic_slice_in_dim(features, side * half_rows, half_rows, 0)
+    give = lax.dynamic_slice_in_dim(features, (1 - side) * half_rows, half_rows, 0)
     shift, radix = groups[0]
-    pieces = [keep] + [swap_to(give, s << shift, owners) for s in range(1, radix)]
-    cot_other = swap_to(cotangent, 0, owners)
+    pieces = [keep] + [across(give, s << shift, owners, 1) for s in range(1, radix)]
+    vals = block_vals[0]
     for shift, radix in groups[1:]:
-        held, dense, cot_other = lax.optimization_barrier((jnp.concatenate(pieces), dense, cot_other))
-        pieces = [swap_to(held, s << shift, owners) for s in range(radix)]
+        held, vals = lax.optimization_barrier((jnp.concatenate(pieces), vals))
+        pieces = [held] + [across(held, s << shift, owners, 0) for s in range(1, radix)]
+
+    index = lax.axis_index(BOTH).reshape(1).astype(jnp.int32)
+    dense, cot_mine, weight, bias = place_blocks(
+        index, block_count, block_cols[0], vals, cotangent, weight, bias.reshape(1, -1), owners
+    )
+    cot_other = across(cot_mine, 0, owners, 1)
+    dense, cot_other = lax.optimization_barrier((dense, cot_other))
 
     mine = sum_blocks(dense, pieces)
-    other = swap_to(mine, 0, owners)
-    side_arr = side.reshape(1).astype(jnp.int32)
-    activated, parts = layer(
-        side_arr, mine, other, weight, bias.reshape(1, -1), cotangent, cot_other, owners
-    )
+    other = across(mine, 0, owners, 1)
+    activated, parts = layer(index, mine, other, weight, bias, cot_mine, cot_other, owners)
     got = lax.all_to_all(parts, "rows", split_axis=0, concat_axis=0, tiled=True)
-    weight_grad, bias_grad = finish(row_arr, got)
+    weight_grad, bias_grad = finish(index, got)
     return activated, weight_grad.T, bias_grad.reshape(-1)
 
 

time: 38.9 us -> 37.1 us (0.954)
  blocking collectives: 14.4 us -> 13.3 us
  local copies, waits for them, and re-layouts: 3.22 us -> 2.51 us
    all_to_all x1, blocking collectives: 14.4 us -> 13.3 us  [body(): got = lax.all_to_all(parts, 'rows', split_axis=0, concat_axis=0, tiled=True)]
    unnamed x12, local copies, waits for them, and re-layouts: 2.41 us -> 1.73 us
    ppermute x9 -> x8, starting transfers between devices: 9 us -> 9.11 us  [across(): return lax.ppermute(value, BOTH, pairs)]
    ppermute x9 -> x8, waiting for transfers between devices: 7.88 us -> 7.84 us  [across(): return lax.ppermute(value, BOTH, pairs)]
  transfers between devices with their start and end apart: 9 -> 8, of which waited for: 4 -> 6; matrix products, arithmetic and copies ran while one was open for 0% -> 0% of each run, Pallas kernels for 4% -> 4%
where the time goes in v3:
time: 37.1 us; the launch traced here: 36.8 us
  blocking collectives  13.3 us (36%)
  starting transfers between devices  9.11 us (25%)
  waiting for transfers between devices  7.84 us (21%)
  Pallas kernels  3.35 us (9%)
  local copies, waits for them, and re-layouts  2.51 us (7%)
  between operations  0.7 us (2%)
    all_to_all x1, blocking collectives, body(): got = lax.all_to_all(parts, 'rows', split_axis=0, concat_axis=0, tiled=True)  13.3 us
    ppermute x8, starting transfers between devices, across(): return lax.ppermute(value, BOTH, pairs)  9.11 us
    ppermute x8, waiting for transfers between devices, across(): return lax.ppermute(value, BOTH, pairs)  7.84 us
    unnamed x12, local copies, waits for them, and re-layouts  1.73 us
    pallas_call x1, Pallas kernels, place_blocks(): pl.pallas_call(functools.partial(place_kernel, digit_groups(owners)), out...  1.37 us
    pallas_call x1, Pallas kernels, layer(): pl.pallas_call(layer_kernel, out_shape=(jax.ShapeDtypeStruct((half, wide)...  0.93 us
    dynamic_slice x1, local copies, waits for them, and re-layouts, body(): keep = lax.dynamic_slice_in_dim(features, side * half_rows, half_rows, 0)  0.79 us
  transfers between devices with their start and end apart: 8, of which 6 were waited for; matrix products, arithmetic and copies ran while one was open for 0% of the time, Pallas kernels for 4%

profile of v3, /device:TPU:0, one launch (start us, length us, event | category | flops | bytes accessed | tf_op | source)
XLA Modules:
  0.0 36.8 jit_solution(7870094058336580560)
XLA Ops:
  0.6 0.8 %constant_dynamic-slice_fusion.1 = (bf16[128,128]{1,0:T(8,128)(2,1)S(1)}, bf16[128,128]{1,0:T(8,128)(2,1)S(1)}) fusion(bf16[256,128]{1,0:T(8,128)(2,1)} %param.7, s32[]{:T(128)S(6)} %select_n.6, s32[]{:T(128)S(6)} %select_n.7), kind=kLoop, calls=%fused_computation.2 | loop fusion | bytes 131080 | tf_op jit(solution)/shard_map/dynamic_slice | solution.py:218
  1.4 4.5 %collective-permute-start.2 = (bf16[128,128]{1,0:T(8,128)(2,1)S(1)}, bf16[128,128]{1,0:T(8,128)(2,1)S(1)}, u32[]{:S(2)}, u32[]{:S(2)}) collective-permute-start(bf16[128,128]{1,0:T(8,128)(2,1)S(1)} %get-tuple-element.28), channel_id=1, source_target_pairs={{0,25},{1,24},{2,27},{3,26},{4,29},{5,28},{6,31},{7,30},{8,17},{9,... | collective-permute-start | bytes 98312 | tf_op jit(solution)/shard_map/ppermute | solution.py:29
  5.9 0.0 collective-permute-start.1
  5.9 0.9 %collective-permute-start = (bf16[128,128]{1,0:T(8,128)(2,1)S(1)}, bf16[128,128]{1,0:T(8,128)(2,1)S(1)}, u32[]{:S(2)}, u32[]{:S(2)}) collective-permute-start(bf16[128,128]{1,0:T(8,128)(2,1)S(1)} %get-tuple-element.28), channel_id=1, source_target_pairs={{0,9},{1,8},{2,11},{3,10},{4,13},{5,12},{6,15},{7,14},{8,1},{9,0},... | collective-permute-start | bytes 98312 | tf_op jit(solution)/shard_map/ppermute | solution.py:29
  6.8 0.9 %collective-permute-done.2 = bf16[128,128]{1,0:T(8,128)(2,1)S(1)} collective-permute-done((bf16[128,128]{1,0:T(8,128)(2,1)S(1)}, bf16[128,128]{1,0:T(8,128)(2,1)S(1)}, u32[]{:S(2)}, u32[]{:S(2)}) %collective-permute-start.2) | collective-permute-done | bytes 32800 | tf_op jit(solution)/shard_map/ppermute | solution.py:29
  7.7 2.8 %collective-permute-done.1 = bf16[128,128]{1,0:T(8,128)(2,1)S(1)} collective-permute-done((bf16[128,128]{1,0:T(8,128)(2,1)S(1)}, bf16[128,128]{1,0:T(8,128)(2,1)S(1)}, u32[]{:S(2)}, u32[]{:S(2)}) %collective-permute-start.1) | collective-permute-done | bytes 32800 | tf_op jit(solution)/shard_map/ppermute | solution.py:29
  10.4 0.0 collective-permute-done
  10.5 0.0 copy-start.1
  10.5 0.0 copy-start.2
  10.5 2.5 %collective-permute-start.6 = (bf16[512,128]{1,0:T(8,128)(2,1)S(1)}, bf16[512,128]{1,0:T(8,128)(2,1)S(1)}, u32[]{:S(2)}, u32[]{:S(2)}) collective-permute-start(bf16[512,128]{1,0:T(8,128)(2,1)S(1)} %pad_maximum_fusion.refs_0_), channel_id=1, source_target_pairs={{0,6},{1,7},{2,4},{3,5},{4,2},{5,3},{6,0},{7,1},{8,14},{9,15},{10,... | collective-permute-start | bytes 393224 | tf_op jit(solution)/shard_map/ppermute | solution.py:29
  13.0 0.5 %collective-permute-start.5 = (bf16[512,128]{1,0:T(8,128)(2,1)S(1)}, bf16[512,128]{1,0:T(8,128)(2,1)S(1)}, u32[]{:S(2)}, u32[]{:S(2)}) collective-permute-start(bf16[512,128]{1,0:T(8,128)(2,1)S(1)} %pad_maximum_fusion.refs_0_), channel_id=1, source_target_pairs={{0,4},{1,5},{2,6},{3,7},{4,0},{5,1},{6,2},{7,3},{8,12},{9,13},{10,... | collective-permute-start | bytes 393224 | tf_op jit(solution)/shard_map/ppermute | solution.py:29
  13.5 0.5 %collective-permute-start.4 = (bf16[512,128]{1,0:T(8,128)(2,1)S(1)}, bf16[512,128]{1,0:T(8,128)(2,1)S(1)}, u32[]{:S(2)}, u32[]{:S(2)}) collective-permute-start(bf16[512,128]{1,0:T(8,128)(2,1)S(1)} %pad_maximum_fusion.refs_0_), channel_id=1, source_target_pairs={{0,2},{1,3},{2,0},{3,1},{4,6},{5,7},{6,4},{7,5},{8,10},{9,11},{10,... | collective-permute-start | bytes 393224 | tf_op jit(solution)/shard_map/ppermute | solution.py:29
  14.0 0.0 copy-start.3
  14.0 0.0 copy-start.4
  14.0 0.0 copy-start.5
  14.0 0.0 copy-done.1
  14.1 0.0 copy-done.2
  14.1 0.7 %copy-done.3 = s32[1,4,16]{2,1,0:T(4,128)S(1)} copy-done((s32[1,4,16]{2,1,0:T(4,128)S(1)}, s32[1,4,16]{2,1,0:T(4,128)}, u32[]{:S(2)}) %copy-start.3) | copy-done | bytes 280
  14.7 0.0 copy-done.4
  14.7 0.0 copy-done.5
  14.7 0.0 copy-start
  14.7 1.0 %copy-done = bf16[1,4,16,4096]{3,2,1,0:T(8,128)(2,1)S(1)} copy-done((bf16[1,4,16,4096]{3,2,1,0:T(8,128)(2,1)S(1)}, bf16[1,4,16,4096]{3,2,1,0:T(8,128)(2,1)}, u32[]{:S(2)}) %copy-start) | copy-done | bytes 524312
  15.8 1.4 %place.1 = (bf16[16,256,128]{2,1,0:T(8,128)(2,1)S(1)}, bf16[128,256]{1,0:T(8,128)(2,1)S(1)}, bf16[128,256]{1,0:T(8,128)(2,1)S(1)}, f32[1,256]{1,0:T(1,128)S(1)}) custom-call(s32[1]{0:T(128)} %bitcast.index, s32[1,4]{1,0:T(1,128)S(1)} %copy-done.5, s32[4,16]{1,0:T(4,128)S(1)} %bitcast.7, bf16[4,16,4096]{2,1,0:T(8,128)(2,1)S(1)} %bitcast.6, ...), custom_call_target="tpu_custom_call" | custom-call | tf_op jit(solution)/shard_map/place/pallas_call | solution.py:95
  17.2 0.1 collective-permute-start.3
  17.2 1.2 %collective-permute-done.3.cot_other = bf16[128,256]{1,0:T(8,128)(2,1)S(1)} collective-permute-done((bf16[128,256]{1,0:T(8,128)(2,1)S(1)}, bf16[128,256]{1,0:T(8,128)(2,1)S(1)}, u32[]{:S(2)}, u32[]{:S(2)}) %collective-permute-start.3) | collective-permute-done | bytes 65568 | tf_op jit(solution)/shard_map/ppermute | solution.py:29
  18.5 0.0 collective-permute-done.6.refs_3_
  18.5 1.5 %collective-permute-done.5.refs_2_ = bf16[512,128]{1,0:T(8,128)(2,1)S(1)} collective-permute-done((bf16[512,128]{1,0:T(8,128)(2,1)S(1)}, bf16[512,128]{1,0:T(8,128)(2,1)S(1)}, u32[]{:S(2)}, u32[]{:S(2)}) %collective-permute-start.5) | collective-permute-done | bytes 131104 | tf_op jit(solution)/shard_map/ppermute | solution.py:29
  20.0 0.1 collective-permute-done.4.refs_1_
  20.1 0.4 %block_sum.1.mine = f32[256,128]{1,0:T(8,128)S(1)} custom-call(bf16[16,256,128]{2,1,0:T(8,128)(2,1)S(1)} %get-tuple-element.18.dense, bf16[512,128]{1,0:T(8,128)(2,1)S(1)} %pad_maximum_fusion.refs_0_, bf16[512,128]{1,0:T(8,128)(2,1)S(1)} %collective-permute-done.4.refs_1_, bf16[512,128]{1,0:T(8,128)(2,1)S(1)} %collective-permute-done.5.refs_2_, ...), custom_call_target="tpu_custom_call" | custom-call | tf_op jit(solution)/shard_map/block_sum/pallas_call | solution.py:135
  20.6 0.1 collective-permute-start.7
  20.6 1.3 %collective-permute-done.7.other = f32[256,128]{1,0:T(8,128)S(1)} collective-permute-done((f32[256,128]{1,0:T(8,128)S(1)}, f32[256,128]{1,0:T(8,128)S(1)}, u32[]{:S(2)}, u32[]{:S(2)}) %collective-permute-start.7) | collective-permute-done | bytes 131104 | tf_op jit(solution)/shard_map/ppermute | solution.py:29
  22.0 0.9 %layer.1 = (bf16[128,256]{1,0:T(8,128)(2,1)}, f32[16,24,128]{2,1,0:T(8,128)S(1)}) custom-call(s32[1]{0:T(128)} %bitcast.index, f32[256,128]{1,0:T(8,128)S(1)} %block_sum.1.mine, f32[256,128]{1,0:T(8,128)S(1)} %collective-permute-done.7.other, bf16[128,256]{1,0:T(8,128)(2,1)S(1)} %get-tuple-element.20.weight, f32[1,256]{1,0:T(1,128)S(1)} %get-tuple-element.21.bias, ...), custom_call_target="tpu_custom_call" | custom-call | tf_op jit(solution)/shard_map/layer/pallas_call | solution.py:173
  22.9 13.3 %all_to_all.5.got = f32[16,24,128]{2,1,0:T(8,128)S(1)} all-to-all(f32[16,24,128]{2,1,0:T(8,128)S(1)} %get-tuple-element.24), channel_id=1, replica_groups=mesh['rows'=16,'rep'=2] {'rows'}, dimensions={0} | all-to-all | bytes 393216 | tf_op jit(solution)/shard_map/all_to_all | solution.py:237
  36.2 0.6 %finish.1 = (f32[16,128]{1,0:T(8,128)}, f32[1,16]{1,0:T(1,128)}) custom-call(s32[1]{0:T(128)} %bitcast.index, f32[16,24,128]{2,1,0:T(8,128)S(1)} %all_to_all.5.got), custom_call_target="tpu_custom_call" | custom-call | tf_op jit(solution)/shard_map/finish/pallas_call | solution.py:199
  (1 shorter events, 0.0 us)
Async XLA Ops:
  1.4 6.3 %collective-permute-start.2 = (bf16[128,128]{1,0:T(8,128)(2,1)S(1)}, bf16[128,128]{1,0:T(8,128)(2,1)S(1)}, u32[]{:S(2)}, u32[]{:S(2)}) collective-permute-start(bf16[128,128]{1,0:T(8,128)(2,1)S(1)} %get-tuple-element.28), channel_id=1, source_target_pairs={{0,25},{1,24},{2,27},{3,26},{4,29},{5,28},{6,31},{7,30},{8,17},{9,... | collective-permute-start | bytes 98312 | tf_op jit(solution)/shard_map/ppermute | solution.py:29
  5.9 4.5 %collective-permute-start.1 = (bf16[128,128]{1,0:T(8,128)(2,1)S(1)}, bf16[128,128]{1,0:T(8,128)(2,1)S(1)}, u32[]{:S(2)}, u32[]{:S(2)}) collective-permute-start(bf16[128,128]{1,0:T(8,128)(2,1)S(1)} %get-tuple-element.28), channel_id=1, source_target_pairs={{0,17},{1,16},{2,19},{3,18},{4,21},{5,20},{6,23},{7,22},{8,25},{9,... | collective-permute-start | bytes 98312 | tf_op jit(solution)/shard_map/ppermute | solution.py:29
  5.9 4.5 %collective-permute-start = (bf16[128,128]{1,0:T(8,128)(2,1)S(1)}, bf16[128,128]{1,0:T(8,128)(2,1)S(1)}, u32[]{:S(2)}, u32[]{:S(2)}) collective-permute-start(bf16[128,128]{1,0:T(8,128)(2,1)S(1)} %get-tuple-element.28), channel_id=1, source_target_pairs={{0,9},{1,8},{2,11},{3,10},{4,13},{5,12},{6,15},{7,14},{8,1},{9,0},... | collective-permute-start | bytes 98312 | tf_op jit(solution)/shard_map/ppermute | solution.py:29
  10.5 3.6 %copy-start.1 = (bf16[128,256]{1,0:T(8,128)(2,1)S(1)}, bf16[128,256]{1,0:T(8,128)(2,1)}, u32[]{:S(2)}) copy-start(bf16[128,256]{1,0:T(8,128)(2,1)} %cot.1) | copy-start | bytes 196612
  10.5 3.6 %copy-start.2 = (bf16[128,256]{1,0:T(8,128)(2,1)S(1)}, bf16[128,256]{1,0:T(8,128)(2,1)}, u32[]{:S(2)}) copy-start(bf16[128,256]{1,0:T(8,128)(2,1)} %weight.1) | copy-start | bytes 196612
  10.5 8.0 %collective-permute-start.6 = (bf16[512,128]{1,0:T(8,128)(2,1)S(1)}, bf16[512,128]{1,0:T(8,128)(2,1)S(1)}, u32[]{:S(2)}, u32[]{:S(2)}) collective-permute-start(bf16[512,128]{1,0:T(8,128)(2,1)S(1)} %pad_maximum_fusion.refs_0_), channel_id=1, source_target_pairs={{0,6},{1,7},{2,4},{3,5},{4,2},{5,3},{6,0},{7,1},{8,14},{9,15},{10,... | collective-permute-start | bytes 393224 | tf_op jit(solution)/shard_map/ppermute | solution.py:29
  13.0 7.0 %collective-permute-start.5 = (bf16[512,128]{1,0:T(8,128)(2,1)S(1)}, bf16[512,128]{1,0:T(8,128)(2,1)S(1)}, u32[]{:S(2)}, u32[]{:S(2)}) collective-permute-start(bf16[512,128]{1,0:T(8,128)(2,1)S(1)} %pad_maximum_fusion.refs_0_), channel_id=1, source_target_pairs={{0,4},{1,5},{2,6},{3,7},{4,0},{5,1},{6,2},{7,3},{8,12},{9,13},{10,... | collective-permute-start | bytes 393224 | tf_op jit(solution)/shard_map/ppermute | solution.py:29
  13.5 6.6 %collective-permute-start.4 = (bf16[512,128]{1,0:T(8,128)(2,1)S(1)}, bf16[512,128]{1,0:T(8,128)(2,1)S(1)}, u32[]{:S(2)}, u32[]{:S(2)}) collective-permute-start(bf16[512,128]{1,0:T(8,128)(2,1)S(1)} %pad_maximum_fusion.refs_0_), channel_id=1, source_target_pairs={{0,2},{1,3},{2,0},{3,1},{4,6},{5,7},{6,4},{7,5},{8,10},{9,11},{10,... | collective-permute-start | bytes 393224 | tf_op jit(solution)/shard_map/ppermute | solution.py:29
  14.0 0.7 %copy-start.3 = (s32[1,4,16]{2,1,0:T(4,128)S(1)}, s32[1,4,16]{2,1,0:T(4,128)}, u32[]{:S(2)}) copy-start(s32[1,4,16]{2,1,0:T(4,128)} %param.11) | copy-start | bytes 772
  14.0 0.7 %copy-start.4 = (f32[256]{0:T(256)S(1)}, f32[256]{0:T(256)}, u32[]{:S(2)}) copy-start(f32[256]{0:T(256)} %param.9) | copy-start | bytes 3076
  14.0 0.7 %copy-start.5 = (s32[1,4]{1,0:T(1,128)S(1)}, s32[1,4]{1,0:T(1,128)}, u32[]{:S(2)}) copy-start(s32[1,4]{1,0:T(1,128)} %counts.1) | copy-start | bytes 52
  14.7 1.0 %copy-start = (bf16[1,4,16,4096]{3,2,1,0:T(8,128)(2,1)S(1)}, bf16[1,4,16,4096]{3,2,1,0:T(8,128)(2,1)}, u32[]{:S(2)}) copy-start(bf16[1,4,16,4096]{3,2,1,0:T(8,128)(2,1)} %param.12) | copy-start | bytes 1572868
  17.2 1.3 %collective-permute-start.3 = (bf16[128,256]{1,0:T(8,128)(2,1)S(1)}, bf16[128,256]{1,0:T(8,128)(2,1)S(1)}, u32[]{:S(2)}, u32[]{:S(2)}) collective-permute-start(bf16[128,256]{1,0:T(8,128)(2,1)S(1)} %get-tuple-element.17.cot_mine), channel_id=1, source_target_pairs={{0,1},{1,0},{2,3},{3,2},{4,5},{5,4},{6,7},{7,6},{8,9},{9,8},{10,11... | collective-permute-start | bytes 196616 | tf_op jit(solution)/shard_map/ppermute | solution.py:29
  20.6 1.4 %collective-permute-start.7 = (f32[256,128]{1,0:T(8,128)S(1)}, f32[256,128]{1,0:T(8,128)S(1)}, u32[]{:S(2)}, u32[]{:S(2)}) collective-permute-start(f32[256,128]{1,0:T(8,128)S(1)} %block_sum.1.mine), channel_id=1, source_target_pairs={{0,1},{1,0},{2,3},{3,2},{4,5},{5,4},{6,7},{7,6},{8,9},{9,8},{10,11... | collective-permute-start | bytes 393224 | tf_op jit(solution)/shard_map/ppermute | solution.py:29

commit v4 on v3

--- a/solution.py
+++ b/solution.py
@@ -33,12 +33,12 @@
     return pltpu.CompilerParams(vmem_limit_bytes=(8 if owners <= 16 else 48) << 20)
 
 
-def place_kernel(groups, index, counts, cols, vals, cot, weight, bias, dense, cot_out, weight_out, bias_out):
+def place_kernel(groups, counts, cols, vals, cot, weight, bias, dense, cot_out, weight_out, bias_out):
     nblk, slots, flat = vals.shape
     owners = dense.shape[0]
-    cot_out[...] = cot[...]
-    weight_out[...] = weight[...]
-    bias_out[...] = bias[...]
+    cot_out[...] = cot[...].astype(jnp.float32).T.astype(jnp.bfloat16)
+    weight_out[...] = weight[...].astype(jnp.float32).T.astype(jnp.bfloat16)
+    bias_out[...] = jnp.broadcast_to(bias[...], (128, bias.shape[1])).T
     wide = flat // 128
     deep = 16 * slots
     lane = lax.broadcasted_iota(jnp.int32, (slots, deep), 1)
@@ -46,7 +46,7 @@
     spread = (lane % slots == slot).astype(jnp.bfloat16)
     named = jnp.dot(cols[...].astype(jnp.bfloat16), spread, preferred_element_type=jnp.float32)
     named = named.astype(jnp.int32)
-    apart = (named >> 1) ^ (index[0] >> 1)
+    apart = (named >> 1) ^ lax.axis_index("rows")
     place = jnp.zeros_like(apart)
     stride = 1
     for shift, radix in groups:
@@ -89,22 +89,22 @@
             pl.loop(0, owners // 16)(put)
 
 
-def place_blocks(index, counts, cols, vals, cot, weight, bias, owners):
+def place_blocks(counts, cols, vals, cot, weight, bias, owners):
     nblk, slots, flat = vals.shape
     wide = flat // 128
     return pl.pallas_call(
         functools.partial(place_kernel, digit_groups(owners)),
         out_shape=(
             jax.ShapeDtypeStruct((owners, 2 * nblk * wide, 128), jnp.bfloat16),
-            jax.ShapeDtypeStruct(cot.shape, cot.dtype),
-            jax.ShapeDtypeStruct(weight.shape, weight.dtype),
-            jax.ShapeDtypeStruct(bias.shape, bias.dtype),
+            jax.ShapeDtypeStruct(cot.shape[::-1], cot.dtype),
+            jax.ShapeDtypeStruct(weight.shape[::-1], weight.dtype),
+            jax.ShapeDtypeStruct((bias.shape[1], 128), bias.dtype),
         ),
-        in_specs=[SMEM, SMEM] + [VMEM] * 5,
+        in_specs=[SMEM] + [VMEM] * 5,
         out_specs=(VMEM,) * 4,
         compiler_params=limit(owners),
         name="place",
-    )(index, counts, cols, vals, cot, weight, bias)
+    )(counts, cols, vals, cot, weight, bias)
 
 
 def sum_kernel(dense, *refs):
@@ -142,71 +142,72 @@
     )(dense, *pieces)
 
 
-def layer_kernel(index, mine, other, weight, bias, cot_mine, cot_other, act, parts, value):
-    half = cot_mine.shape[0]
-    side = index[0] & 1
+NT = (((1,), (1,)), ((), ()))
+
+
+def layer_kernel(mine, other, weight_t, bias_t, cot_mine, cot_other, parts):
+    first = lax.axis_index("rep") == 0
     owners, chunk, _ = parts.shape
-    share = 256 // owners
+    share = weight_t.shape[0] // owners
     aggregated = (mine[...] + other[...]).astype(jnp.bfloat16)
-    pre = jnp.dot(aggregated, weight[...], preferred_element_type=jnp.float32) + bias[...]
+    pre = lax.dot_general(weight_t[...], aggregated, NT, preferred_element_type=jnp.float32)
+    pre = pre + jnp.concatenate([bias_t[...]] * (pre.shape[1] // 128), axis=1)
     sig = 1.0 / (1.0 + jnp.exp(-pre))
-    value[...] = pre * sig
-    act[...] = value[pl.ds(pl.multiple_of(side * half, half), half), :].astype(jnp.bfloat16)
-    first = side == 0
-    cot_a = cot_mine[...].astype(jnp.float32)
-    cot_b = cot_other[...].astype(jnp.float32)
-    cot = jnp.concatenate([jnp.where(first, cot_a, cot_b), jnp.where(first, cot_b, cot_a)], axis=0)
+    cot_a, cot_b = cot_mine[...].astype(jnp.float32), cot_other[...].astype(jnp.float32)
+    cot = jnp.concatenate([jnp.where(first, cot_a, cot_b), jnp.where(first, cot_b, cot_a)], axis=1)
     delta = (cot * sig * (1.0 + pre * (1.0 - sig))).astype(jnp.bfloat16)
-    grad = lax.dot_general(delta, aggregated, (((0,), (0,)), ((), ())), preferred_element_type=jnp.float32)
-    total = jnp.sum(delta.astype(jnp.float32), axis=0, keepdims=True)
-    tail = jnp.concatenate(
-        [total[:, :128], total[:, 128:], jnp.zeros((chunk - share - 2, 128), jnp.float32)], axis=0
-    )
+    grad = jnp.dot(delta, aggregated, preferred_element_type=jnp.float32)
+    ones = jnp.ones((16, delta.shape[1]), jnp.bfloat16)
+    total = lax.dot_general(ones, delta, NT, preferred_element_type=jnp.float32)[:1]
+    blank = jnp.zeros((chunk - share - 2, 128), jnp.float32)
+    tail = jnp.concatenate([total[:, :128], total[:, 128:], blank], axis=0)
     for r in range(owners):
-        parts[r] = jnp.concatenate([grad[r * share : (r + 1) * share], tail], axis=0)
-
-
-def layer(index, mine, other, weight, bias, cot_mine, cot_other, owners):
-    nodes = mine.shape[0]
-    half, wide = cot_mine.shape
-    chunk = -(-(wide // owners + 2) // 8) * 8
+        parts[r] = jnp.concatenate([grad[r * share : (r + 1) * share], tail], axis=0).astype(parts.dtype)
+
+
+def layer(mine, other, weight_t, bias_t, cot_mine, cot_other, owners):
+    share = weight_t.shape[0] // owners
+    chunk = -(-(share + 2) // 8) * 8
     return pl.pallas_call(
         layer_kernel,
-        out_shape=(
-            jax.ShapeDtypeStruct((half, wide), jnp.bfloat16),
-            jax.ShapeDtypeStruct((owners, chunk, 128), jnp.float32),
-        ),
-        in_specs=[SMEM] + [VMEM] * 6,
-        out_specs=(VMEM, VMEM),
-        scratch_shapes=[pltpu.VMEM((nodes, wide), jnp.float32)],
+        out_shape=jax.ShapeDtypeStruct((owners, chunk, 128), jnp.float32),
+        in_specs=[VMEM] * 6,
+        out_specs=VMEM,
         compiler_params=limit(owners),
         name="layer",
-    )(index, mine, other, weight, bias, cot_mine, cot_other)
-
-
-def finish_kernel(index, got, weight_grad, bias_grad):
+    )(mine, other, weight_t, bias_t, cot_mine, cot_other)
+
+
+def finish_kernel(mine, other, weight, bias, got, act, weight_grad, bias_grad):
+    half = act.shape[0]
+    own = pl.ds(pl.multiple_of(lax.axis_index("rep") * half, half), half)
+    aggregated = (mine[own, :] + other[own, :]).astype(jnp.bfloat16)
+    pre = jnp.dot(aggregated, weight[...], preferred_element_type=jnp.float32) + bias[...]
+    act[...] = (pre / (1.0 + jnp.exp(-pre))).astype(act.dtype)
     share = weight_grad.shape[0]
     total = jnp.sum(got[...], axis=0)
     weight_grad[...] = total[:share]
     flat = jnp.concatenate([total[share : share + 1], total[share + 1 : share + 2]], axis=1)
     flat = jnp.broadcast_to(flat, (8, 256))
-    flat = pltpu.roll(flat, lax.rem(256 - (index[0] >> 1) * share, 256), 1)
+    flat = pltpu.roll(flat, lax.rem(256 - lax.axis_index("rows") * share, 256), 1)
     bias_grad[...] = flat[:1, :share]
 
 
-def finish(index, got):
-    share = 256 // got.shape[0]
+def finish(mine, other, weight, bias, got):
+    owners = got.shape[0]
+    share = weight.shape[1] // owners
     return pl.pallas_call(
         finish_kernel,
         out_shape=(
+            jax.ShapeDtypeStruct((mine.shape[0] // 2, weight.shape[1]), jnp.bfloat16),
             jax.ShapeDtypeStruct((share, 128), jnp.float32),
             jax.ShapeDtypeStruct((1, share), jnp.float32),
         ),
-        in_specs=[SMEM, VMEM],
-        out_specs=(VMEM, VMEM),
-        compiler_params=limit(got.shape[0]),
+        in_specs=[VMEM] * 5,
+        out_specs=(VMEM,) * 3,
+        compiler_params=limit(owners),
         name="finish",
-    )(index, got)
+    )(mine, other, weight, bias, got)
 
 
 def body(features, weight, bias, block_count, block_cols, block_vals, cotangent):
@@ -224,18 +225,18 @@
         held, vals = lax.optimization_barrier((jnp.concatenate(pieces), vals))
         pieces = [held] + [across(held, s << shift, owners, 0) for s in range(1, radix)]
 
-    index = lax.axis_index(BOTH).reshape(1).astype(jnp.int32)
-    dense, cot_mine, weight, bias = place_blocks(
-        index, block_count, block_cols[0], vals, cotangent, weight, bias.reshape(1, -1), owners
+    bias = bias.reshape(1, -1)
+    dense, cot_mine, weight_t, bias_t = place_blocks(
+        block_count, block_cols[0], vals, cotangent, weight, bias, owners
     )
     cot_other = across(cot_mine, 0, owners, 1)
     dense, cot_other = lax.optimization_barrier((dense, cot_other))
 
     mine = sum_blocks(dense, pieces)
     other = across(mine, 0, owners, 1)
-    activated, parts = layer(index, mine, other, weight, bias, cot_mine, cot_other, owners)
+    parts = layer(mine, other, weight_t, bias_t, cot_mine, cot_other, owners)
     got = lax.all_to_all(parts, "rows", split_axis=0, concat_axis=0, tiled=True)
-    weight_grad, bias_grad = finish(index, got)
+    activated, weight_grad, bias_grad = finish(mine, other, weight, bias, got)
     return activated, weight_grad.T, bias_grad.reshape(-1)
 
 

time: 37.1 us -> 36.8 us (level)
  no operation moved by 1% of the time
where the time goes in v4:
time: 36.8 us; the launch traced here: 36.5 us
  blocking collectives  13.3 us (36%)
  starting transfers between devices  9.11 us (25%)
  waiting for transfers between devices  7.86 us (21%)
  Pallas kernels  3.01 us (8%)
  local copies, waits for them, and re-layouts  2.5 us (7%)
  between operations  0.71 us (2%)
    all_to_all x1, blocking collectives, body(): got = lax.all_to_all(parts, 'rows', split_axis=0, concat_axis=0, tiled=True)  13.3 us
    ppermute x8, starting transfers between devices, across(): return lax.ppermute(value, BOTH, pairs)  9.11 us
    ppermute x8, waiting for transfers between devices, across(): return lax.ppermute(value, BOTH, pairs)  7.86 us
    unnamed x12, local copies, waits for them, and re-layouts  1.72 us
    pallas_call x1, Pallas kernels, place_blocks(): pl.pallas_call(functools.partial(place_kernel, digit_groups(owners)), out...  1.37 us
    pallas_call x1, Pallas kernels, finish(): pl.pallas_call(finish_kernel, out_shape=(jax.ShapeDtypeStruct((mine.shape...  0.83 us
    dynamic_slice x1, local copies, waits for them, and re-layouts, body(): keep = lax.dynamic_slice_in_dim(features, side * half_rows, half_rows, 0)  0.79 us
  transfers between devices with their start and end apart: 8, of which 6 were waited for; matrix products, arithmetic and copies ran while one was open for 0% of the time, Pallas kernels for 4%

profile of v4, /device:TPU:0, one launch (start us, length us, event | category | flops | bytes accessed | tf_op | source)
XLA Modules:
  0.0 36.5 jit_solution(8119284241886180946)
XLA Ops:
  0.6 0.8 %constant_dynamic-slice_fusion.1 = (bf16[128,128]{1,0:T(8,128)(2,1)S(1)}, bf16[128,128]{1,0:T(8,128)(2,1)S(1)}) fusion(bf16[256,128]{1,0:T(8,128)(2,1)} %param.7, s32[]{:T(128)S(6)} %select_n.6, s32[]{:T(128)S(6)} %select_n.7), kind=kLoop, calls=%fused_computation.2 | loop fusion | bytes 131080 | tf_op jit(solution)/shard_map/dynamic_slice | solution.py:219
  1.4 4.5 %collective-permute-start.2 = (bf16[128,128]{1,0:T(8,128)(2,1)S(1)}, bf16[128,128]{1,0:T(8,128)(2,1)S(1)}, u32[]{:S(2)}, u32[]{:S(2)}) collective-permute-start(bf16[128,128]{1,0:T(8,128)(2,1)S(1)} %get-tuple-element.26), channel_id=1, source_target_pairs={{0,25},{1,24},{2,27},{3,26},{4,29},{5,28},{6,31},{7,30},{8,17},{9,... | collective-permute-start | bytes 98312 | tf_op jit(solution)/shard_map/ppermute | solution.py:29
  5.9 0.0 collective-permute-start.1
  5.9 0.9 %collective-permute-start = (bf16[128,128]{1,0:T(8,128)(2,1)S(1)}, bf16[128,128]{1,0:T(8,128)(2,1)S(1)}, u32[]{:S(2)}, u32[]{:S(2)}) collective-permute-start(bf16[128,128]{1,0:T(8,128)(2,1)S(1)} %get-tuple-element.26), channel_id=1, source_target_pairs={{0,9},{1,8},{2,11},{3,10},{4,13},{5,12},{6,15},{7,14},{8,1},{9,0},... | collective-permute-start | bytes 98312 | tf_op jit(solution)/shard_map/ppermute | solution.py:29
  6.8 0.9 %collective-permute-done.2 = bf16[128,128]{1,0:T(8,128)(2,1)S(1)} collective-permute-done((bf16[128,128]{1,0:T(8,128)(2,1)S(1)}, bf16[128,128]{1,0:T(8,128)(2,1)S(1)}, u32[]{:S(2)}, u32[]{:S(2)}) %collective-permute-start.2) | collective-permute-done | bytes 32800 | tf_op jit(solution)/shard_map/ppermute | solution.py:29
  7.7 2.8 %collective-permute-done.1 = bf16[128,128]{1,0:T(8,128)(2,1)S(1)} collective-permute-done((bf16[128,128]{1,0:T(8,128)(2,1)S(1)}, bf16[128,128]{1,0:T(8,128)(2,1)S(1)}, u32[]{:S(2)}, u32[]{:S(2)}) %collective-permute-start.1) | collective-permute-done | bytes 32800 | tf_op jit(solution)/shard_map/ppermute | solution.py:29
  10.4 0.0 collective-permute-done
  10.5 0.0 copy-start.1
  10.5 0.0 copy-start.2
  10.5 0.0 copy-start.4
  10.5 2.5 %collective-permute-start.6 = (bf16[512,128]{1,0:T(8,128)(2,1)S(1)}, bf16[512,128]{1,0:T(8,128)(2,1)S(1)}, u32[]{:S(2)}, u32[]{:S(2)}) collective-permute-start(bf16[512,128]{1,0:T(8,128)(2,1)S(1)} %pad_maximum_fusion.refs_0_), channel_id=1, source_target_pairs={{0,6},{1,7},{2,4},{3,5},{4,2},{5,3},{6,0},{7,1},{8,14},{9,15},{10,... | collective-permute-start | bytes 393224 | tf_op jit(solution)/shard_map/ppermute | solution.py:29
  13.0 0.5 %collective-permute-start.5 = (bf16[512,128]{1,0:T(8,128)(2,1)S(1)}, bf16[512,128]{1,0:T(8,128)(2,1)S(1)}, u32[]{:S(2)}, u32[]{:S(2)}) collective-permute-start(bf16[512,128]{1,0:T(8,128)(2,1)S(1)} %pad_maximum_fusion.refs_0_), channel_id=1, source_target_pairs={{0,4},{1,5},{2,6},{3,7},{4,0},{5,1},{6,2},{7,3},{8,12},{9,13},{10,... | collective-permute-start | bytes 393224 | tf_op jit(solution)/shard_map/ppermute | solution.py:29
  13.5 0.5 %collective-permute-start.4 = (bf16[512,128]{1,0:T(8,128)(2,1)S(1)}, bf16[512,128]{1,0:T(8,128)(2,1)S(1)}, u32[]{:S(2)}, u32[]{:S(2)}) collective-permute-start(bf16[512,128]{1,0:T(8,128)(2,1)S(1)} %pad_maximum_fusion.refs_0_), channel_id=1, source_target_pairs={{0,2},{1,3},{2,0},{3,1},{4,6},{5,7},{6,4},{7,5},{8,10},{9,11},{10,... | collective-permute-start | bytes 393224 | tf_op jit(solution)/shard_map/ppermute | solution.py:29
  14.1 0.0 copy-start.3
  14.1 0.0 copy-start.5
  14.1 0.0 copy-done.1
  14.1 0.0 copy-done.2
  14.1 0.0 copy-done.4
  14.1 0.7 %copy-done.3 = f32[256]{0:T(256)S(1)} copy-done((f32[256]{0:T(256)S(1)}, f32[256]{0:T(256)}, u32[]{:S(2)}) %copy-start.3) | copy-done | bytes 1048
  14.7 0.0 copy-done.5
  14.7 0.0 copy-start
  14.7 1.0 %copy-done = bf16[1,4,16,4096]{3,2,1,0:T(8,128)(2,1)S(1)} copy-done((bf16[1,4,16,4096]{3,2,1,0:T(8,128)(2,1)S(1)}, bf16[1,4,16,4096]{3,2,1,0:T(8,128)(2,1)}, u32[]{:S(2)}) %copy-start) | copy-done | bytes 524312
  15.8 1.4 %place.1 = (bf16[16,256,128]{2,1,0:T(8,128)(2,1)S(1)}, bf16[256,128]{1,0:T(8,128)(2,1)S(1)}, bf16[256,128]{1,0:T(8,128)(2,1)S(1)}, f32[256,128]{1,0:T(8,128)S(1)}) custom-call(s32[1,4]{1,0:T(1,128)S(1)} %copy-done.5, s32[4,16]{1,0:T(4,128)S(1)} %bitcast.8, bf16[4,16,4096]{2,1,0:T(8,128)(2,1)S(1)} %bitcast.5, bf16[128,256]{1,0:T(8,128)(2,1)S(1)} %copy-done.2, ...), custom_call_target="tpu_custom_call" | custom-call | tf_op jit(solution)/shard_map/place/pallas_call | solution.py:95
  17.2 0.1 collective-permute-start.3
  17.2 1.2 %collective-permute-done.3.cot_other = bf16[256,128]{1,0:T(8,128)(2,1)S(1)} collective-permute-done((bf16[256,128]{1,0:T(8,128)(2,1)S(1)}, bf16[256,128]{1,0:T(8,128)(2,1)S(1)}, u32[]{:S(2)}, u32[]{:S(2)}) %collective-permute-start.3) | collective-permute-done | bytes 65568 | tf_op jit(solution)/shard_map/ppermute | solution.py:29
  18.5 0.0 collective-permute-done.6.refs_3_
  18.5 1.6 %collective-permute-done.5.refs_2_ = bf16[512,128]{1,0:T(8,128)(2,1)S(1)} collective-permute-done((bf16[512,128]{1,0:T(8,128)(2,1)S(1)}, bf16[512,128]{1,0:T(8,128)(2,1)S(1)}, u32[]{:S(2)}, u32[]{:S(2)}) %collective-permute-start.5) | collective-permute-done | bytes 131104 | tf_op jit(solution)/shard_map/ppermute | solution.py:29
  20.0 0.1 collective-permute-done.4.refs_1_
  20.1 0.4 %block_sum.1.mine = f32[256,128]{1,0:T(8,128)S(1)} custom-call(bf16[16,256,128]{2,1,0:T(8,128)(2,1)S(1)} %get-tuple-element.17.dense, bf16[512,128]{1,0:T(8,128)(2,1)S(1)} %pad_maximum_fusion.refs_0_, bf16[512,128]{1,0:T(8,128)(2,1)S(1)} %collective-permute-done.4.refs_1_, bf16[512,128]{1,0:T(8,128)(2,1)S(1)} %collective-permute-done.5.refs_2_, ...), custom_call_target="tpu_custom_call" | custom-call | tf_op jit(solution)/shard_map/block_sum/pallas_call | solution.py:135
  20.6 0.1 collective-permute-start.7
  20.6 1.3 %collective-permute-done.7.other = f32[256,128]{1,0:T(8,128)S(1)} collective-permute-done((f32[256,128]{1,0:T(8,128)S(1)}, f32[256,128]{1,0:T(8,128)S(1)}, u32[]{:S(2)}, u32[]{:S(2)}) %collective-permute-start.7) | collective-permute-done | bytes 131104 | tf_op jit(solution)/shard_map/ppermute | solution.py:29
  22.0 0.4 %layer.1 = f32[16,24,128]{2,1,0:T(8,128)S(1)} custom-call(f32[256,128]{1,0:T(8,128)S(1)} %block_sum.1.mine, f32[256,128]{1,0:T(8,128)S(1)} %collective-permute-done.7.other, bf16[256,128]{1,0:T(8,128)(2,1)S(1)} %get-tuple-element.19.weight_t, f32[256,128]{1,0:T(8,128)S(1)} %get-tuple-element.20.bias_t, bf16[256,128]{1,0:T(8,128)(2,1)S(1)} %get-tuple-element.16.cot_mine, ...), custom_call_target="tpu_custom_call" | custom-call | tf_op jit(solution)/shard_map/layer/pallas_call | solution.py:171
  22.4 13.3 %all_to_all.5.got = f32[16,24,128]{2,1,0:T(8,128)S(1)} all-to-all(f32[16,24,128]{2,1,0:T(8,128)S(1)} %layer.1), channel_id=1, replica_groups=mesh['rows'=16,'rep'=2] {'rows'}, dimensions={0} | all-to-all | bytes 393216 | tf_op jit(solution)/shard_map/all_to_all | solution.py:238
  35.7 0.8 %finish.1 = (bf16[128,256]{1,0:T(8,128)(2,1)}, f32[16,128]{1,0:T(8,128)}, f32[1,16]{1,0:T(1,128)}) custom-call(f32[256,128]{1,0:T(8,128)S(1)} %block_sum.1.mine, f32[256,128]{1,0:T(8,128)S(1)} %collective-permute-done.7.other, bf16[128,256]{1,0:T(8,128)(2,1)S(1)} %copy-done.1, f32[1,256]{1,0:T(1,128)S(1)} %bitcast.7, f32[16,24,128]{2,1,0:T(8,128)S(1)} %all_to_all.5.got), custom_call_target="tpu_custom_call" | custom-call | tf_op jit(solution)/shard_map/finish/pallas_call | solution.py:199
  (1 shorter events, 0.0 us)
Async XLA Ops:
  1.4 6.3 %collective-permute-start.2 = (bf16[128,128]{1,0:T(8,128)(2,1)S(1)}, bf16[128,128]{1,0:T(8,128)(2,1)S(1)}, u32[]{:S(2)}, u32[]{:S(2)}) collective-permute-start(bf16[128,128]{1,0:T(8,128)(2,1)S(1)} %get-tuple-element.26), channel_id=1, source_target_pairs={{0,25},{1,24},{2,27},{3,26},{4,29},{5,28},{6,31},{7,30},{8,17},{9,... | collective-permute-start | bytes 98312 | tf_op jit(solution)/shard_map/ppermute | solution.py:29
  5.9 4.5 %collective-permute-start.1 = (bf16[128,128]{1,0:T(8,128)(2,1)S(1)}, bf16[128,128]{1,0:T(8,128)(2,1)S(1)}, u32[]{:S(2)}, u32[]{:S(2)}) collective-permute-start(bf16[128,128]{1,0:T(8,128)(2,1)S(1)} %get-tuple-element.26), channel_id=1, source_target_pairs={{0,17},{1,16},{2,19},{3,18},{4,21},{5,20},{6,23},{7,22},{8,25},{9,... | collective-permute-start | bytes 98312 | tf_op jit(solution)/shard_map/ppermute | solution.py:29
  5.9 4.5 %collective-permute-start = (bf16[128,128]{1,0:T(8,128)(2,1)S(1)}, bf16[128,128]{1,0:T(8,128)(2,1)S(1)}, u32[]{:S(2)}, u32[]{:S(2)}) collective-permute-start(bf16[128,128]{1,0:T(8,128)(2,1)S(1)} %get-tuple-element.26), channel_id=1, source_target_pairs={{0,9},{1,8},{2,11},{3,10},{4,13},{5,12},{6,15},{7,14},{8,1},{9,0},... | collective-permute-start | bytes 98312 | tf_op jit(solution)/shard_map/ppermute | solution.py:29
  10.5 3.6 %copy-start.1 = (bf16[128,256]{1,0:T(8,128)(2,1)S(1)}, bf16[128,256]{1,0:T(8,128)(2,1)}, u32[]{:S(2)}) copy-start(bf16[128,256]{1,0:T(8,128)(2,1)} %weight.3) | copy-start | bytes 196612
  10.5 3.6 %copy-start.2 = (bf16[128,256]{1,0:T(8,128)(2,1)S(1)}, bf16[128,256]{1,0:T(8,128)(2,1)}, u32[]{:S(2)}) copy-start(bf16[128,256]{1,0:T(8,128)(2,1)} %cot.1) | copy-start | bytes 196612
  10.5 3.6 %copy-start.4 = (s32[1,4,16]{2,1,0:T(4,128)S(1)}, s32[1,4,16]{2,1,0:T(4,128)}, u32[]{:S(2)}) copy-start(s32[1,4,16]{2,1,0:T(4,128)} %param.11) | copy-start | bytes 772
  10.5 8.0 %collective-permute-start.6 = (bf16[512,128]{1,0:T(8,128)(2,1)S(1)}, bf16[512,128]{1,0:T(8,128)(2,1)S(1)}, u32[]{:S(2)}, u32[]{:S(2)}) collective-permute-start(bf16[512,128]{1,0:T(8,128)(2,1)S(1)} %pad_maximum_fusion.refs_0_), channel_id=1, source_target_pairs={{0,6},{1,7},{2,4},{3,5},{4,2},{5,3},{6,0},{7,1},{8,14},{9,15},{10,... | collective-permute-start | bytes 393224 | tf_op jit(solution)/shard_map/ppermute | solution.py:29
  13.0 7.0 %collective-permute-start.5 = (bf16[512,128]{1,0:T(8,128)(2,1)S(1)}, bf16[512,128]{1,0:T(8,128)(2,1)S(1)}, u32[]{:S(2)}, u32[]{:S(2)}) collective-permute-start(bf16[512,128]{1,0:T(8,128)(2,1)S(1)} %pad_maximum_fusion.refs_0_), channel_id=1, source_target_pairs={{0,4},{1,5},{2,6},{3,7},{4,0},{5,1},{6,2},{7,3},{8,12},{9,13},{10,... | collective-permute-start | bytes 393224 | tf_op jit(solution)/shard_map/ppermute | solution.py:29
  13.5 6.6 %collective-permute-start.4 = (bf16[512,128]{1,0:T(8,128)(2,1)S(1)}, bf16[512,128]{1,0:T(8,128)(2,1)S(1)}, u32[]{:S(2)}, u32[]{:S(2)}) collective-permute-start(bf16[512,128]{1,0:T(8,128)(2,1)S(1)} %pad_maximum_fusion.refs_0_), channel_id=1, source_target_pairs={{0,2},{1,3},{2,0},{3,1},{4,6},{5,7},{6,4},{7,5},{8,10},{9,11},{10,... | collective-permute-start | bytes 393224 | tf_op jit(solution)/shard_map/ppermute | solution.py:29
  14.1 0.7 %copy-start.3 = (f32[256]{0:T(256)S(1)}, f32[256]{0:T(256)}, u32[]{:S(2)}) copy-start(f32[256]{0:T(256)} %param.9) | copy-start | bytes 3076
  14.1 0.7 %copy-start.5 = (s32[1,4]{1,0:T(1,128)S(1)}, s32[1,4]{1,0:T(1,128)}, u32[]{:S(2)}) copy-start(s32[1,4]{1,0:T(1,128)} %counts.1) | copy-start | bytes 52
  14.7 1.0 %copy-start = (bf16[1,4,16,4096]{3,2,1,0:T(8,128)(2,1)S(1)}, bf16[1,4,16,4096]{3,2,1,0:T(8,128)(2,1)}, u32[]{:S(2)}) copy-start(bf16[1,4,16,4096]{3,2,1,0:T(8,128)(2,1)} %param.12) | copy-start | bytes 1572868
  17.2 1.3 %collective-permute-start.3 = (bf16[256,128]{1,0:T(8,128)(2,1)S(1)}, bf16[256,128]{1,0:T(8,128)(2,1)S(1)}, u32[]{:S(2)}, u32[]{:S(2)}) collective-permute-start(bf16[256,128]{1,0:T(8,128)(2,1)S(1)} %get-tuple-element.16.cot_mine), channel_id=1, source_target_pairs={{0,1},{1,0},{2,3},{3,2},{4,5},{5,4},{6,7},{7,6},{8,9},{9,8},{10,11... | collective-permute-start | bytes 196616 | tf_op jit(solution)/shard_map/ppermute | solution.py:29
  20.6 1.4 %collective-permute-start.7 = (f32[256,128]{1,0:T(8,128)S(1)}, f32[256,128]{1,0:T(8,128)S(1)}, u32[]{:S(2)}, u32[]{:S(2)}) collective-permute-start(f32[256,128]{1,0:T(8,128)S(1)} %block_sum.1.mine), channel_id=1, source_target_pairs={{0,1},{1,0},{2,3},{3,2},{4,5},{5,4},{6,7},{7,6},{8,9},{9,8},{10,11... | collective-permute-start | bytes 393224 | tf_op jit(solution)/shard_map/ppermute | solution.py:29

commit v5 on v4

--- a/solution.py
+++ b/solution.py
@@ -167,10 +167,10 @@
 
 def layer(mine, other, weight_t, bias_t, cot_mine, cot_other, owners):
     share = weight_t.shape[0] // owners
-    chunk = -(-(share + 2) // 8) * 8
+    chunk = -(-(share + 2) // 16) * 16
     return pl.pallas_call(
         layer_kernel,
-        out_shape=jax.ShapeDtypeStruct((owners, chunk, 128), jnp.float32),
+        out_shape=jax.ShapeDtypeStruct((owners, chunk, 128), jnp.bfloat16),
         in_specs=[VMEM] * 6,
         out_specs=VMEM,
         compiler_params=limit(owners),
@@ -185,7 +185,7 @@
     pre = jnp.dot(aggregated, weight[...], preferred_element_type=jnp.float32) + bias[...]
     act[...] = (pre / (1.0 + jnp.exp(-pre))).astype(act.dtype)
     share = weight_grad.shape[0]
-    total = jnp.sum(got[...], axis=0)
+    total = jnp.sum(got[...].astype(jnp.float32), axis=0)
     weight_grad[...] = total[:share]
     flat = jnp.concatenate([total[share : share + 1], total[share + 1 : share + 2]], axis=1)
     flat = jnp.broadcast_to(flat, (8, 256))

time: 36.8 us -> 35.6 us (0.967)
  blocking collectives: 13.3 us -> 12.1 us
    all_to_all x1, blocking collectives: 13.3 us -> 12.1 us  [body(): got = lax.all_to_all(parts, 'rows', split_axis=0, concat_axis=0, tiled=True)]
where the time goes in v5:
time: 35.6 us; the launch traced here: 35.3 us
  blocking collectives  12.1 us (34%)
  starting transfers between devices  9.11 us (26%)
  waiting for transfers between devices  7.86 us (22%)
  Pallas kernels  3.01 us (8%)
  local copies, waits for them, and re-layouts  2.5 us (7%)
  between operations  0.71 us (2%)
    all_to_all x1, blocking collectives, body(): got = lax.all_to_all(parts, 'rows', split_axis=0, concat_axis=0, tiled=True)  12.1 us
    ppermute x8, starting transfers between devices, across(): return lax.ppermute(value, BOTH, pairs)  9.11 us
    ppermute x8, waiting for transfers between devices, across(): return lax.ppermute(value, BOTH, pairs)  7.86 us
    unnamed x12, local copies, waits for them, and re-layouts  1.72 us
    pallas_call x1, Pallas kernels, place_blocks(): pl.pallas_call(functools.partial(place_kernel, digit_groups(owners)), out...  1.37 us
    pallas_call x1, Pallas kernels, finish(): pl.pallas_call(finish_kernel, out_shape=(jax.ShapeDtypeStruct((mine.shape...  0.82 us
    dynamic_slice x1, local copies, waits for them, and re-layouts, body(): keep = lax.dynamic_slice_in_dim(features, side * half_rows, half_rows, 0)  0.79 us
  transfers between devices with their start and end apart: 8, of which 6 were waited for; matrix products, arithmetic and copies ran while one was open for 0% of the time, Pallas kernels for 4%

profile of v5, /device:TPU:0, one launch (start us, length us, event | category | flops | bytes accessed | tf_op | source)
XLA Modules:
  0.0 35.3 jit_solution(7212344008369907800)
XLA Ops:
  0.6 0.8 %constant_dynamic-slice_fusion.1 = (bf16[128,128]{1,0:T(8,128)(2,1)S(1)}, bf16[128,128]{1,0:T(8,128)(2,1)S(1)}) fusion(bf16[256,128]{1,0:T(8,128)(2,1)} %param.7, s32[]{:T(128)S(6)} %select_n.6, s32[]{:T(128)S(6)} %select_n.7), kind=kLoop, calls=%fused_computation.2 | loop fusion | bytes 131080 | tf_op jit(solution)/shard_map/dynamic_slice | solution.py:219
  1.4 4.5 %collective-permute-start.2 = (bf16[128,128]{1,0:T(8,128)(2,1)S(1)}, bf16[128,128]{1,0:T(8,128)(2,1)S(1)}, u32[]{:S(2)}, u32[]{:S(2)}) collective-permute-start(bf16[128,128]{1,0:T(8,128)(2,1)S(1)} %get-tuple-element.26), channel_id=1, source_target_pairs={{0,25},{1,24},{2,27},{3,26},{4,29},{5,28},{6,31},{7,30},{8,17},{9,... | collective-permute-start | bytes 98312 | tf_op jit(solution)/shard_map/ppermute | solution.py:29
  5.9 0.0 collective-permute-start.1
  5.9 0.9 %collective-permute-start = (bf16[128,128]{1,0:T(8,128)(2,1)S(1)}, bf16[128,128]{1,0:T(8,128)(2,1)S(1)}, u32[]{:S(2)}, u32[]{:S(2)}) collective-permute-start(bf16[128,128]{1,0:T(8,128)(2,1)S(1)} %get-tuple-element.26), channel_id=1, source_target_pairs={{0,9},{1,8},{2,11},{3,10},{4,13},{5,12},{6,15},{7,14},{8,1},{9,0},... | collective-permute-start | bytes 98312 | tf_op jit(solution)/shard_map/ppermute | solution.py:29
  6.8 0.9 %collective-permute-done.2 = bf16[128,128]{1,0:T(8,128)(2,1)S(1)} collective-permute-done((bf16[128,128]{1,0:T(8,128)(2,1)S(1)}, bf16[128,128]{1,0:T(8,128)(2,1)S(1)}, u32[]{:S(2)}, u32[]{:S(2)}) %collective-permute-start.2) | collective-permute-done | bytes 32800 | tf_op jit(solution)/shard_map/ppermute | solution.py:29
  7.7 2.8 %collective-permute-done.1 = bf16[128,128]{1,0:T(8,128)(2,1)S(1)} collective-permute-done((bf16[128,128]{1,0:T(8,128)(2,1)S(1)}, bf16[128,128]{1,0:T(8,128)(2,1)S(1)}, u32[]{:S(2)}, u32[]{:S(2)}) %collective-permute-start.1) | collective-permute-done | bytes 32800 | tf_op jit(solution)/shard_map/ppermute | solution.py:29
  10.4 0.0 collective-permute-done
  10.5 0.0 copy-start.1
  10.5 0.0 copy-start.2
  10.5 0.0 copy-start.4
  10.5 2.5 %collective-permute-start.6 = (bf16[512,128]{1,0:T(8,128)(2,1)S(1)}, bf16[512,128]{1,0:T(8,128)(2,1)S(1)}, u32[]{:S(2)}, u32[]{:S(2)}) collective-permute-start(bf16[512,128]{1,0:T(8,128)(2,1)S(1)} %pad_maximum_fusion.refs_0_), channel_id=1, source_target_pairs={{0,6},{1,7},{2,4},{3,5},{4,2},{5,3},{6,0},{7,1},{8,14},{9,15},{10,... | collective-permute-start | bytes 393224 | tf_op jit(solution)/shard_map/ppermute | solution.py:29
  13.0 0.5 %collective-permute-start.5 = (bf16[512,128]{1,0:T(8,128)(2,1)S(1)}, bf16[512,128]{1,0:T(8,128)(2,1)S(1)}, u32[]{:S(2)}, u32[]{:S(2)}) collective-permute-start(bf16[512,128]{1,0:T(8,128)(2,1)S(1)} %pad_maximum_fusion.refs_0_), channel_id=1, source_target_pairs={{0,4},{1,5},{2,6},{3,7},{4,0},{5,1},{6,2},{7,3},{8,12},{9,13},{10,... | collective-permute-start | bytes 393224 | tf_op jit(solution)/shard_map/ppermute | solution.py:29
  13.5 0.5 %collective-permute-start.4 = (bf16[512,128]{1,0:T(8,128)(2,1)S(1)}, bf16[512,128]{1,0:T(8,128)(2,1)S(1)}, u32[]{:S(2)}, u32[]{:S(2)}) collective-permute-start(bf16[512,128]{1,0:T(8,128)(2,1)S(1)} %pad_maximum_fusion.refs_0_), channel_id=1, source_target_pairs={{0,2},{1,3},{2,0},{3,1},{4,6},{5,7},{6,4},{7,5},{8,10},{9,11},{10,... | collective-permute-start | bytes 393224 | tf_op jit(solution)/shard_map/ppermute | solution.py:29
  14.1 0.0 copy-start.3
  14.1 0.0 copy-start.5
  14.1 0.0 copy-done.1
  14.1 0.0 copy-done.2
  14.1 0.0 copy-done.4
  14.1 0.7 %copy-done.3 = f32[256]{0:T(256)S(1)} copy-done((f32[256]{0:T(256)S(1)}, f32[256]{0:T(256)}, u32[]{:S(2)}) %copy-start.3) | copy-done | bytes 1048
  14.7 0.0 copy-done.5
  14.7 0.0 copy-start
  14.7 1.0 %copy-done = bf16[1,4,16,4096]{3,2,1,0:T(8,128)(2,1)S(1)} copy-done((bf16[1,4,16,4096]{3,2,1,0:T(8,128)(2,1)S(1)}, bf16[1,4,16,4096]{3,2,1,0:T(8,128)(2,1)}, u32[]{:S(2)}) %copy-start) | copy-done | bytes 524312
  15.8 1.4 %place.1 = (bf16[16,256,128]{2,1,0:T(8,128)(2,1)S(1)}, bf16[256,128]{1,0:T(8,128)(2,1)S(1)}, bf16[256,128]{1,0:T(8,128)(2,1)S(1)}, f32[256,128]{1,0:T(8,128)S(1)}) custom-call(s32[1,4]{1,0:T(1,128)S(1)} %copy-done.5, s32[4,16]{1,0:T(4,128)S(1)} %bitcast.8, bf16[4,16,4096]{2,1,0:T(8,128)(2,1)S(1)} %bitcast.5, bf16[128,256]{1,0:T(8,128)(2,1)S(1)} %copy-done.2, ...), custom_call_target="tpu_custom_call" | custom-call | tf_op jit(solution)/shard_map/place/pallas_call | solution.py:95
  17.2 0.1 collective-permute-start.3
  17.2 1.2 %collective-permute-done.3.cot_other = bf16[256,128]{1,0:T(8,128)(2,1)S(1)} collective-permute-done((bf16[256,128]{1,0:T(8,128)(2,1)S(1)}, bf16[256,128]{1,0:T(8,128)(2,1)S(1)}, u32[]{:S(2)}, u32[]{:S(2)}) %collective-permute-start.3) | collective-permute-done | bytes 65568 | tf_op jit(solution)/shard_map/ppermute | solution.py:29
  18.5 0.0 collective-permute-done.6.refs_3_
  18.5 1.6 %collective-permute-done.5.refs_2_ = bf16[512,128]{1,0:T(8,128)(2,1)S(1)} collective-permute-done((bf16[512,128]{1,0:T(8,128)(2,1)S(1)}, bf16[512,128]{1,0:T(8,128)(2,1)S(1)}, u32[]{:S(2)}, u32[]{:S(2)}) %collective-permute-start.5) | collective-permute-done | bytes 131104 | tf_op jit(solution)/shard_map/ppermute | solution.py:29
  20.0 0.1 collective-permute-done.4.refs_1_
  20.1 0.4 %block_sum.1.mine = f32[256,128]{1,0:T(8,128)S(1)} custom-call(bf16[16,256,128]{2,1,0:T(8,128)(2,1)S(1)} %get-tuple-element.17.dense, bf16[512,128]{1,0:T(8,128)(2,1)S(1)} %pad_maximum_fusion.refs_0_, bf16[512,128]{1,0:T(8,128)(2,1)S(1)} %collective-permute-done.4.refs_1_, bf16[512,128]{1,0:T(8,128)(2,1)S(1)} %collective-permute-done.5.refs_2_, ...), custom_call_target="tpu_custom_call" | custom-call | tf_op jit(solution)/shard_map/block_sum/pallas_call | solution.py:135
  20.6 0.1 collective-permute-start.7
  20.6 1.3 %collective-permute-done.7.other = f32[256,128]{1,0:T(8,128)S(1)} collective-permute-done((f32[256,128]{1,0:T(8,128)S(1)}, f32[256,128]{1,0:T(8,128)S(1)}, u32[]{:S(2)}, u32[]{:S(2)}) %collective-permute-start.7) | collective-permute-done | bytes 131104 | tf_op jit(solution)/shard_map/ppermute | solution.py:29
  22.0 0.4 %layer.1 = bf16[16,32,128]{2,1,0:T(8,128)(2,1)S(1)} custom-call(f32[256,128]{1,0:T(8,128)S(1)} %block_sum.1.mine, f32[256,128]{1,0:T(8,128)S(1)} %collective-permute-done.7.other, bf16[256,128]{1,0:T(8,128)(2,1)S(1)} %get-tuple-element.19.weight_t, f32[256,128]{1,0:T(8,128)S(1)} %get-tuple-element.20.bias_t, ...), custom_call_target="tpu_custom_call" | custom-call | tf_op jit(solution)/shard_map/layer/pallas_call | solution.py:171
  22.4 12.1 %all_to_all.5.got = bf16[16,32,128]{2,1,0:T(8,128)(2,1)S(1)} all-to-all(bf16[16,32,128]{2,1,0:T(8,128)(2,1)S(1)} %layer.1), channel_id=1, replica_groups=mesh['rows'=16,'rep'=2] {'rows'}, dimensions={0} | all-to-all | bytes 262144 | tf_op jit(solution)/shard_map/all_to_all | solution.py:238
  34.5 0.8 %finish.1 = (bf16[128,256]{1,0:T(8,128)(2,1)}, f32[16,128]{1,0:T(8,128)}, f32[1,16]{1,0:T(1,128)}) custom-call(f32[256,128]{1,0:T(8,128)S(1)} %block_sum.1.mine, f32[256,128]{1,0:T(8,128)S(1)} %collective-permute-done.7.other, bf16[128,256]{1,0:T(8,128)(2,1)S(1)} %copy-done.1, f32[1,256]{1,0:T(1,128)S(1)} %bitcast.7, bf16[16,32,128]{2,1,0:T(8,128)(2,1)S(1)} %all_to_all.5.got), custom_call_target="tpu_custom_call" | custom-call | tf_op jit(solution)/shard_map/finish/pallas_call | solution.py:199
  (1 shorter events, 0.0 us)
Async XLA Ops:
  1.4 6.3 %collective-permute-start.2 = (bf16[128,128]{1,0:T(8,128)(2,1)S(1)}, bf16[128,128]{1,0:T(8,128)(2,1)S(1)}, u32[]{:S(2)}, u32[]{:S(2)}) collective-permute-start(bf16[128,128]{1,0:T(8,128)(2,1)S(1)} %get-tuple-element.26), channel_id=1, source_target_pairs={{0,25},{1,24},{2,27},{3,26},{4,29},{5,28},{6,31},{7,30},{8,17},{9,... | collective-permute-start | bytes 98312 | tf_op jit(solution)/shard_map/ppermute | solution.py:29
  5.9 4.5 %collective-permute-start.1 = (bf16[128,128]{1,0:T(8,128)(2,1)S(1)}, bf16[128,128]{1,0:T(8,128)(2,1)S(1)}, u32[]{:S(2)}, u32[]{:S(2)}) collective-permute-start(bf16[128,128]{1,0:T(8,128)(2,1)S(1)} %get-tuple-element.26), channel_id=1, source_target_pairs={{0,17},{1,16},{2,19},{3,18},{4,21},{5,20},{6,23},{7,22},{8,25},{9,... | collective-permute-start | bytes 98312 | tf_op jit(solution)/shard_map/ppermute | solution.py:29
  5.9 4.5 %collective-permute-start = (bf16[128,128]{1,0:T(8,128)(2,1)S(1)}, bf16[128,128]{1,0:T(8,128)(2,1)S(1)}, u32[]{:S(2)}, u32[]{:S(2)}) collective-permute-start(bf16[128,128]{1,0:T(8,128)(2,1)S(1)} %get-tuple-element.26), channel_id=1, source_target_pairs={{0,9},{1,8},{2,11},{3,10},{4,13},{5,12},{6,15},{7,14},{8,1},{9,0},... | collective-permute-start | bytes 98312 | tf_op jit(solution)/shard_map/ppermute | solution.py:29
  10.5 3.6 %copy-start.1 = (bf16[128,256]{1,0:T(8,128)(2,1)S(1)}, bf16[128,256]{1,0:T(8,128)(2,1)}, u32[]{:S(2)}) copy-start(bf16[128,256]{1,0:T(8,128)(2,1)} %weight.3) | copy-start | bytes 196612
  10.5 3.6 %copy-start.2 = (bf16[128,256]{1,0:T(8,128)(2,1)S(1)}, bf16[128,256]{1,0:T(8,128)(2,1)}, u32[]{:S(2)}) copy-start(bf16[128,256]{1,0:T(8,128)(2,1)} %cot.1) | copy-start | bytes 196612
  10.5 3.6 %copy-start.4 = (s32[1,4,16]{2,1,0:T(4,128)S(1)}, s32[1,4,16]{2,1,0:T(4,128)}, u32[]{:S(2)}) copy-start(s32[1,4,16]{2,1,0:T(4,128)} %param.11) | copy-start | bytes 772
  10.5 8.0 %collective-permute-start.6 = (bf16[512,128]{1,0:T(8,128)(2,1)S(1)}, bf16[512,128]{1,0:T(8,128)(2,1)S(1)}, u32[]{:S(2)}, u32[]{:S(2)}) collective-permute-start(bf16[512,128]{1,0:T(8,128)(2,1)S(1)} %pad_maximum_fusion.refs_0_), channel_id=1, source_target_pairs={{0,6},{1,7},{2,4},{3,5},{4,2},{5,3},{6,0},{7,1},{8,14},{9,15},{10,... | collective-permute-start | bytes 393224 | tf_op jit(solution)/shard_map/ppermute | solution.py:29
  13.0 7.0 %collective-permute-start.5 = (bf16[512,128]{1,0:T(8,128)(2,1)S(1)}, bf16[512,128]{1,0:T(8,128)(2,1)S(1)}, u32[]{:S(2)}, u32[]{:S(2)}) collective-permute-start(bf16[512,128]{1,0:T(8,128)(2,1)S(1)} %pad_maximum_fusion.refs_0_), channel_id=1, source_target_pairs={{0,4},{1,5},{2,6},{3,7},{4,0},{5,1},{6,2},{7,3},{8,12},{9,13},{10,... | collective-permute-start | bytes 393224 | tf_op jit(solution)/shard_map/ppermute | solution.py:29
  13.5 6.6 %collective-permute-start.4 = (bf16[512,128]{1,0:T(8,128)(2,1)S(1)}, bf16[512,128]{1,0:T(8,128)(2,1)S(1)}, u32[]{:S(2)}, u32[]{:S(2)}) collective-permute-start(bf16[512,128]{1,0:T(8,128)(2,1)S(1)} %pad_maximum_fusion.refs_0_), channel_id=1, source_target_pairs={{0,2},{1,3},{2,0},{3,1},{4,6},{5,7},{6,4},{7,5},{8,10},{9,11},{10,... | collective-permute-start | bytes 393224 | tf_op jit(solution)/shard_map/ppermute | solution.py:29
  14.1 0.7 %copy-start.3 = (f32[256]{0:T(256)S(1)}, f32[256]{0:T(256)}, u32[]{:S(2)}) copy-start(f32[256]{0:T(256)} %param.9) | copy-start | bytes 3076
  14.1 0.7 %copy-start.5 = (s32[1,4]{1,0:T(1,128)S(1)}, s32[1,4]{1,0:T(1,128)}, u32[]{:S(2)}) copy-start(s32[1,4]{1,0:T(1,128)} %counts.1) | copy-start | bytes 52
  14.7 1.0 %copy-start = (bf16[1,4,16,4096]{3,2,1,0:T(8,128)(2,1)S(1)}, bf16[1,4,16,4096]{3,2,1,0:T(8,128)(2,1)}, u32[]{:S(2)}) copy-start(bf16[1,4,16,4096]{3,2,1,0:T(8,128)(2,1)} %param.12) | copy-start | bytes 1572868
  17.2 1.3 %collective-permute-start.3 = (bf16[256,128]{1,0:T(8,128)(2,1)S(1)}, bf16[256,128]{1,0:T(8,128)(2,1)S(1)}, u32[]{:S(2)}, u32[]{:S(2)}) collective-permute-start(bf16[256,128]{1,0:T(8,128)(2,1)S(1)} %get-tuple-element.16.cot_mine), channel_id=1, source_target_pairs={{0,1},{1,0},{2,3},{3,2},{4,5},{5,4},{6,7},{7,6},{8,9},{9,8},{10,11... | collective-permute-start | bytes 196616 | tf_op jit(solution)/shard_map/ppermute | solution.py:29
  20.6 1.4 %collective-permute-start.7 = (f32[256,128]{1,0:T(8,128)S(1)}, f32[256,128]{1,0:T(8,128)S(1)}, u32[]{:S(2)}, u32[]{:S(2)}) collective-permute-start(f32[256,128]{1,0:T(8,128)S(1)} %block_sum.1.mine), channel_id=1, source_target_pairs={{0,1},{1,0},{2,3},{3,2},{4,5},{5,4},{6,7},{7,6},{8,9},{9,8},{10,11... | collective-permute-start | bytes 393224 | tf_op jit(solution)/shard_map/ppermute | solution.py:29

commit v6 on v5

--- a/solution.py
+++ b/solution.py
@@ -217,9 +217,8 @@
     half_rows = features.shape[0] // 2
 
     keep = lax.dynamic_slice_in_dim(features, side * half_rows, half_rows, 0)
-    give = lax.dynamic_slice_in_dim(features, (1 - side) * half_rows, half_rows, 0)
     shift, radix = groups[0]
-    pieces = [keep] + [across(give, s << shift, owners, 1) for s in range(1, radix)]
+    pieces = [keep] + [across(keep, s << shift, owners, 0) for s in range(1, radix)]
     vals = block_vals[0]
     for shift, radix in groups[1:]:
         held, vals = lax.optimization_barrier((jnp.concatenate(pieces), vals))

time: 35.6 us -> 35.6 us (level)
  waiting for transfers between devices: 7.86 us -> 6.85 us
  blocking collectives: 12.1 us -> 12.8 us
  starting transfers between devices: 9.11 us -> 9.48 us
    ppermute x8, waiting for transfers between devices: 7.86 us -> 6.85 us  [across(): return lax.ppermute(value, BOTH, pairs)]
    unnamed x12 -> x14, local copies, waits for them, and re-layouts: 1.72 us -> 2.55 us
    dynamic_slice x1, local copies, waits for them, and re-layouts: 0.79 us -> 0.01 us  [body(): keep = lax.dynamic_slice_in_dim(features, side * half_rows, half_rows, 0)]
    all_to_all x1, blocking collectives: 12.1 us -> 12.8 us  [body(): got = lax.all_to_all(parts, 'rows', split_axis=0, concat_axis=0, tiled=True)]
    ppermute x8, starting transfers between devices: 9.11 us -> 9.48 us  [across(): return lax.ppermute(value, BOTH, pairs)]
  transfers between devices with their start and end apart: 8 -> 8, of which waited for: 6 -> 5; matrix products, arithmetic and copies ran while one was open for 0% -> 0% of each run, Pallas kernels for 4% -> 4%
where the time goes in v6:
time: 35.6 us; the launch traced here: 35.4 us
  blocking collectives  12.8 us (36%)
  starting transfers between devices  9.48 us (27%)
  waiting for transfers between devices  6.85 us (19%)
  Pallas kernels  3.02 us (8%)
  local copies, waits for them, and re-layouts  2.55 us (7%)
  between operations  0.71 us (2%)
    all_to_all x1, blocking collectives, body(): got = lax.all_to_all(parts, 'rows', split_axis=0, concat_axis=0, tiled=True)  12.8 us
    ppermute x8, starting transfers between devices, across(): return lax.ppermute(value, BOTH, pairs)  9.48 us
    ppermute x8, waiting for transfers between devices, across(): return lax.ppermute(value, BOTH, pairs)  6.85 us
    unnamed x14, local copies, waits for them, and re-layouts  2.55 us
    pallas_call x1, Pallas kernels, place_blocks(): pl.pallas_call(functools.partial(place_kernel, digit_groups(owners)), out...  1.37 us
    pallas_call x1, Pallas kernels, finish(): pl.pallas_call(finish_kernel, out_shape=(jax.ShapeDtypeStruct((mine.shape...  0.82 us
  transfers between devices with their start and end apart: 8, of which 5 were waited for; matrix products, arithmetic and copies ran while one was open for 0% of the time, Pallas kernels for 4%

profile of v6, /device:TPU:0, one launch (start us, length us, event | category | flops | bytes accessed | tf_op | source)
XLA Modules:
  0.0 35.4 jit_solution(6237564538207896657)
XLA Ops:
  0.6 0.0 copy-start
  0.6 0.8 %copy-done = bf16[256,128]{1,0:T(8,128)(2,1)S(1)} copy-done((bf16[256,128]{1,0:T(8,128)(2,1)S(1)}, bf16[256,128]{1,0:T(8,128)(2,1)}, u32[]{:S(2)}) %copy-start) | copy-done | bytes 65560
  1.5 0.0 copy-start.2
  1.5 0.0 copy-start.3
  1.5 5.1 %collective-permute-start.2 = (bf16[128,128]{1,0:T(8,128)(2,1)S(1)}, bf16[128,128]{1,0:T(8,128)(2,1)S(1)}, u32[]{:S(2)}, u32[]{:S(2)}) collective-permute-start(bf16[128,128]{1,0:T(8,128)(2,1)S(1)} %constant_dynamic-slice_fusion), channel_id=1, source_target_pairs={{0,24},{1,25},{2,26},{3,27},{4,28},{5,29},{6,30},{7,31},{8,16},{9,... | collective-permute-start | bytes 98312 | tf_op jit(solution)/shard_map/ppermute | solution.py:29
  6.6 0.0 collective-permute-start.1
  6.6 0.6 %collective-permute-start = (bf16[128,128]{1,0:T(8,128)(2,1)S(1)}, bf16[128,128]{1,0:T(8,128)(2,1)S(1)}, u32[]{:S(2)}, u32[]{:S(2)}) collective-permute-start(bf16[128,128]{1,0:T(8,128)(2,1)S(1)} %constant_dynamic-slice_fusion), channel_id=1, source_target_pairs={{0,8},{1,9},{2,10},{3,11},{4,12},{5,13},{6,14},{7,15},{8,0},{9,1},... | collective-permute-start | bytes 98312 | tf_op jit(solution)/shard_map/ppermute | solution.py:29
  7.2 1.3 %collective-permute-done.2 = bf16[128,128]{1,0:T(8,128)(2,1)S(1)} collective-permute-done((bf16[128,128]{1,0:T(8,128)(2,1)S(1)}, bf16[128,128]{1,0:T(8,128)(2,1)S(1)}, u32[]{:S(2)}, u32[]{:S(2)}) %collective-permute-start.2) | collective-permute-done | bytes 32800 | tf_op jit(solution)/shard_map/ppermute | solution.py:29
  8.5 2.9 %collective-permute-done.1 = bf16[128,128]{1,0:T(8,128)(2,1)S(1)} collective-permute-done((bf16[128,128]{1,0:T(8,128)(2,1)S(1)}, bf16[128,128]{1,0:T(8,128)(2,1)S(1)}, u32[]{:S(2)}, u32[]{:S(2)}) %collective-permute-start.1) | collective-permute-done | bytes 32800 | tf_op jit(solution)/shard_map/ppermute | solution.py:29
  11.4 0.0 collective-permute-done
  11.4 0.0 copy-start.5
  11.4 2.5 %collective-permute-start.6 = (bf16[512,128]{1,0:T(8,128)(2,1)S(1)}, bf16[512,128]{1,0:T(8,128)(2,1)S(1)}, u32[]{:S(2)}, u32[]{:S(2)}) collective-permute-start(bf16[512,128]{1,0:T(8,128)(2,1)S(1)} %pad_maximum_fusion.refs_0_), channel_id=1, source_target_pairs={{0,6},{1,7},{2,4},{3,5},{4,2},{5,3},{6,0},{7,1},{8,14},{9,15},{10,... | collective-permute-start | bytes 393224 | tf_op jit(solution)/shard_map/ppermute | solution.py:29
  13.9 0.5 %collective-permute-start.5 = (bf16[512,128]{1,0:T(8,128)(2,1)S(1)}, bf16[512,128]{1,0:T(8,128)(2,1)S(1)}, u32[]{:S(2)}, u32[]{:S(2)}) collective-permute-start(bf16[512,128]{1,0:T(8,128)(2,1)S(1)} %pad_maximum_fusion.refs_0_), channel_id=1, source_target_pairs={{0,4},{1,5},{2,6},{3,7},{4,0},{5,1},{6,2},{7,3},{8,12},{9,13},{10,... | collective-permute-start | bytes 393224 | tf_op jit(solution)/shard_map/ppermute | solution.py:29
  14.5 0.5 %collective-permute-start.4 = (bf16[512,128]{1,0:T(8,128)(2,1)S(1)}, bf16[512,128]{1,0:T(8,128)(2,1)S(1)}, u32[]{:S(2)}, u32[]{:S(2)}) collective-permute-start(bf16[512,128]{1,0:T(8,128)(2,1)S(1)} %pad_maximum_fusion.refs_0_), channel_id=1, source_target_pairs={{0,2},{1,3},{2,0},{3,1},{4,6},{5,7},{6,4},{7,5},{8,10},{9,11},{10,... | collective-permute-start | bytes 393224 | tf_op jit(solution)/shard_map/ppermute | solution.py:29
  15.0 0.0 copy-start.4
  15.0 0.0 copy-start.6
  15.0 0.0 copy-done.2
  15.0 0.0 copy-done.3
  15.0 0.0 copy-done.5
  15.0 0.7 %copy-done.4 = f32[256]{0:T(256)S(1)} copy-done((f32[256]{0:T(256)S(1)}, f32[256]{0:T(256)}, u32[]{:S(2)}) %copy-start.4) | copy-done | bytes 1048
  15.7 0.0 copy-done.6
  15.7 0.0 copy-start.1
  15.7 1.0 %copy-done.1 = bf16[1,4,16,4096]{3,2,1,0:T(8,128)(2,1)S(1)} copy-done((bf16[1,4,16,4096]{3,2,1,0:T(8,128)(2,1)S(1)}, bf16[1,4,16,4096]{3,2,1,0:T(8,128)(2,1)}, u32[]{:S(2)}) %copy-start.1) | copy-done | bytes 524312
  16.7 1.4 %place.1 = (bf16[16,256,128]{2,1,0:T(8,128)(2,1)S(1)}, bf16[256,128]{1,0:T(8,128)(2,1)S(1)}, bf16[256,128]{1,0:T(8,128)(2,1)S(1)}, f32[256,128]{1,0:T(8,128)S(1)}) custom-call(s32[1,4]{1,0:T(1,128)S(1)} %copy-done.6, s32[4,16]{1,0:T(4,128)S(1)} %bitcast.8, bf16[4,16,4096]{2,1,0:T(8,128)(2,1)S(1)} %bitcast.5, bf16[128,256]{1,0:T(8,128)(2,1)S(1)} %copy-done.3, ...), custom_call_target="tpu_custom_call" | custom-call | tf_op jit(solution)/shard_map/place/pallas_call | solution.py:95
  18.1 0.1 collective-permute-start.3
  18.2 1.2 %collective-permute-done.3.cot_other = bf16[256,128]{1,0:T(8,128)(2,1)S(1)} collective-permute-done((bf16[256,128]{1,0:T(8,128)(2,1)S(1)}, bf16[256,128]{1,0:T(8,128)(2,1)S(1)}, u32[]{:S(2)}, u32[]{:S(2)}) %collective-permute-start.3) | collective-permute-done | bytes 65568 | tf_op jit(solution)/shard_map/ppermute | solution.py:29
  19.4 0.0 collective-permute-done.6.refs_3_
  19.4 0.1 collective-permute-done.5.refs_2_
  19.5 0.0 collective-permute-done.4.refs_1_
  19.6 0.4 %block_sum.1.mine = f32[256,128]{1,0:T(8,128)S(1)} custom-call(bf16[16,256,128]{2,1,0:T(8,128)(2,1)S(1)} %get-tuple-element.17.dense, bf16[512,128]{1,0:T(8,128)(2,1)S(1)} %pad_maximum_fusion.refs_0_, bf16[512,128]{1,0:T(8,128)(2,1)S(1)} %collective-permute-done.4.refs_1_, bf16[512,128]{1,0:T(8,128)(2,1)S(1)} %collective-permute-done.5.refs_2_, ...), custom_call_target="tpu_custom_call" | custom-call | tf_op jit(solution)/shard_map/block_sum/pallas_call | solution.py:135
  20.0 0.1 collective-permute-start.7
  20.1 1.3 %collective-permute-done.7.other = f32[256,128]{1,0:T(8,128)S(1)} collective-permute-done((f32[256,128]{1,0:T(8,128)S(1)}, f32[256,128]{1,0:T(8,128)S(1)}, u32[]{:S(2)}, u32[]{:S(2)}) %collective-permute-start.7) | collective-permute-done | bytes 131104 | tf_op jit(solution)/shard_map/ppermute | solution.py:29
  21.4 0.4 %layer.1 = bf16[16,32,128]{2,1,0:T(8,128)(2,1)S(1)} custom-call(f32[256,128]{1,0:T(8,128)S(1)} %block_sum.1.mine, f32[256,128]{1,0:T(8,128)S(1)} %collective-permute-done.7.other, bf16[256,128]{1,0:T(8,128)(2,1)S(1)} %get-tuple-element.19.weight_t, f32[256,128]{1,0:T(8,128)S(1)} %get-tuple-element.20.bias_t, ...), custom_call_target="tpu_custom_call" | custom-call | tf_op jit(solution)/shard_map/layer/pallas_call | solution.py:171
  21.8 12.8 %all_to_all.5.got = bf16[16,32,128]{2,1,0:T(8,128)(2,1)S(1)} all-to-all(bf16[16,32,128]{2,1,0:T(8,128)(2,1)S(1)} %layer.1), channel_id=1, replica_groups=mesh['rows'=16,'rep'=2] {'rows'}, dimensions={0} | all-to-all | bytes 262144 | tf_op jit(solution)/shard_map/all_to_all | solution.py:237
  34.6 0.8 %finish.1 = (bf16[128,256]{1,0:T(8,128)(2,1)}, f32[16,128]{1,0:T(8,128)}, f32[1,16]{1,0:T(1,128)}) custom-call(f32[256,128]{1,0:T(8,128)S(1)} %block_sum.1.mine, f32[256,128]{1,0:T(8,128)S(1)} %collective-permute-done.7.other, bf16[128,256]{1,0:T(8,128)(2,1)S(1)} %copy-done.2, f32[1,256]{1,0:T(1,128)S(1)} %bitcast.7, bf16[16,32,128]{2,1,0:T(8,128)(2,1)S(1)} %all_to_all.5.got), custom_call_target="tpu_custom_call" | custom-call | tf_op jit(solution)/shard_map/finish/pallas_call | solution.py:199
  (2 shorter events, 0.0 us)
Async XLA Ops:
  0.6 0.8 %copy-start = (bf16[256,128]{1,0:T(8,128)(2,1)S(1)}, bf16[256,128]{1,0:T(8,128)(2,1)}, u32[]{:S(2)}) copy-start(bf16[256,128]{1,0:T(8,128)(2,1)} %param.7) | copy-start | bytes 196612
  1.5 13.5 %copy-start.2 = (bf16[128,256]{1,0:T(8,128)(2,1)S(1)}, bf16[128,256]{1,0:T(8,128)(2,1)}, u32[]{:S(2)}) copy-start(bf16[128,256]{1,0:T(8,128)(2,1)} %weight.3) | copy-start | bytes 196612
  1.5 13.5 %copy-start.3 = (bf16[128,256]{1,0:T(8,128)(2,1)S(1)}, bf16[128,256]{1,0:T(8,128)(2,1)}, u32[]{:S(2)}) copy-start(bf16[128,256]{1,0:T(8,128)(2,1)} %cot.1) | copy-start | bytes 196612
  1.5 7.0 %collective-permute-start.2 = (bf16[128,128]{1,0:T(8,128)(2,1)S(1)}, bf16[128,128]{1,0:T(8,128)(2,1)S(1)}, u32[]{:S(2)}, u32[]{:S(2)}) collective-permute-start(bf16[128,128]{1,0:T(8,128)(2,1)S(1)} %constant_dynamic-slice_fusion), channel_id=1, source_target_pairs={{0,24},{1,25},{2,26},{3,27},{4,28},{5,29},{6,30},{7,31},{8,16},{9,... | collective-permute-start | bytes 98312 | tf_op jit(solution)/shard_map/ppermute | solution.py:29
  6.6 4.8 %collective-permute-start.1 = (bf16[128,128]{1,0:T(8,128)(2,1)S(1)}, bf16[128,128]{1,0:T(8,128)(2,1)S(1)}, u32[]{:S(2)}, u32[]{:S(2)}) collective-permute-start(bf16[128,128]{1,0:T(8,128)(2,1)S(1)} %constant_dynamic-slice_fusion), channel_id=1, source_target_pairs={{0,16},{1,17},{2,18},{3,19},{4,20},{5,21},{6,22},{7,23},{8,24},{9,... | collective-permute-start | bytes 98312 | tf_op jit(solution)/shard_map/ppermute | solution.py:29
  6.6 4.8 %collective-permute-start = (bf16[128,128]{1,0:T(8,128)(2,1)S(1)}, bf16[128,128]{1,0:T(8,128)(2,1)S(1)}, u32[]{:S(2)}, u32[]{:S(2)}) collective-permute-start(bf16[128,128]{1,0:T(8,128)(2,1)S(1)} %constant_dynamic-slice_fusion), channel_id=1, source_target_pairs={{0,8},{1,9},{2,10},{3,11},{4,12},{5,13},{6,14},{7,15},{8,0},{9,1},... | collective-permute-start | bytes 98312 | tf_op jit(solution)/shard_map/ppermute | solution.py:29
  11.4 3.6 %copy-start.5 = (s32[1,4,16]{2,1,0:T(4,128)S(1)}, s32[1,4,16]{2,1,0:T(4,128)}, u32[]{:S(2)}) copy-start(s32[1,4,16]{2,1,0:T(4,128)} %param.11) | copy-start | bytes 772
  11.4 8.0 %collective-permute-start.6 = (bf16[512,128]{1,0:T(8,128)(2,1)S(1)}, bf16[512,128]{1,0:T(8,128)(2,1)S(1)}, u32[]{:S(2)}, u32[]{:S(2)}) collective-permute-start(bf16[512,128]{1,0:T(8,128)(2,1)S(1)} %pad_maximum_fusion.refs_0_), channel_id=1, source_target_pairs={{0,6},{1,7},{2,4},{3,5},{4,2},{5,3},{6,0},{7,1},{8,14},{9,15},{10,... | collective-permute-start | bytes 393224 | tf_op jit(solution)/shard_map/ppermute | solution.py:29
  13.9 5.6 %collective-permute-start.5 = (bf16[512,128]{1,0:T(8,128)(2,1)S(1)}, bf16[512,128]{1,0:T(8,128)(2,1)S(1)}, u32[]{:S(2)}, u32[]{:S(2)}) collective-permute-start(bf16[512,128]{1,0:T(8,128)(2,1)S(1)} %pad_maximum_fusion.refs_0_), channel_id=1, source_target_pairs={{0,4},{1,5},{2,6},{3,7},{4,0},{5,1},{6,2},{7,3},{8,12},{9,13},{10,... | collective-permute-start | bytes 393224 | tf_op jit(solution)/shard_map/ppermute | solution.py:29
  14.5 5.1 %collective-permute-start.4 = (bf16[512,128]{1,0:T(8,128)(2,1)S(1)}, bf16[512,128]{1,0:T(8,128)(2,1)S(1)}, u32[]{:S(2)}, u32[]{:S(2)}) collective-permute-start(bf16[512,128]{1,0:T(8,128)(2,1)S(1)} %pad_maximum_fusion.refs_0_), channel_id=1, source_target_pairs={{0,2},{1,3},{2,0},{3,1},{4,6},{5,7},{6,4},{7,5},{8,10},{9,11},{10,... | collective-permute-start | bytes 393224 | tf_op jit(solution)/shard_map/ppermute | solution.py:29
  15.0 0.7 %copy-start.4 = (f32[256]{0:T(256)S(1)}, f32[256]{0:T(256)}, u32[]{:S(2)}) copy-start(f32[256]{0:T(256)} %param.9) | copy-start | bytes 3076
  15.0 0.7 %copy-start.6 = (s32[1,4]{1,0:T(1,128)S(1)}, s32[1,4]{1,0:T(1,128)}, u32[]{:S(2)}) copy-start(s32[1,4]{1,0:T(1,128)} %counts.1) | copy-start | bytes 52
  15.7 1.0 %copy-start.1 = (bf16[1,4,16,4096]{3,2,1,0:T(8,128)(2,1)S(1)}, bf16[1,4,16,4096]{3,2,1,0:T(8,128)(2,1)}, u32[]{:S(2)}) copy-start(bf16[1,4,16,4096]{3,2,1,0:T(8,128)(2,1)} %param.12) | copy-start | bytes 1572868
  18.1 1.3 %collective-permute-start.3 = (bf16[256,128]{1,0:T(8,128)(2,1)S(1)}, bf16[256,128]{1,0:T(8,128)(2,1)S(1)}, u32[]{:S(2)}, u32[]{:S(2)}) collective-permute-start(bf16[256,128]{1,0:T(8,128)(2,1)S(1)} %get-tuple-element.16.cot_mine), channel_id=1, source_target_pairs={{0,1},{1,0},{2,3},{3,2},{4,5},{5,4},{6,7},{7,6},{8,9},{9,8},{10,11... | collective-permute-start | bytes 196616 | tf_op jit(solution)/shard_map/ppermute | solution.py:29
  20.0 1.4 %collective-permute-start.7 = (f32[256,128]{1,0:T(8,128)S(1)}, f32[256,128]{1,0:T(8,128)S(1)}, u32[]{:S(2)}, u32[]{:S(2)}) collective-permute-start(f32[256,128]{1,0:T(8,128)S(1)} %block_sum.1.mine), channel_id=1, source_target_pairs={{0,1},{1,0},{2,3},{3,2},{4,5},{5,4},{6,7},{7,6},{8,9},{9,8},{10,11... | collective-permute-start | bytes 393224 | tf_op jit(solution)/shard_map/ppermute | solution.py:29

commit v7 on v6

--- a/solution.py
+++ b/solution.py
@@ -27,6 +27,25 @@
 def across(value, mask, owners, swap):
     pairs = [(i, i ^ (2 * mask + swap)) for i in range(2 * owners)]
     return lax.ppermute(value, BOTH, pairs)
+
+
+def copy_kernel(value, out):
+    out[...] = value[...]
+
+
+def copies(value, count):
+    out = [value]
+    while len(out) < count:
+        one = pl.pallas_call(
+            copy_kernel,
+            out_shape=jax.ShapeDtypeStruct(value.shape, value.dtype),
+            in_specs=[VMEM],
+            out_specs=VMEM,
+            compiler_params=pltpu.CompilerParams(vmem_limit_bytes=16 << 20),
+            name="copy",
+        )(out[-1])
+        out.append(one)
+    return out
 
 
 def limit(owners):
@@ -218,11 +237,13 @@
 
     keep = lax.dynamic_slice_in_dim(features, side * half_rows, half_rows, 0)
     shift, radix = groups[0]
-    pieces = [keep] + [across(keep, s << shift, owners, 0) for s in range(1, radix)]
+    sent = zip(range(1, radix), copies(keep, radix - 1))
+    pieces = [keep] + [across(value, s << shift, owners, 0) for s, value in sent]
     vals = block_vals[0]
     for shift, radix in groups[1:]:
         held, vals = lax.optimization_barrier((jnp.concatenate(pieces), vals))
-        pieces = [held] + [across(held, s << shift, owners, 0) for s in range(1, radix)]
+        sent = zip(range(1, radix), copies(held, radix - 1))
+        pieces = [held] + [across(value, s << shift, owners, 0) for s, value in sent]
 
     bias = bias.reshape(1, -1)
     dense, cot_mine, weight_t, bias_t = place_blocks(

time: 35.6 us -> 34.7 us (0.975)
  waiting for transfers between devices: 6.85 us -> 7.93 us
  local copies, waits for them, and re-layouts: 2.55 us -> 1.5 us
  blocking collectives: 12.8 us -> 11.8 us
    ppermute x8, waiting for transfers between devices: 6.85 us -> 7.93 us  [across(): return lax.ppermute(value, BOTH, pairs)]
    unnamed x14, local copies, waits for them, and re-layouts: 2.55 us -> 1.5 us
    all_to_all x1, blocking collectives: 12.8 us -> 11.8 us  [body(): got = lax.all_to_all(parts, 'rows', split_axis=0, concat_axis=0, tiled=True)]
  transfers between devices with their start and end apart: 8 -> 8, of which waited for: 5 -> 6; matrix products, arithmetic and copies ran while one was open for 0% -> 0% of each run, Pallas kernels for 4% -> 4%
where the time goes in v7:
time: 34.7 us; the launch traced here: 34.5 us
  blocking collectives  11.8 us (34%)
  starting transfers between devices  9.45 us (27%)
  waiting for transfers between devices  7.93 us (23%)
  Pallas kernels  3.04 us (9%)
  local copies, waits for them, and re-layouts  1.5 us (4%)
  between operations  0.76 us (2%)
    all_to_all x1, blocking collectives, body(): got = lax.all_to_all(parts, 'rows', split_axis=0, concat_axis=0, tiled=True)  11.8 us
    ppermute x8, starting transfers between devices, across(): return lax.ppermute(value, BOTH, pairs)  9.45 us
    ppermute x8, waiting for transfers between devices, across(): return lax.ppermute(value, BOTH, pairs)  7.93 us
    unnamed x14, local copies, waits for them, and re-layouts  1.5 us
    pallas_call x1, Pallas kernels, place_blocks(): pl.pallas_call(functools.partial(place_kernel, digit_groups(owners)), out...  1.36 us
    pallas_call x1, Pallas kernels, finish(): pl.pallas_call(finish_kernel, out_shape=(jax.ShapeDtypeStruct((mine.shape...  0.82 us
  transfers between devices with their start and end apart: 8, of which 6 were waited for; matrix products, arithmetic and copies ran while one was open for 0% of the time, Pallas kernels for 4%

profile of v7, /device:TPU:0, one launch (start us, length us, event | category | flops | bytes accessed | tf_op | source)
XLA Modules:
  0.0 34.5 jit_solution(785557476027353760)
XLA Ops:
  0.6 0.0 copy-start
  0.6 0.0 copy-start.1
  0.7 0.8 %copy-done = bf16[256,128]{1,0:T(8,128)(2,1)S(1)} copy-done((bf16[256,128]{1,0:T(8,128)(2,1)S(1)}, bf16[256,128]{1,0:T(8,128)(2,1)}, u32[]{:S(2)}) %copy-start) | copy-done | bytes 65560
  1.5 5.1 %collective-permute-start.2 = (bf16[128,128]{1,0:T(8,128)(2,1)S(1)}, bf16[128,128]{1,0:T(8,128)(2,1)S(1)}, u32[]{:S(2)}, u32[]{:S(2)}) collective-permute-start(bf16[128,128]{1,0:T(8,128)(2,1)S(1)} %copy.15), channel_id=1, source_target_pairs={{0,24},{1,25},{2,26},{3,27},{4,28},{5,29},{6,30},{7,31},{8,16},{9,... | collective-permute-start | bytes 98312 | tf_op jit(solution)/shard_map/ppermute | solution.py:29
  6.6 0.0 collective-permute-start.1
  6.6 0.6 %collective-permute-start = (bf16[128,128]{1,0:T(8,128)(2,1)S(1)}, bf16[128,128]{1,0:T(8,128)(2,1)S(1)}, u32[]{:S(2)}, u32[]{:S(2)}) collective-permute-start(bf16[128,128]{1,0:T(8,128)(2,1)S(1)} %constant_dynamic-slice_fusion.value), channel_id=1, source_target_pairs={{0,8},{1,9},{2,10},{3,11},{4,12},{5,13},{6,14},{7,15},{8,0},{9,1},... | collective-permute-start | bytes 98312 | tf_op jit(solution)/shard_map/ppermute | solution.py:29
  7.2 1.3 %collective-permute-done.2 = bf16[128,128]{1,0:T(8,128)(2,1)S(1)} collective-permute-done((bf16[128,128]{1,0:T(8,128)(2,1)S(1)}, bf16[128,128]{1,0:T(8,128)(2,1)S(1)}, u32[]{:S(2)}, u32[]{:S(2)}) %collective-permute-start.2) | collective-permute-done | bytes 32800 | tf_op jit(solution)/shard_map/ppermute | solution.py:29
  8.5 2.9 %collective-permute-done.1 = bf16[128,128]{1,0:T(8,128)(2,1)S(1)} collective-permute-done((bf16[128,128]{1,0:T(8,128)(2,1)S(1)}, bf16[128,128]{1,0:T(8,128)(2,1)S(1)}, u32[]{:S(2)}, u32[]{:S(2)}) %collective-permute-start.1) | collective-permute-done | bytes 32800 | tf_op jit(solution)/shard_map/ppermute | solution.py:29
  11.4 0.0 collective-permute-done
  11.5 0.0 copy-start.2
  11.5 0.0 copy-start.3
  11.5 0.0 copy-start.5
  11.5 2.5 %collective-permute-start.6 = (bf16[512,128]{1,0:T(8,128)(2,1)S(1)}, bf16[512,128]{1,0:T(8,128)(2,1)S(1)}, u32[]{:S(2)}, u32[]{:S(2)}) collective-permute-start(bf16[512,128]{1,0:T(8,128)(2,1)S(1)} %copy.17), channel_id=1, source_target_pairs={{0,6},{1,7},{2,4},{3,5},{4,2},{5,3},{6,0},{7,1},{8,14},{9,15},{10,... | collective-permute-start | bytes 393224 | tf_op jit(solution)/shard_map/ppermute | solution.py:29
  14.0 0.5 %collective-permute-start.5 = (bf16[512,128]{1,0:T(8,128)(2,1)S(1)}, bf16[512,128]{1,0:T(8,128)(2,1)S(1)}, u32[]{:S(2)}, u32[]{:S(2)}) collective-permute-start(bf16[512,128]{1,0:T(8,128)(2,1)S(1)} %copy.16.value), channel_id=1, source_target_pairs={{0,4},{1,5},{2,6},{3,7},{4,0},{5,1},{6,2},{7,3},{8,12},{9,13},{10,... | collective-permute-start | bytes 393224 | tf_op jit(solution)/shard_map/ppermute | solution.py:29
  14.5 0.5 %collective-permute-start.4 = (bf16[512,128]{1,0:T(8,128)(2,1)S(1)}, bf16[512,128]{1,0:T(8,128)(2,1)S(1)}, u32[]{:S(2)}, u32[]{:S(2)}) collective-permute-start(bf16[512,128]{1,0:T(8,128)(2,1)S(1)} %pad_maximum_fusion.value.refs_0_), channel_id=1, source_target_pairs={{0,2},{1,3},{2,0},{3,1},{4,6},{5,7},{6,4},{7,5},{8,10},{9,11},{10,... | collective-permute-start | bytes 393224 | tf_op jit(solution)/shard_map/ppermute | solution.py:29
  15.1 0.0 copy-start.4
  15.1 0.0 copy-start.6
  15.1 0.0 copy-done.1
  15.1 0.0 copy-done.2
  15.1 0.0 copy-done.3
  15.1 0.0 copy-done.5
  15.1 0.6 %copy-done.4 = f32[256]{0:T(256)S(1)} copy-done((f32[256]{0:T(256)S(1)}, f32[256]{0:T(256)}, u32[]{:S(2)}) %copy-start.4) | copy-done | bytes 1048
  15.7 0.0 copy-done.6
  15.7 1.4 %place.1 = (bf16[16,256,128]{2,1,0:T(8,128)(2,1)S(1)}, bf16[256,128]{1,0:T(8,128)(2,1)S(1)}, bf16[256,128]{1,0:T(8,128)(2,1)S(1)}, f32[256,128]{1,0:T(8,128)S(1)}) custom-call(s32[1,4]{1,0:T(1,128)S(1)} %copy-done.6, s32[4,16]{1,0:T(4,128)S(1)} %bitcast.8, bf16[4,16,4096]{2,1,0:T(8,128)(2,1)S(1)} %bitcast.5, bf16[128,256]{1,0:T(8,128)(2,1)S(1)} %copy-done.3, ...), custom_call_target="tpu_custom_call" | custom-call | tf_op jit(solution)/shard_map/place/pallas_call | solution.py:114
  17.1 0.1 collective-permute-start.3
  17.2 1.2 %collective-permute-done.3.cot_other = bf16[256,128]{1,0:T(8,128)(2,1)S(1)} collective-permute-done((bf16[256,128]{1,0:T(8,128)(2,1)S(1)}, bf16[256,128]{1,0:T(8,128)(2,1)S(1)}, u32[]{:S(2)}, u32[]{:S(2)}) %collective-permute-start.3) | collective-permute-done | bytes 65568 | tf_op jit(solution)/shard_map/ppermute | solution.py:29
  18.4 0.4 %collective-permute-done.6.refs_3_ = bf16[512,128]{1,0:T(8,128)(2,1)S(1)} collective-permute-done((bf16[512,128]{1,0:T(8,128)(2,1)S(1)}, bf16[512,128]{1,0:T(8,128)(2,1)S(1)}, u32[]{:S(2)}, u32[]{:S(2)}) %collective-permute-start.6) | collective-permute-done | bytes 131104 | tf_op jit(solution)/shard_map/ppermute | solution.py:29
  18.8 0.8 %collective-permute-done.5.refs_2_ = bf16[512,128]{1,0:T(8,128)(2,1)S(1)} collective-permute-done((bf16[512,128]{1,0:T(8,128)(2,1)S(1)}, bf16[512,128]{1,0:T(8,128)(2,1)S(1)}, u32[]{:S(2)}, u32[]{:S(2)}) %collective-permute-start.5) | collective-permute-done | bytes 131104 | tf_op jit(solution)/shard_map/ppermute | solution.py:29
  19.6 0.0 collective-permute-done.4.refs_1_
  19.6 0.4 %block_sum.1.mine = f32[256,128]{1,0:T(8,128)S(1)} custom-call(bf16[16,256,128]{2,1,0:T(8,128)(2,1)S(1)} %get-tuple-element.17.dense, bf16[512,128]{1,0:T(8,128)(2,1)S(1)} %pad_maximum_fusion.value.refs_0_, bf16[512,128]{1,0:T(8,128)(2,1)S(1)} %collective-permute-done.4.refs_1_, bf16[512,128]{1,0:T(8,128)(2,1)S(1)} %collective-permute-done.5.refs_2_, ...), custom_call_target="tpu_custom_call" | custom-call | tf_op jit(solution)/shard_map/block_sum/pallas_call | solution.py:154
  20.1 0.1 collective-permute-start.7
  20.1 1.3 %collective-permute-done.7.other = f32[256,128]{1,0:T(8,128)S(1)} collective-permute-done((f32[256,128]{1,0:T(8,128)S(1)}, f32[256,128]{1,0:T(8,128)S(1)}, u32[]{:S(2)}, u32[]{:S(2)}) %collective-permute-start.7) | collective-permute-done | bytes 131104 | tf_op jit(solution)/shard_map/ppermute | solution.py:29
  21.5 0.4 %layer.1 = bf16[16,32,128]{2,1,0:T(8,128)(2,1)S(1)} custom-call(f32[256,128]{1,0:T(8,128)S(1)} %block_sum.1.mine, f32[256,128]{1,0:T(8,128)S(1)} %collective-permute-done.7.other, bf16[256,128]{1,0:T(8,128)(2,1)S(1)} %get-tuple-element.19.weight_t, f32[256,128]{1,0:T(8,128)S(1)} %get-tuple-element.20.bias_t, ...), custom_call_target="tpu_custom_call" | custom-call | tf_op jit(solution)/shard_map/layer/pallas_call | solution.py:190
  21.9 11.8 %all_to_all.5.got = bf16[16,32,128]{2,1,0:T(8,128)(2,1)S(1)} all-to-all(bf16[16,32,128]{2,1,0:T(8,128)(2,1)S(1)} %layer.1), channel_id=1, replica_groups=mesh['rows'=16,'rep'=2] {'rows'}, dimensions={0} | all-to-all | bytes 262144 | tf_op jit(solution)/shard_map/all_to_all | solution.py:258
  33.7 0.8 %finish.1 = (bf16[128,256]{1,0:T(8,128)(2,1)}, f32[16,128]{1,0:T(8,128)}, f32[1,16]{1,0:T(1,128)}) custom-call(f32[256,128]{1,0:T(8,128)S(1)} %block_sum.1.mine, f32[256,128]{1,0:T(8,128)S(1)} %collective-permute-done.7.other, bf16[128,256]{1,0:T(8,128)(2,1)S(1)} %copy-done.2, f32[1,256]{1,0:T(1,128)S(1)} %bitcast.7, bf16[16,32,128]{2,1,0:T(8,128)(2,1)S(1)} %all_to_all.5.got), custom_call_target="tpu_custom_call" | custom-call | tf_op jit(solution)/shard_map/finish/pallas_call | solution.py:218
  (6 shorter events, 0.0 us)
Async XLA Ops:
  0.6 0.8 %copy-start = (bf16[256,128]{1,0:T(8,128)(2,1)S(1)}, bf16[256,128]{1,0:T(8,128)(2,1)}, u32[]{:S(2)}) copy-start(bf16[256,128]{1,0:T(8,128)(2,1)} %param.7) | copy-start | bytes 196612
  0.6 14.4 %copy-start.1 = (bf16[1,4,16,4096]{3,2,1,0:T(8,128)(2,1)S(1)}, bf16[1,4,16,4096]{3,2,1,0:T(8,128)(2,1)}, u32[]{:S(2)}) copy-start(bf16[1,4,16,4096]{3,2,1,0:T(8,128)(2,1)} %param.12) | copy-start | bytes 1572868
  1.5 7.0 %collective-permute-start.2 = (bf16[128,128]{1,0:T(8,128)(2,1)S(1)}, bf16[128,128]{1,0:T(8,128)(2,1)S(1)}, u32[]{:S(2)}, u32[]{:S(2)}) collective-permute-start(bf16[128,128]{1,0:T(8,128)(2,1)S(1)} %copy.15), channel_id=1, source_target_pairs={{0,24},{1,25},{2,26},{3,27},{4,28},{5,29},{6,30},{7,31},{8,16},{9,... | collective-permute-start | bytes 98312 | tf_op jit(solution)/shard_map/ppermute | solution.py:29
  6.6 4.8 %collective-permute-start.1 = (bf16[128,128]{1,0:T(8,128)(2,1)S(1)}, bf16[128,128]{1,0:T(8,128)(2,1)S(1)}, u32[]{:S(2)}, u32[]{:S(2)}) collective-permute-start(bf16[128,128]{1,0:T(8,128)(2,1)S(1)} %copy.14.value), channel_id=1, source_target_pairs={{0,16},{1,17},{2,18},{3,19},{4,20},{5,21},{6,22},{7,23},{8,24},{9,... | collective-permute-start | bytes 98312 | tf_op jit(solution)/shard_map/ppermute | solution.py:29
  6.6 4.8 %collective-permute-start = (bf16[128,128]{1,0:T(8,128)(2,1)S(1)}, bf16[128,128]{1,0:T(8,128)(2,1)S(1)}, u32[]{:S(2)}, u32[]{:S(2)}) collective-permute-start(bf16[128,128]{1,0:T(8,128)(2,1)S(1)} %constant_dynamic-slice_fusion.value), channel_id=1, source_target_pairs={{0,8},{1,9},{2,10},{3,11},{4,12},{5,13},{6,14},{7,15},{8,0},{9,1},... | collective-permute-start | bytes 98312 | tf_op jit(solution)/shard_map/ppermute | solution.py:29
  11.5 3.6 %copy-start.2 = (bf16[128,256]{1,0:T(8,128)(2,1)S(1)}, bf16[128,256]{1,0:T(8,128)(2,1)}, u32[]{:S(2)}) copy-start(bf16[128,256]{1,0:T(8,128)(2,1)} %weight.3) | copy-start | bytes 196612
  11.5 3.6 %copy-start.3 = (bf16[128,256]{1,0:T(8,128)(2,1)S(1)}, bf16[128,256]{1,0:T(8,128)(2,1)}, u32[]{:S(2)}) copy-start(bf16[128,256]{1,0:T(8,128)(2,1)} %cot.1) | copy-start | bytes 196612
  11.5 3.6 %copy-start.5 = (s32[1,4,16]{2,1,0:T(4,128)S(1)}, s32[1,4,16]{2,1,0:T(4,128)}, u32[]{:S(2)}) copy-start(s32[1,4,16]{2,1,0:T(4,128)} %param.11) | copy-start | bytes 772
  11.5 7.3 %collective-permute-start.6 = (bf16[512,128]{1,0:T(8,128)(2,1)S(1)}, bf16[512,128]{1,0:T(8,128)(2,1)S(1)}, u32[]{:S(2)}, u32[]{:S(2)}) collective-permute-start(bf16[512,128]{1,0:T(8,128)(2,1)S(1)} %copy.17), channel_id=1, source_target_pairs={{0,6},{1,7},{2,4},{3,5},{4,2},{5,3},{6,0},{7,1},{8,14},{9,15},{10,... | collective-permute-start | bytes 393224 | tf_op jit(solution)/shard_map/ppermute | solution.py:29
  14.0 5.6 %collective-permute-start.5 = (bf16[512,128]{1,0:T(8,128)(2,1)S(1)}, bf16[512,128]{1,0:T(8,128)(2,1)S(1)}, u32[]{:S(2)}, u32[]{:S(2)}) collective-permute-start(bf16[512,128]{1,0:T(8,128)(2,1)S(1)} %copy.16.value), channel_id=1, source_target_pairs={{0,4},{1,5},{2,6},{3,7},{4,0},{5,1},{6,2},{7,3},{8,12},{9,13},{10,... | collective-permute-start | bytes 393224 | tf_op jit(solution)/shard_map/ppermute | solution.py:29
  14.5 5.1 %collective-permute-start.4 = (bf16[512,128]{1,0:T(8,128)(2,1)S(1)}, bf16[512,128]{1,0:T(8,128)(2,1)S(1)}, u32[]{:S(2)}, u32[]{:S(2)}) collective-permute-start(bf16[512,128]{1,0:T(8,128)(2,1)S(1)} %pad_maximum_fusion.value.refs_0_), channel_id=1, source_target_pairs={{0,2},{1,3},{2,0},{3,1},{4,6},{5,7},{6,4},{7,5},{8,10},{9,11},{10,... | collective-permute-start | bytes 393224 | tf_op jit(solution)/shard_map/ppermute | solution.py:29
  15.1 0.7 %copy-start.4 = (f32[256]{0:T(256)S(1)}, f32[256]{0:T(256)}, u32[]{:S(2)}) copy-start(f32[256]{0:T(256)} %param.9) | copy-start | bytes 3076
  15.1 0.7 %copy-start.6 = (s32[1,4]{1,0:T(1,128)S(1)}, s32[1,4]{1,0:T(1,128)}, u32[]{:S(2)}) copy-start(s32[1,4]{1,0:T(1,128)} %counts.1) | copy-start | bytes 52
  17.1 1.3 %collective-permute-start.3 = (bf16[256,128]{1,0:T(8,128)(2,1)S(1)}, bf16[256,128]{1,0:T(8,128)(2,1)S(1)}, u32[]{:S(2)}, u32[]{:S(2)}) collective-permute-start(bf16[256,128]{1,0:T(8,128)(2,1)S(1)} %get-tuple-element.16.cot_mine), channel_id=1, source_target_pairs={{0,1},{1,0},{2,3},{3,2},{4,5},{5,4},{6,7},{7,6},{8,9},{9,8},{10,11... | collective-permute-start | bytes 196616 | tf_op jit(solution)/shard_map/ppermute | solution.py:29
  20.1 1.4 %collective-permute-start.7 = (f32[256,128]{1,0:T(8,128)S(1)}, f32[256,128]{1,0:T(8,128)S(1)}, u32[]{:S(2)}, u32[]{:S(2)}) collective-permute-start(f32[256,128]{1,0:T(8,128)S(1)} %block_sum.1.mine), channel_id=1, source_target_pairs={{0,1},{1,0},{2,3},{3,2},{4,5},{5,4},{6,7},{7,6},{8,9},{9,8},{10,11... | collective-permute-start | bytes 393224 | tf_op jit(solution)/shard_map/ppermute | solution.py:29

commit v8 on v7

--- a/solution.py
+++ b/solution.py
@@ -52,10 +52,9 @@
     return pltpu.CompilerParams(vmem_limit_bytes=(8 if owners <= 16 else 48) << 20)
 
 
-def place_kernel(groups, counts, cols, vals, cot, weight, bias, dense, cot_out, weight_out, bias_out):
+def place_kernel(groups, counts, cols, vals, weight, bias, dense, weight_out, bias_out):
     nblk, slots, flat = vals.shape
     owners = dense.shape[0]
-    cot_out[...] = cot[...].astype(jnp.float32).T.astype(jnp.bfloat16)
     weight_out[...] = weight[...].astype(jnp.float32).T.astype(jnp.bfloat16)
     bias_out[...] = jnp.broadcast_to(bias[...], (128, bias.shape[1])).T
     wide = flat // 128
@@ -108,34 +107,35 @@
             pl.loop(0, owners // 16)(put)
 
 
-def place_blocks(counts, cols, vals, cot, weight, bias, owners):
+def place_blocks(counts, cols, vals, weight, bias, owners):
     nblk, slots, flat = vals.shape
     wide = flat // 128
     return pl.pallas_call(
         functools.partial(place_kernel, digit_groups(owners)),
         out_shape=(
             jax.ShapeDtypeStruct((owners, 2 * nblk * wide, 128), jnp.bfloat16),
-            jax.ShapeDtypeStruct(cot.shape[::-1], cot.dtype),
             jax.ShapeDtypeStruct(weight.shape[::-1], weight.dtype),
             jax.ShapeDtypeStruct((bias.shape[1], 128), bias.dtype),
         ),
-        in_specs=[SMEM] + [VMEM] * 5,
-        out_specs=(VMEM,) * 4,
+        in_specs=[SMEM] + [VMEM] * 4,
+        out_specs=(VMEM,) * 3,
         compiler_params=limit(owners),
         name="place",
-    )(counts, cols, vals, cot, weight, bias)
-
-
-def sum_kernel(dense, *refs):
+    )(counts, cols, vals, weight, bias)
+
+
+def sum_kernel(places, last, dense, *refs):
     pieces, out = refs[:-1], refs[-1]
-    owners, rows, _ = dense.shape
-    each = owners // len(pieces)
-    acc = jnp.zeros((rows, 128), jnp.float32)
-    for s, feats in enumerate(pieces):
+    rows = dense.shape[1]
+    if last:
+        acc, pieces = pieces[0][...], pieces[1:]
+    else:
+        acc = jnp.zeros((rows, 128), jnp.float32)
+    for start, feats in zip(places, pieces):
+        each = feats.shape[0] // 128
 
         def two(q, acc):
-            at = s * each + 2 * q
-            left = jnp.concatenate([dense[at], dense[at + 1]], axis=1)
+            left = jnp.concatenate([dense[start + 2 * q], dense[start + 2 * q + 1]], axis=1)
             right = feats[pl.ds(pl.multiple_of(q * 256, 256), 256), :]
             return acc + jnp.dot(left, right, preferred_element_type=jnp.float32)
 
@@ -144,37 +144,63 @@
                 acc = two(q, acc)
         else:
             acc = lax.fori_loop(0, each // 2, two, acc)
+    if not last:
+        out[...] = acc
+        return
     nblk = rows // 64
     for p in range(2):
         for r in range(nblk):
             out[pl.ds(r * 64 + p, 32, stride=2), :] = acc[(p * nblk + r) * 32 : (p * nblk + r + 1) * 32]
 
 
-def sum_blocks(dense, pieces):
-    return pl.pallas_call(
-        sum_kernel,
+def sum_blocks(dense, operands, places, last):
+    return pl.pallas_call(
+        functools.partial(sum_kernel, places, last),
         out_shape=jax.ShapeDtypeStruct((dense.shape[1], 128), jnp.float32),
-        in_specs=[VMEM] * (1 + len(pieces)),
+        in_specs=[VMEM] * (1 + len(operands)),
         out_specs=VMEM,
         compiler_params=limit(dense.shape[0]),
         name="block_sum",
-    )(dense, *pieces)
+    )(dense, *operands)
+
+
+def turn_kernel(mine, other, turned):
+    first = lax.axis_index("rep") == 0
+    half = mine.shape[0]
+    here, there = mine[...].astype(jnp.float32).T, other[...].astype(jnp.float32).T
+    turned[:, :half] = jnp.where(first, here, there).astype(turned.dtype)
+    turned[:, half:] = jnp.where(first, there, here).astype(turned.dtype)
+
+
+def turn(mine, other):
+    half, wide = mine.shape
+    return pl.pallas_call(
+        turn_kernel,
+        out_shape=jax.ShapeDtypeStruct((wide, 2 * half), mine.dtype),
+        in_specs=[VMEM, VMEM],
+        out_specs=VMEM,
+        compiler_params=limit(16),
+        name="turn",
+    )(mine, other)
 
 
 NT = (((1,), (1,)), ((), ()))
 
 
-def layer_kernel(mine, other, weight_t, bias_t, cot_mine, cot_other, parts):
-    first = lax.axis_index("rep") == 0
+def layer_kernel(mine, other, weight, bias, weight_t, bias_t, cot_t, parts, act):
     owners, chunk, _ = parts.shape
     share = weight_t.shape[0] // owners
     aggregated = (mine[...] + other[...]).astype(jnp.bfloat16)
     pre = lax.dot_general(weight_t[...], aggregated, NT, preferred_element_type=jnp.float32)
     pre = pre + jnp.concatenate([bias_t[...]] * (pre.shape[1] // 128), axis=1)
     sig = 1.0 / (1.0 + jnp.exp(-pre))
-    cot_a, cot_b = cot_mine[...].astype(jnp.float32), cot_other[...].astype(jnp.float32)
-    cot = jnp.concatenate([jnp.where(first, cot_a, cot_b), jnp.where(first, cot_b, cot_a)], axis=1)
+    cot = cot_t[...].astype(jnp.float32)
     delta = (cot * sig * (1.0 + pre * (1.0 - sig))).astype(jnp.bfloat16)
+    half = act.shape[0]
+    own = pl.ds(pl.multiple_of(lax.axis_index("rep") * half, half), half)
+    nodes = (mine[own, :] + other[own, :]).astype(jnp.bfloat16)
+    value = jnp.dot(nodes, weight[...], preferred_element_type=jnp.float32) + bias[...]
+    act[...] = (value / (1.0 + jnp.exp(-value))).astype(act.dtype)
     grad = jnp.dot(delta, aggregated, preferred_element_type=jnp.float32)
     ones = jnp.ones((16, delta.shape[1]), jnp.bfloat16)
     total = lax.dot_general(ones, delta, NT, preferred_element_type=jnp.float32)[:1]
@@ -184,25 +210,24 @@
         parts[r] = jnp.concatenate([grad[r * share : (r + 1) * share], tail], axis=0).astype(parts.dtype)
 
 
-def layer(mine, other, weight_t, bias_t, cot_mine, cot_other, owners):
+def layer(mine, other, weight, bias, weight_t, bias_t, cot_t, owners):
     share = weight_t.shape[0] // owners
     chunk = -(-(share + 2) // 16) * 16
     return pl.pallas_call(
         layer_kernel,
-        out_shape=jax.ShapeDtypeStruct((owners, chunk, 128), jnp.bfloat16),
-        in_specs=[VMEM] * 6,
-        out_specs=VMEM,
+        out_shape=(
+            jax.ShapeDtypeStruct((owners, chunk, 128), jnp.bfloat16),
+            jax.ShapeDtypeStruct((mine.shape[0] // 2, weight.shape[1]), jnp.bfloat16),
+        ),
+        in_specs=[VMEM] * 7,
+        out_specs=(VMEM, VMEM),
         compiler_params=limit(owners),
         name="layer",
-    )(mine, other, weight_t, bias_t, cot_mine, cot_other)
-
-
-def finish_kernel(mine, other, weight, bias, got, act, weight_grad, bias_grad):
-    half = act.shape[0]
-    own = pl.ds(pl.multiple_of(lax.axis_index("rep") * half, half), half)
-    aggregated = (mine[own, :] + other[own, :]).astype(jnp.bfloat16)
-    pre = jnp.dot(aggregated, weight[...], preferred_element_type=jnp.float32) + bias[...]
-    act[...] = (pre / (1.0 + jnp.exp(-pre))).astype(act.dtype)
+    )(mine, other, weight, bias, weight_t, bias_t, cot_t)
+
+
+def finish_kernel(act_in, got, act, weight_grad, bias_grad):
+    act[...] = act_in[...]
     share = weight_grad.shape[0]
     total = jnp.sum(got[...].astype(jnp.float32), axis=0)
     weight_grad[...] = total[:share]
@@ -212,21 +237,21 @@
     bias_grad[...] = flat[:1, :share]
 
 
-def finish(mine, other, weight, bias, got):
+def finish(act, got):
     owners = got.shape[0]
-    share = weight.shape[1] // owners
+    share = act.shape[1] // owners
     return pl.pallas_call(
         finish_kernel,
         out_shape=(
-            jax.ShapeDtypeStruct((mine.shape[0] // 2, weight.shape[1]), jnp.bfloat16),
+            jax.ShapeDtypeStruct(act.shape, act.dtype),
             jax.ShapeDtypeStruct((share, 128), jnp.float32),
             jax.ShapeDtypeStruct((1, share), jnp.float32),
         ),
-        in_specs=[VMEM] * 5,
+        in_specs=[VMEM] * 2,
         out_specs=(VMEM,) * 3,
         compiler_params=limit(owners),
         name="finish",
-    )(mine, other, weight, bias, got)
+    )(act, got)
 
 
 def body(features, weight, bias, block_count, block_cols, block_vals, cotangent):
@@ -241,22 +266,23 @@
     pieces = [keep] + [across(value, s << shift, owners, 0) for s, value in sent]
     vals = block_vals[0]
     for shift, radix in groups[1:]:
-        held, vals = lax.optimization_barrier((jnp.concatenate(pieces), vals))
+        held, vals, cotangent = lax.optimization_barrier((jnp.concatenate(pieces), vals, cotangent))
         sent = zip(range(1, radix), copies(held, radix - 1))
         pieces = [held] + [across(value, s << shift, owners, 0) for s, value in sent]
 
     bias = bias.reshape(1, -1)
-    dense, cot_mine, weight_t, bias_t = place_blocks(
-        block_count, block_cols[0], vals, cotangent, weight, bias, owners
-    )
-    cot_other = across(cot_mine, 0, owners, 1)
-    dense, cot_other = lax.optimization_barrier((dense, cot_other))
-
-    mine = sum_blocks(dense, pieces)
+    dense, weight_t, bias_t = place_blocks(block_count, block_cols[0], vals, weight, bias, owners)
+    cot_t = turn(cotangent, across(cotangent, 0, owners, 1))
+    dense, cot_t = lax.optimization_barrier((dense, cot_t))
+    each = pieces[0].shape[0] // 128
+    places = [s * each for s in range(len(pieces))]
+    early = sum_blocks(dense, [pieces[s] for s in (0, len(pieces) - 1)], [places[s] for s in (0, len(pieces) - 1)], False)
+    late = [s for s in range(len(pieces)) if s not in (0, len(pieces) - 1)]
+    mine = sum_blocks(dense, [early] + [pieces[s] for s in late], [places[s] for s in late], True)
     other = across(mine, 0, owners, 1)
-    parts = layer(mine, other, weight_t, bias_t, cot_mine, cot_other, owners)
+    parts, activated = layer(mine, other, weight, bias, weight_t, bias_t, cot_t, owners)
     got = lax.all_to_all(parts, "rows", split_axis=0, concat_axis=0, tiled=True)
-    activated, weight_grad, bias_grad = finish(mine, other, weight, bias, got)
+    activated, weight_grad, bias_grad = finish(activated, got)
     return activated, weight_grad.T, bias_grad.reshape(-1)
 
 

time: 34.7 us -> 34.4 us (level)
  waiting for transfers between devices: 7.93 us -> 7.58 us
    ppermute x8, waiting for transfers between devices: 7.93 us -> 7.58 us  [across(): return lax.ppermute(value, BOTH, pairs)]
    pallas_call x3 -> x5, Pallas kernels: 1.65 us -> 1.75 us  [the longest x1 0.65 us: finish(): pl.pallas_call(finish_kernel, out_shape=(jax.ShapeDtypeStruct(act.shape,...]
  transfers between devices with their start and end apart: 8 -> 8, of which waited for: 6 -> 5; matrix products, arithmetic and copies ran while one was open for 0% -> 0% of each run, Pallas kernels for 4% -> 5%
where the time goes in v8:
time: 34.4 us; the launch traced here: 34.2 us
  blocking collectives  11.8 us (34%)
  starting transfers between devices  9.38 us (27%)
  waiting for transfers between devices  7.58 us (22%)
  Pallas kernels  3.14 us (9%)
  local copies, waits for them, and re-layouts  1.5 us (4%)
  between operations  0.79 us (2%)
    all_to_all x1, blocking collectives, body(): got = lax.all_to_all(parts, 'rows', split_axis=0, concat_axis=0, tiled=True)  11.8 us
    ppermute x8, starting transfers between devices, across(): return lax.ppermute(value, BOTH, pairs)  9.38 us
    ppermute x8, waiting for transfers between devices, across(): return lax.ppermute(value, BOTH, pairs)  7.58 us
    unnamed x14, local copies, waits for them, and re-layouts  1.49 us
    pallas_call x1, Pallas kernels, place_blocks(): pl.pallas_call(functools.partial(place_kernel, digit_groups(owners)), out...  1.36 us
  transfers between devices with their start and end apart: 8, of which 5 were waited for; matrix products, arithmetic and copies ran while one was open for 0% of the time, Pallas kernels for 5%

profile of v8, /device:TPU:0, one launch (start us, length us, event | category | flops | bytes accessed | tf_op | source)
XLA Modules:
  0.0 34.2 jit_solution(5577373261190572260)
XLA Ops:
  0.6 0.0 copy-start
  0.6 0.0 copy-start.1
  0.7 0.8 %copy-done = bf16[256,128]{1,0:T(8,128)(2,1)S(1)} copy-done((bf16[256,128]{1,0:T(8,128)(2,1)S(1)}, bf16[256,128]{1,0:T(8,128)(2,1)}, u32[]{:S(2)}) %copy-start) | copy-done | bytes 65560
  1.5 5.1 %collective-permute-start.2 = (bf16[128,128]{1,0:T(8,128)(2,1)S(1)}, bf16[128,128]{1,0:T(8,128)(2,1)S(1)}, u32[]{:S(2)}, u32[]{:S(2)}) collective-permute-start(bf16[128,128]{1,0:T(8,128)(2,1)S(1)} %copy.15), channel_id=1, source_target_pairs={{0,24},{1,25},{2,26},{3,27},{4,28},{5,29},{6,30},{7,31},{8,16},{9,... | collective-permute-start | bytes 98312 | tf_op jit(solution)/shard_map/ppermute | solution.py:29
  6.6 0.0 collective-permute-start.1
  6.6 0.6 %collective-permute-start = (bf16[128,128]{1,0:T(8,128)(2,1)S(1)}, bf16[128,128]{1,0:T(8,128)(2,1)S(1)}, u32[]{:S(2)}, u32[]{:S(2)}) collective-permute-start(bf16[128,128]{1,0:T(8,128)(2,1)S(1)} %constant_dynamic-slice_fusion.value), channel_id=1, source_target_pairs={{0,8},{1,9},{2,10},{3,11},{4,12},{5,13},{6,14},{7,15},{8,0},{9,1},... | collective-permute-start | bytes 98312 | tf_op jit(solution)/shard_map/ppermute | solution.py:29
  7.2 1.3 %collective-permute-done.2 = bf16[128,128]{1,0:T(8,128)(2,1)S(1)} collective-permute-done((bf16[128,128]{1,0:T(8,128)(2,1)S(1)}, bf16[128,128]{1,0:T(8,128)(2,1)S(1)}, u32[]{:S(2)}, u32[]{:S(2)}) %collective-permute-start.2) | collective-permute-done | bytes 32800 | tf_op jit(solution)/shard_map/ppermute | solution.py:29
  8.5 2.9 %collective-permute-done.1 = bf16[128,128]{1,0:T(8,128)(2,1)S(1)} collective-permute-done((bf16[128,128]{1,0:T(8,128)(2,1)S(1)}, bf16[128,128]{1,0:T(8,128)(2,1)S(1)}, u32[]{:S(2)}, u32[]{:S(2)}) %collective-permute-start.1) | collective-permute-done | bytes 32800 | tf_op jit(solution)/shard_map/ppermute | solution.py:29
  11.4 0.0 collective-permute-done
  11.5 0.0 copy-start.3
  11.5 0.0 copy-start.2
  11.5 0.0 copy-start.5
  11.5 2.5 %collective-permute-start.4 = (bf16[512,128]{1,0:T(8,128)(2,1)S(1)}, bf16[512,128]{1,0:T(8,128)(2,1)S(1)}, u32[]{:S(2)}, u32[]{:S(2)}) collective-permute-start(bf16[512,128]{1,0:T(8,128)(2,1)S(1)} %copy.17), channel_id=1, source_target_pairs={{0,6},{1,7},{2,4},{3,5},{4,2},{5,3},{6,0},{7,1},{8,14},{9,15},{10,... | collective-permute-start | bytes 393224 | tf_op jit(solution)/shard_map/ppermute | solution.py:29
  14.0 0.5 %collective-permute-start.6 = (bf16[512,128]{1,0:T(8,128)(2,1)S(1)}, bf16[512,128]{1,0:T(8,128)(2,1)S(1)}, u32[]{:S(2)}, u32[]{:S(2)}) collective-permute-start(bf16[512,128]{1,0:T(8,128)(2,1)S(1)} %copy.16.value), channel_id=1, source_target_pairs={{0,4},{1,5},{2,6},{3,7},{4,0},{5,1},{6,2},{7,3},{8,12},{9,13},{10,... | collective-permute-start | bytes 393224 | tf_op jit(solution)/shard_map/ppermute | solution.py:29
  14.5 0.5 %collective-permute-start.5 = (bf16[512,128]{1,0:T(8,128)(2,1)S(1)}, bf16[512,128]{1,0:T(8,128)(2,1)S(1)}, u32[]{:S(2)}, u32[]{:S(2)}) collective-permute-start(bf16[512,128]{1,0:T(8,128)(2,1)S(1)} %pad_maximum_fusion.value.refs_0_), channel_id=1, source_target_pairs={{0,2},{1,3},{2,0},{3,1},{4,6},{5,7},{6,4},{7,5},{8,10},{9,11},{10,... | collective-permute-start | bytes 393224 | tf_op jit(solution)/shard_map/ppermute | solution.py:29
  15.1 0.0 copy-done.3
  15.1 0.0 collective-permute-start.3
  15.1 0.0 copy-start.4
  15.1 0.0 copy-start.6
  15.1 0.0 copy-done.1
  15.1 0.0 copy-done.2
  15.1 0.0 copy-done.5
  15.1 0.6 %copy-done.4 = f32[256]{0:T(256)S(1)} copy-done((f32[256]{0:T(256)S(1)}, f32[256]{0:T(256)}, u32[]{:S(2)}) %copy-start.4) | copy-done | bytes 1048
  15.8 0.0 copy-done.6
  15.8 1.4 %place.1 = (bf16[16,256,128]{2,1,0:T(8,128)(2,1)S(1)}, bf16[256,128]{1,0:T(8,128)(2,1)S(1)}, f32[256,128]{1,0:T(8,128)S(1)}) custom-call(s32[1,4]{1,0:T(1,128)S(1)} %copy-done.6, s32[4,16]{1,0:T(4,128)S(1)} %bitcast.8, bf16[4,16,4096]{2,1,0:T(8,128)(2,1)S(1)} %bitcast.5, bf16[128,256]{1,0:T(8,128)(2,1)S(1)} %copy-done.2, f32[1,256]{1,0:T(1,128)S(1)} %bitcast.6), custom_call_target="tpu_custom_call" | custom-call | tf_op jit(solution)/shard_map/place/pallas_call | solution.py:113
  17.1 0.0 collective-permute-done.3.other
  17.1 0.1 turn.1.cot_t
  17.2 1.6 %collective-permute-done.4.refs_1_ = bf16[512,128]{1,0:T(8,128)(2,1)S(1)} collective-permute-done((bf16[512,128]{1,0:T(8,128)(2,1)S(1)}, bf16[512,128]{1,0:T(8,128)(2,1)S(1)}, u32[]{:S(2)}, u32[]{:S(2)}) %collective-permute-start.4) | collective-permute-done | bytes 131104 | tf_op jit(solution)/shard_map/ppermute | solution.py:29
  18.8 0.3 block_sum.2.refs_0_
  19.1 0.5 %collective-permute-done.6.refs_2_ = bf16[512,128]{1,0:T(8,128)(2,1)S(1)} collective-permute-done((bf16[512,128]{1,0:T(8,128)(2,1)S(1)}, bf16[512,128]{1,0:T(8,128)(2,1)S(1)}, u32[]{:S(2)}, u32[]{:S(2)}) %collective-permute-start.6) | collective-permute-done | bytes 131104 | tf_op jit(solution)/shard_map/ppermute | solution.py:29
  19.6 0.0 collective-permute-done.5.refs_1_
  19.6 0.3 block_sum.3.mine
  19.9 0.1 collective-permute-start.7
  20.0 1.3 %collective-permute-done.7.other = f32[256,128]{1,0:T(8,128)S(1)} collective-permute-done((f32[256,128]{1,0:T(8,128)S(1)}, f32[256,128]{1,0:T(8,128)S(1)}, u32[]{:S(2)}, u32[]{:S(2)}) %collective-permute-start.7) | collective-permute-done | bytes 131104 | tf_op jit(solution)/shard_map/ppermute | solution.py:29
  21.3 0.4 %layer.1 = (bf16[16,32,128]{2,1,0:T(8,128)(2,1)S(1)}, bf16[128,256]{1,0:T(8,128)(2,1)S(1)}) custom-call(f32[256,128]{1,0:T(8,128)S(1)} %block_sum.3.mine, f32[256,128]{1,0:T(8,128)S(1)} %collective-permute-done.7.other, bf16[128,256]{1,0:T(8,128)(2,1)S(1)} %copy-done.2, f32[1,256]{1,0:T(1,128)S(1)} %bitcast.7, ...), custom_call_target="tpu_custom_call" | custom-call | tf_op jit(solution)/shard_map/layer/pallas_call | solution.py:216
  21.8 11.8 %all_to_all.5.got = bf16[16,32,128]{2,1,0:T(8,128)(2,1)S(1)} all-to-all(bf16[16,32,128]{2,1,0:T(8,128)(2,1)S(1)} %get-tuple-element.25), channel_id=1, replica_groups=mesh['rows'=16,'rep'=2] {'rows'}, dimensions={0} | all-to-all | bytes 262144 | tf_op jit(solution)/shard_map/all_to_all | solution.py:284
  33.6 0.6 %finish.1 = (bf16[128,256]{1,0:T(8,128)(2,1)}, f32[16,128]{1,0:T(8,128)}, f32[1,16]{1,0:T(1,128)}) custom-call(bf16[128,256]{1,0:T(8,128)(2,1)S(1)} %get-tuple-element.24.act_in, bf16[16,32,128]{2,1,0:T(8,128)(2,1)S(1)} %all_to_all.5.got), custom_call_target="tpu_custom_call" | custom-call | tf_op jit(solution)/shard_map/finish/pallas_call | solution.py:243
  (6 shorter events, 0.0 us)
Async XLA Ops:
  0.6 0.8 %copy-start = (bf16[256,128]{1,0:T(8,128)(2,1)S(1)}, bf16[256,128]{1,0:T(8,128)(2,1)}, u32[]{:S(2)}) copy-start(bf16[256,128]{1,0:T(8,128)(2,1)} %param.7) | copy-start | bytes 196612
  0.6 14.4 %copy-start.1 = (bf16[1,4,16,4096]{3,2,1,0:T(8,128)(2,1)S(1)}, bf16[1,4,16,4096]{3,2,1,0:T(8,128)(2,1)}, u32[]{:S(2)}) copy-start(bf16[1,4,16,4096]{3,2,1,0:T(8,128)(2,1)} %param.12) | copy-start | bytes 1572868
  1.5 7.0 %collective-permute-start.2 = (bf16[128,128]{1,0:T(8,128)(2,1)S(1)}, bf16[128,128]{1,0:T(8,128)(2,1)S(1)}, u32[]{:S(2)}, u32[]{:S(2)}) collective-permute-start(bf16[128,128]{1,0:T(8,128)(2,1)S(1)} %copy.15), channel_id=1, source_target_pairs={{0,24},{1,25},{2,26},{3,27},{4,28},{5,29},{6,30},{7,31},{8,16},{9,... | collective-permute-start | bytes 98312 | tf_op jit(solution)/shard_map/ppermute | solution.py:29
  6.6 4.8 %collective-permute-start.1 = (bf16[128,128]{1,0:T(8,128)(2,1)S(1)}, bf16[128,128]{1,0:T(8,128)(2,1)S(1)}, u32[]{:S(2)}, u32[]{:S(2)}) collective-permute-start(bf16[128,128]{1,0:T(8,128)(2,1)S(1)} %copy.14.value), channel_id=1, source_target_pairs={{0,16},{1,17},{2,18},{3,19},{4,20},{5,21},{6,22},{7,23},{8,24},{9,... | collective-permute-start | bytes 98312 | tf_op jit(solution)/shard_map/ppermute | solution.py:29
  6.6 4.8 %collective-permute-start = (bf16[128,128]{1,0:T(8,128)(2,1)S(1)}, bf16[128,128]{1,0:T(8,128)(2,1)S(1)}, u32[]{:S(2)}, u32[]{:S(2)}) collective-permute-start(bf16[128,128]{1,0:T(8,128)(2,1)S(1)} %constant_dynamic-slice_fusion.value), channel_id=1, source_target_pairs={{0,8},{1,9},{2,10},{3,11},{4,12},{5,13},{6,14},{7,15},{8,0},{9,1},... | collective-permute-start | bytes 98312 | tf_op jit(solution)/shard_map/ppermute | solution.py:29
  11.5 3.6 %copy-start.3 = (bf16[128,256]{1,0:T(8,128)(2,1)S(1)}, bf16[128,256]{1,0:T(8,128)(2,1)}, u32[]{:S(2)}) copy-start(bf16[128,256]{1,0:T(8,128)(2,1)} %mine) | copy-start | bytes 196612
  11.5 3.6 %copy-start.2 = (bf16[128,256]{1,0:T(8,128)(2,1)S(1)}, bf16[128,256]{1,0:T(8,128)(2,1)}, u32[]{:S(2)}) copy-start(bf16[128,256]{1,0:T(8,128)(2,1)} %weight.3) | copy-start | bytes 196612
  11.5 3.6 %copy-start.5 = (s32[1,4,16]{2,1,0:T(4,128)S(1)}, s32[1,4,16]{2,1,0:T(4,128)}, u32[]{:S(2)}) copy-start(s32[1,4,16]{2,1,0:T(4,128)} %param.11) | copy-start | bytes 772
  11.5 7.3 %collective-permute-start.4 = (bf16[512,128]{1,0:T(8,128)(2,1)S(1)}, bf16[512,128]{1,0:T(8,128)(2,1)S(1)}, u32[]{:S(2)}, u32[]{:S(2)}) collective-permute-start(bf16[512,128]{1,0:T(8,128)(2,1)S(1)} %copy.17), channel_id=1, source_target_pairs={{0,6},{1,7},{2,4},{3,5},{4,2},{5,3},{6,0},{7,1},{8,14},{9,15},{10,... | collective-permute-start | bytes 393224 | tf_op jit(solution)/shard_map/ppermute | solution.py:29
  14.0 5.6 %collective-permute-start.6 = (bf16[512,128]{1,0:T(8,128)(2,1)S(1)}, bf16[512,128]{1,0:T(8,128)(2,1)S(1)}, u32[]{:S(2)}, u32[]{:S(2)}) collective-permute-start(bf16[512,128]{1,0:T(8,128)(2,1)S(1)} %copy.16.value), channel_id=1, source_target_pairs={{0,4},{1,5},{2,6},{3,7},{4,0},{5,1},{6,2},{7,3},{8,12},{9,13},{10,... | collective-permute-start | bytes 393224 | tf_op jit(solution)/shard_map/ppermute | solution.py:29
  14.5 5.1 %collective-permute-start.5 = (bf16[512,128]{1,0:T(8,128)(2,1)S(1)}, bf16[512,128]{1,0:T(8,128)(2,1)S(1)}, u32[]{:S(2)}, u32[]{:S(2)}) collective-permute-start(bf16[512,128]{1,0:T(8,128)(2,1)S(1)} %pad_maximum_fusion.value.refs_0_), channel_id=1, source_target_pairs={{0,2},{1,3},{2,0},{3,1},{4,6},{5,7},{6,4},{7,5},{8,10},{9,11},{10,... | collective-permute-start | bytes 393224 | tf_op jit(solution)/shard_map/ppermute | solution.py:29
  15.1 2.1 %collective-permute-start.3 = (bf16[128,256]{1,0:T(8,128)(2,1)S(1)}, bf16[128,256]{1,0:T(8,128)(2,1)S(1)}, u32[]{:S(2)}, u32[]{:S(2)}) collective-permute-start(bf16[128,256]{1,0:T(8,128)(2,1)S(1)} %copy-done.3), channel_id=1, source_target_pairs={{0,1},{1,0},{2,3},{3,2},{4,5},{5,4},{6,7},{7,6},{8,9},{9,8},{10,11... | collective-permute-start | bytes 196616 | tf_op jit(solution)/shard_map/ppermute | solution.py:29
  15.1 0.7 %copy-start.4 = (f32[256]{0:T(256)S(1)}, f32[256]{0:T(256)}, u32[]{:S(2)}) copy-start(f32[256]{0:T(256)} %param.9) | copy-start | bytes 3076
  15.1 0.7 %copy-start.6 = (s32[1,4]{1,0:T(1,128)S(1)}, s32[1,4]{1,0:T(1,128)}, u32[]{:S(2)}) copy-start(s32[1,4]{1,0:T(1,128)} %counts.1) | copy-start | bytes 52
  19.9 1.4 %collective-permute-start.7 = (f32[256,128]{1,0:T(8,128)S(1)}, f32[256,128]{1,0:T(8,128)S(1)}, u32[]{:S(2)}, u32[]{:S(2)}) collective-permute-start(f32[256,128]{1,0:T(8,128)S(1)} %block_sum.3.mine), channel_id=1, source_target_pairs={{0,1},{1,0},{2,3},{3,2},{4,5},{5,4},{6,7},{7,6},{8,9},{9,8},{10,11... | collective-permute-start | bytes 393224 | tf_op jit(solution)/shard_map/ppermute | solution.py:29

commit v9 on v8

--- a/solution.py
+++ b/solution.py
@@ -85,8 +85,10 @@
             for i in range(g * 16, g * 16 + 16):
                 two = vals[r, :, i * 128 : (i + 1) * 128].astype(jnp.float32)
                 turned = pltpu.roll(two, 64, 1)
-                top.append(jnp.concatenate([jnp.where(low, two, 0.0), jnp.where(low, turned, 0.0)], axis=1).astype(jnp.bfloat16))
-                bottom.append(jnp.concatenate([jnp.where(low, 0.0, turned), jnp.where(low, 0.0, two)], axis=1).astype(jnp.bfloat16))
+                both = jnp.concatenate([jnp.where(low, two, 0.0), jnp.where(low, turned, 0.0)], axis=1)
+                top.append(both.astype(jnp.bfloat16))
+                both = jnp.concatenate([jnp.where(low, 0.0, turned), jnp.where(low, 0.0, two)], axis=1)
+                bottom.append(both.astype(jnp.bfloat16))
             rights.append(jnp.concatenate(top + bottom, axis=0))
 
         def put(q):
@@ -144,13 +146,7 @@
                 acc = two(q, acc)
         else:
             acc = lax.fori_loop(0, each // 2, two, acc)
-    if not last:
-        out[...] = acc
-        return
-    nblk = rows // 64
-    for p in range(2):
-        for r in range(nblk):
-            out[pl.ds(r * 64 + p, 32, stride=2), :] = acc[(p * nblk + r) * 32 : (p * nblk + r + 1) * 32]
+    out[...] = acc
 
 
 def sum_blocks(dense, operands, places, last):
@@ -164,12 +160,20 @@
     )(dense, *operands)
 
 
+def node_at(place, nodes):
+    rest = place % (nodes // 2)
+    return rest // 32 * 64 + rest % 32 * 2 + place // (nodes // 2)
+
+
 def turn_kernel(mine, other, turned):
     first = lax.axis_index("rep") == 0
-    half = mine.shape[0]
-    here, there = mine[...].astype(jnp.float32).T, other[...].astype(jnp.float32).T
-    turned[:, :half] = jnp.where(first, here, there).astype(turned.dtype)
-    turned[:, half:] = jnp.where(first, there, here).astype(turned.dtype)
+    here, there = mine[...].astype(jnp.float32), other[...].astype(jnp.float32)
+    both = jnp.concatenate([jnp.where(first, here, there), jnp.where(first, there, here)], axis=0)
+    nodes = both.shape[0]
+    wanted = node_at(lax.broadcasted_iota(jnp.int32, (nodes, nodes), 0), nodes)
+    order = (wanted == lax.broadcasted_iota(jnp.int32, (nodes, nodes), 1)).astype(jnp.bfloat16)
+    both = jnp.dot(order, both.astype(jnp.bfloat16), preferred_element_type=jnp.float32)
+    turned[...] = both.T.astype(turned.dtype)
 
 
 def turn(mine, other):
@@ -197,9 +201,10 @@
     cot = cot_t[...].astype(jnp.float32)
     delta = (cot * sig * (1.0 + pre * (1.0 - sig))).astype(jnp.bfloat16)
     half = act.shape[0]
-    own = pl.ds(pl.multiple_of(lax.axis_index("rep") * half, half), half)
-    nodes = (mine[own, :] + other[own, :]).astype(jnp.bfloat16)
-    value = jnp.dot(nodes, weight[...], preferred_element_type=jnp.float32) + bias[...]
+    own = lax.broadcasted_iota(jnp.int32, (half, 2 * half), 0) + lax.axis_index("rep") * half
+    found = node_at(lax.broadcasted_iota(jnp.int32, (half, 2 * half), 1), 2 * half)
+    nodes = jnp.dot((found == own).astype(jnp.bfloat16), aggregated, preferred_element_type=jnp.float32)
+    value = jnp.dot(nodes.astype(jnp.bfloat16), weight[...], preferred_element_type=jnp.float32) + bias[...]
     act[...] = (value / (1.0 + jnp.exp(-value))).astype(act.dtype)
     grad = jnp.dot(delta, aggregated, preferred_element_type=jnp.float32)
     ones = jnp.ones((16, delta.shape[1]), jnp.bfloat16)
@@ -276,8 +281,9 @@
     dense, cot_t = lax.optimization_barrier((dense, cot_t))
     each = pieces[0].shape[0] // 128
     places = [s * each for s in range(len(pieces))]
-    early = sum_blocks(dense, [pieces[s] for s in (0, len(pieces) - 1)], [places[s] for s in (0, len(pieces) - 1)], False)
-    late = [s for s in range(len(pieces)) if s not in (0, len(pieces) - 1)]
+    ends = (0, len(pieces) - 1)
+    early = sum_blocks(dense, [pieces[s] for s in ends], [places[s] for s in ends], False)
+    late = [s for s in range(len(pieces)) if s not in ends]
     mine = sum_blocks(dense, [early] + [pieces[s] for s in late], [places[s] for s in late], True)
     other = across(mine, 0, owners, 1)
     parts, activated = layer(mine, other, weight, bias, weight_t, bias_t, cot_t, owners)

time: 34.4 us -> 34.4 us (level)
  transfers between devices with their start and end apart: 8 -> 8, of which waited for: 5 -> 5; matrix products, arithmetic and copies ran while one was open for 0% -> 0% of each run, Pallas kernels for 5% -> 6%
where the time goes in v9:
time: 34.4 us; the launch traced here: 34.2 us
  blocking collectives  11.8 us (34%)
  starting transfers between devices  9.38 us (27%)
  waiting for transfers between devices  7.41 us (22%)
  Pallas kernels  3.31 us (10%)
  local copies, waits for them, and re-layouts  1.5 us (4%)
  between operations  0.79 us (2%)
    all_to_all x1, blocking collectives, body(): got = lax.all_to_all(parts, 'rows', split_axis=0, concat_axis=0, tiled=True)  11.8 us
    ppermute x8, starting transfers between devices, across(): return lax.ppermute(value, BOTH, pairs)  9.38 us
    ppermute x8, waiting for transfers between devices, across(): return lax.ppermute(value, BOTH, pairs)  7.41 us
    unnamed x14, local copies, waits for them, and re-layouts  1.49 us
    pallas_call x1, Pallas kernels, place_blocks(): pl.pallas_call(functools.partial(place_kernel, digit_groups(owners)), out...  1.36 us
  transfers between devices with their start and end apart: 8, of which 5 were waited for; matrix products, arithmetic and copies ran while one was open for 0% of the time, Pallas kernels for 6%

profile of v9, /device:TPU:0, one launch (start us, length us, event | category | flops | bytes accessed | tf_op | source)
XLA Modules:
  0.0 34.2 jit_solution(1904160745712171478)
XLA Ops:
  0.6 0.0 copy-start
  0.6 0.0 copy-start.1
  0.7 0.8 %copy-done = bf16[256,128]{1,0:T(8,128)(2,1)S(1)} copy-done((bf16[256,128]{1,0:T(8,128)(2,1)S(1)}, bf16[256,128]{1,0:T(8,128)(2,1)}, u32[]{:S(2)}) %copy-start) | copy-done | bytes 65560
  1.5 5.1 %collective-permute-start.2 = (bf16[128,128]{1,0:T(8,128)(2,1)S(1)}, bf16[128,128]{1,0:T(8,128)(2,1)S(1)}, u32[]{:S(2)}, u32[]{:S(2)}) collective-permute-start(bf16[128,128]{1,0:T(8,128)(2,1)S(1)} %copy.15), channel_id=1, source_target_pairs={{0,24},{1,25},{2,26},{3,27},{4,28},{5,29},{6,30},{7,31},{8,16},{9,... | collective-permute-start | bytes 98312 | tf_op jit(solution)/shard_map/ppermute | solution.py:29
  6.6 0.0 collective-permute-start.1
  6.6 0.6 %collective-permute-start = (bf16[128,128]{1,0:T(8,128)(2,1)S(1)}, bf16[128,128]{1,0:T(8,128)(2,1)S(1)}, u32[]{:S(2)}, u32[]{:S(2)}) collective-permute-start(bf16[128,128]{1,0:T(8,128)(2,1)S(1)} %constant_dynamic-slice_fusion.value), channel_id=1, source_target_pairs={{0,8},{1,9},{2,10},{3,11},{4,12},{5,13},{6,14},{7,15},{8,0},{9,1},... | collective-permute-start | bytes 98312 | tf_op jit(solution)/shard_map/ppermute | solution.py:29
  7.2 1.3 %collective-permute-done.2 = bf16[128,128]{1,0:T(8,128)(2,1)S(1)} collective-permute-done((bf16[128,128]{1,0:T(8,128)(2,1)S(1)}, bf16[128,128]{1,0:T(8,128)(2,1)S(1)}, u32[]{:S(2)}, u32[]{:S(2)}) %collective-permute-start.2) | collective-permute-done | bytes 32800 | tf_op jit(solution)/shard_map/ppermute | solution.py:29
  8.5 2.9 %collective-permute-done.1 = bf16[128,128]{1,0:T(8,128)(2,1)S(1)} collective-permute-done((bf16[128,128]{1,0:T(8,128)(2,1)S(1)}, bf16[128,128]{1,0:T(8,128)(2,1)S(1)}, u32[]{:S(2)}, u32[]{:S(2)}) %collective-permute-start.1) | collective-permute-done | bytes 32800 | tf_op jit(solution)/shard_map/ppermute | solution.py:29
  11.4 0.0 collective-permute-done
  11.5 0.0 copy-start.3
  11.5 0.0 copy-start.2
  11.5 0.0 copy-start.5
  11.5 2.5 %collective-permute-start.4 = (bf16[512,128]{1,0:T(8,128)(2,1)S(1)}, bf16[512,128]{1,0:T(8,128)(2,1)S(1)}, u32[]{:S(2)}, u32[]{:S(2)}) collective-permute-start(bf16[512,128]{1,0:T(8,128)(2,1)S(1)} %copy.17), channel_id=1, source_target_pairs={{0,6},{1,7},{2,4},{3,5},{4,2},{5,3},{6,0},{7,1},{8,14},{9,15},{10,... | collective-permute-start | bytes 393224 | tf_op jit(solution)/shard_map/ppermute | solution.py:29
  14.0 0.5 %collective-permute-start.6 = (bf16[512,128]{1,0:T(8,128)(2,1)S(1)}, bf16[512,128]{1,0:T(8,128)(2,1)S(1)}, u32[]{:S(2)}, u32[]{:S(2)}) collective-permute-start(bf16[512,128]{1,0:T(8,128)(2,1)S(1)} %copy.16.value), channel_id=1, source_target_pairs={{0,4},{1,5},{2,6},{3,7},{4,0},{5,1},{6,2},{7,3},{8,12},{9,13},{10,... | collective-permute-start | bytes 393224 | tf_op jit(solution)/shard_map/ppermute | solution.py:29
  14.5 0.5 %collective-permute-start.5 = (bf16[512,128]{1,0:T(8,128)(2,1)S(1)}, bf16[512,128]{1,0:T(8,128)(2,1)S(1)}, u32[]{:S(2)}, u32[]{:S(2)}) collective-permute-start(bf16[512,128]{1,0:T(8,128)(2,1)S(1)} %pad_maximum_fusion.value.refs_0_), channel_id=1, source_target_pairs={{0,2},{1,3},{2,0},{3,1},{4,6},{5,7},{6,4},{7,5},{8,10},{9,11},{10,... | collective-permute-start | bytes 393224 | tf_op jit(solution)/shard_map/ppermute | solution.py:29
  15.1 0.0 copy-done.3
  15.1 0.0 collective-permute-start.3
  15.1 0.0 copy-start.4
  15.1 0.0 copy-start.6
  15.1 0.0 copy-done.1
  15.1 0.0 copy-done.2
  15.1 0.0 copy-done.5
  15.1 0.6 %copy-done.4 = f32[256]{0:T(256)S(1)} copy-done((f32[256]{0:T(256)S(1)}, f32[256]{0:T(256)}, u32[]{:S(2)}) %copy-start.4) | copy-done | bytes 1048
  15.8 0.0 copy-done.6
  15.8 1.4 %place.1 = (bf16[16,256,128]{2,1,0:T(8,128)(2,1)S(1)}, bf16[256,128]{1,0:T(8,128)(2,1)S(1)}, f32[256,128]{1,0:T(8,128)S(1)}) custom-call(s32[1,4]{1,0:T(1,128)S(1)} %copy-done.6, s32[4,16]{1,0:T(4,128)S(1)} %bitcast.8, bf16[4,16,4096]{2,1,0:T(8,128)(2,1)S(1)} %bitcast.5, bf16[128,256]{1,0:T(8,128)(2,1)S(1)} %copy-done.2, f32[1,256]{1,0:T(1,128)S(1)} %bitcast.6), custom_call_target="tpu_custom_call" | custom-call | tf_op jit(solution)/shard_map/place/pallas_call | solution.py:115
  17.1 0.0 collective-permute-done.3.other
  17.1 0.3 turn.1.cot_t
  17.4 1.4 %collective-permute-done.4.refs_1_ = bf16[512,128]{1,0:T(8,128)(2,1)S(1)} collective-permute-done((bf16[512,128]{1,0:T(8,128)(2,1)S(1)}, bf16[512,128]{1,0:T(8,128)(2,1)S(1)}, u32[]{:S(2)}, u32[]{:S(2)}) %collective-permute-start.4) | collective-permute-done | bytes 131104 | tf_op jit(solution)/shard_map/ppermute | solution.py:29
  18.8 0.3 block_sum.2.refs_0_
  19.1 0.5 %collective-permute-done.6.refs_2_ = bf16[512,128]{1,0:T(8,128)(2,1)S(1)} collective-permute-done((bf16[512,128]{1,0:T(8,128)(2,1)S(1)}, bf16[512,128]{1,0:T(8,128)(2,1)S(1)}, u32[]{:S(2)}, u32[]{:S(2)}) %collective-permute-start.6) | collective-permute-done | bytes 131104 | tf_op jit(solution)/shard_map/ppermute | solution.py:29
  19.6 0.0 collective-permute-done.5.refs_1_
  19.6 0.3 block_sum.3.mine
  19.9 0.1 collective-permute-start.7
  20.0 1.3 %collective-permute-done.7.other = f32[256,128]{1,0:T(8,128)S(1)} collective-permute-done((f32[256,128]{1,0:T(8,128)S(1)}, f32[256,128]{1,0:T(8,128)S(1)}, u32[]{:S(2)}, u32[]{:S(2)}) %collective-permute-start.7) | collective-permute-done | bytes 131104 | tf_op jit(solution)/shard_map/ppermute | solution.py:29
  21.3 0.4 %layer.1 = (bf16[16,32,128]{2,1,0:T(8,128)(2,1)S(1)}, bf16[128,256]{1,0:T(8,128)(2,1)S(1)}) custom-call(f32[256,128]{1,0:T(8,128)S(1)} %block_sum.3.mine, f32[256,128]{1,0:T(8,128)S(1)} %collective-permute-done.7.other, bf16[128,256]{1,0:T(8,128)(2,1)S(1)} %copy-done.2, f32[1,256]{1,0:T(1,128)S(1)} %bitcast.7, ...), custom_call_target="tpu_custom_call" | custom-call | tf_op jit(solution)/shard_map/layer/pallas_call | solution.py:221
  21.7 11.8 %all_to_all.5.got = bf16[16,32,128]{2,1,0:T(8,128)(2,1)S(1)} all-to-all(bf16[16,32,128]{2,1,0:T(8,128)(2,1)S(1)} %get-tuple-element.25), channel_id=1, replica_groups=mesh['rows'=16,'rep'=2] {'rows'}, dimensions={0} | all-to-all | bytes 262144 | tf_op jit(solution)/shard_map/all_to_all | solution.py:290
  33.6 0.6 %finish.1 = (bf16[128,256]{1,0:T(8,128)(2,1)}, f32[16,128]{1,0:T(8,128)}, f32[1,16]{1,0:T(1,128)}) custom-call(bf16[128,256]{1,0:T(8,128)(2,1)S(1)} %get-tuple-element.24.act_in, bf16[16,32,128]{2,1,0:T(8,128)(2,1)S(1)} %all_to_all.5.got), custom_call_target="tpu_custom_call" | custom-call | tf_op jit(solution)/shard_map/finish/pallas_call | solution.py:248
  (6 shorter events, 0.0 us)
Async XLA Ops:
  0.6 0.8 %copy-start = (bf16[256,128]{1,0:T(8,128)(2,1)S(1)}, bf16[256,128]{1,0:T(8,128)(2,1)}, u32[]{:S(2)}) copy-start(bf16[256,128]{1,0:T(8,128)(2,1)} %param.7) | copy-start | bytes 196612
  0.6 14.4 %copy-start.1 = (bf16[1,4,16,4096]{3,2,1,0:T(8,128)(2,1)S(1)}, bf16[1,4,16,4096]{3,2,1,0:T(8,128)(2,1)}, u32[]{:S(2)}) copy-start(bf16[1,4,16,4096]{3,2,1,0:T(8,128)(2,1)} %param.12) | copy-start | bytes 1572868
  1.5 7.0 %collective-permute-start.2 = (bf16[128,128]{1,0:T(8,128)(2,1)S(1)}, bf16[128,128]{1,0:T(8,128)(2,1)S(1)}, u32[]{:S(2)}, u32[]{:S(2)}) collective-permute-start(bf16[128,128]{1,0:T(8,128)(2,1)S(1)} %copy.15), channel_id=1, source_target_pairs={{0,24},{1,25},{2,26},{3,27},{4,28},{5,29},{6,30},{7,31},{8,16},{9,... | collective-permute-start | bytes 98312 | tf_op jit(solution)/shard_map/ppermute | solution.py:29
  6.6 4.8 %collective-permute-start.1 = (bf16[128,128]{1,0:T(8,128)(2,1)S(1)}, bf16[128,128]{1,0:T(8,128)(2,1)S(1)}, u32[]{:S(2)}, u32[]{:S(2)}) collective-permute-start(bf16[128,128]{1,0:T(8,128)(2,1)S(1)} %copy.14.value), channel_id=1, source_target_pairs={{0,16},{1,17},{2,18},{3,19},{4,20},{5,21},{6,22},{7,23},{8,24},{9,... | collective-permute-start | bytes 98312 | tf_op jit(solution)/shard_map/ppermute | solution.py:29
  6.6 4.8 %collective-permute-start = (bf16[128,128]{1,0:T(8,128)(2,1)S(1)}, bf16[128,128]{1,0:T(8,128)(2,1)S(1)}, u32[]{:S(2)}, u32[]{:S(2)}) collective-permute-start(bf16[128,128]{1,0:T(8,128)(2,1)S(1)} %constant_dynamic-slice_fusion.value), channel_id=1, source_target_pairs={{0,8},{1,9},{2,10},{3,11},{4,12},{5,13},{6,14},{7,15},{8,0},{9,1},... | collective-permute-start | bytes 98312 | tf_op jit(solution)/shard_map/ppermute | solution.py:29
  11.5 3.6 %copy-start.3 = (bf16[128,256]{1,0:T(8,128)(2,1)S(1)}, bf16[128,256]{1,0:T(8,128)(2,1)}, u32[]{:S(2)}) copy-start(bf16[128,256]{1,0:T(8,128)(2,1)} %mine) | copy-start | bytes 196612
  11.5 3.6 %copy-start.2 = (bf16[128,256]{1,0:T(8,128)(2,1)S(1)}, bf16[128,256]{1,0:T(8,128)(2,1)}, u32[]{:S(2)}) copy-start(bf16[128,256]{1,0:T(8,128)(2,1)} %weight.3) | copy-start | bytes 196612
  11.5 3.6 %copy-start.5 = (s32[1,4,16]{2,1,0:T(4,128)S(1)}, s32[1,4,16]{2,1,0:T(4,128)}, u32[]{:S(2)}) copy-start(s32[1,4,16]{2,1,0:T(4,128)} %param.11) | copy-start | bytes 772
  11.5 7.3 %collective-permute-start.4 = (bf16[512,128]{1,0:T(8,128)(2,1)S(1)}, bf16[512,128]{1,0:T(8,128)(2,1)S(1)}, u32[]{:S(2)}, u32[]{:S(2)}) collective-permute-start(bf16[512,128]{1,0:T(8,128)(2,1)S(1)} %copy.17), channel_id=1, source_target_pairs={{0,6},{1,7},{2,4},{3,5},{4,2},{5,3},{6,0},{7,1},{8,14},{9,15},{10,... | collective-permute-start | bytes 393224 | tf_op jit(solution)/shard_map/ppermute | solution.py:29
  14.0 5.6 %collective-permute-start.6 = (bf16[512,128]{1,0:T(8,128)(2,1)S(1)}, bf16[512,128]{1,0:T(8,128)(2,1)S(1)}, u32[]{:S(2)}, u32[]{:S(2)}) collective-permute-start(bf16[512,128]{1,0:T(8,128)(2,1)S(1)} %copy.16.value), channel_id=1, source_target_pairs={{0,4},{1,5},{2,6},{3,7},{4,0},{5,1},{6,2},{7,3},{8,12},{9,13},{10,... | collective-permute-start | bytes 393224 | tf_op jit(solution)/shard_map/ppermute | solution.py:29
  14.5 5.1 %collective-permute-start.5 = (bf16[512,128]{1,0:T(8,128)(2,1)S(1)}, bf16[512,128]{1,0:T(8,128)(2,1)S(1)}, u32[]{:S(2)}, u32[]{:S(2)}) collective-permute-start(bf16[512,128]{1,0:T(8,128)(2,1)S(1)} %pad_maximum_fusion.value.refs_0_), channel_id=1, source_target_pairs={{0,2},{1,3},{2,0},{3,1},{4,6},{5,7},{6,4},{7,5},{8,10},{9,11},{10,... | collective-permute-start | bytes 393224 | tf_op jit(solution)/shard_map/ppermute | solution.py:29
  15.1 2.1 %collective-permute-start.3 = (bf16[128,256]{1,0:T(8,128)(2,1)S(1)}, bf16[128,256]{1,0:T(8,128)(2,1)S(1)}, u32[]{:S(2)}, u32[]{:S(2)}) collective-permute-start(bf16[128,256]{1,0:T(8,128)(2,1)S(1)} %copy-done.3), channel_id=1, source_target_pairs={{0,1},{1,0},{2,3},{3,2},{4,5},{5,4},{6,7},{7,6},{8,9},{9,8},{10,11... | collective-permute-start | bytes 196616 | tf_op jit(solution)/shard_map/ppermute | solution.py:29
  15.1 0.7 %copy-start.4 = (f32[256]{0:T(256)S(1)}, f32[256]{0:T(256)}, u32[]{:S(2)}) copy-start(f32[256]{0:T(256)} %param.9) | copy-start | bytes 3076
  15.1 0.7 %copy-start.6 = (s32[1,4]{1,0:T(1,128)S(1)}, s32[1,4]{1,0:T(1,128)}, u32[]{:S(2)}) copy-start(s32[1,4]{1,0:T(1,128)} %counts.1) | copy-start | bytes 52
  19.9 1.4 %collective-permute-start.7 = (f32[256,128]{1,0:T(8,128)S(1)}, f32[256,128]{1,0:T(8,128)S(1)}, u32[]{:S(2)}, u32[]{:S(2)}) collective-permute-start(f32[256,128]{1,0:T(8,128)S(1)} %block_sum.3.mine), channel_id=1, source_target_pairs={{0,1},{1,0},{2,3},{3,2},{4,5},{5,4},{6,7},{7,6},{8,9},{9,8},{10,11... | collective-permute-start | bytes 393224 | tf_op jit(solution)/shard_map/ppermute | solution.py:29

commit v10 on v9

--- a/solution.py
+++ b/solution.py
@@ -231,8 +231,9 @@
     )(mine, other, weight, bias, weight_t, bias_t, cot_t)
 
 
-def finish_kernel(act_in, got, act, weight_grad, bias_grad):
-    act[...] = act_in[...]
+def finish_kernel(act_in, got, act, weight_grad, bias_grad, sem):
+    copy = pltpu.make_async_copy(act_in, act, sem)
+    copy.start()
     share = weight_grad.shape[0]
     total = jnp.sum(got[...].astype(jnp.float32), axis=0)
     weight_grad[...] = total[:share]
@@ -240,6 +241,7 @@
     flat = jnp.broadcast_to(flat, (8, 256))
     flat = pltpu.roll(flat, lax.rem(256 - lax.axis_index("rows") * share, 256), 1)
     bias_grad[...] = flat[:1, :share]
+    copy.wait()
 
 
 def finish(act, got):
@@ -253,7 +255,8 @@
             jax.ShapeDtypeStruct((1, share), jnp.float32),
         ),
         in_specs=[VMEM] * 2,
-        out_specs=(VMEM,) * 3,
+        out_specs=(pl.BlockSpec(memory_space=pltpu.HBM), VMEM, VMEM),
+        scratch_shapes=[pltpu.SemaphoreType.DMA],
         compiler_params=limit(owners),
         name="finish",
     )(act, got)

time: 34.4 us -> 35 us (1.017)
  Pallas kernels: 3.31 us -> 3.92 us
    pallas_call x1, Pallas kernels: 0.65 us -> 1.25 us  [finish(): pl.pallas_call(finish_kernel, out_shape=(jax.ShapeDtypeStruct(act.shape,...]
where the time goes in v10:
time: 35 us; the launch traced here: 34.8 us
  blocking collectives  11.8 us (34%)
  starting transfers between devices  9.38 us (27%)
  waiting for transfers between devices  7.41 us (21%)
  Pallas kernels  3.92 us (11%)
  local copies, waits for them, and re-layouts  1.5 us (4%)
  between operations  0.79 us (2%)
    all_to_all x1, blocking collectives, body(): got = lax.all_to_all(parts, 'rows', split_axis=0, concat_axis=0, tiled=True)  11.8 us
    ppermute x8, starting transfers between devices, across(): return lax.ppermute(value, BOTH, pairs)  9.38 us
    ppermute x8, waiting for transfers between devices, across(): return lax.ppermute(value, BOTH, pairs)  7.41 us
    unnamed x14, local copies, waits for them, and re-layouts  1.49 us
    pallas_call x1, Pallas kernels, place_blocks(): pl.pallas_call(functools.partial(place_kernel, digit_groups(owners)), out...  1.36 us
    pallas_call x1, Pallas kernels, finish(): pl.pallas_call(finish_kernel, out_shape=(jax.ShapeDtypeStruct(act.shape,...  1.25 us
  transfers between devices with their start and end apart: 8, of which 5 were waited for; matrix products, arithmetic and copies ran while one was open for 0% of the time, Pallas kernels for 6%

profile of v10, /device:TPU:0, one launch (start us, length us, event | category | flops | bytes accessed | tf_op | source)
XLA Modules:
  0.0 34.8 jit_solution(16050826388651480409)
XLA Ops:
  0.6 0.0 copy-start
  0.6 0.0 copy-start.1
  0.7 0.8 %copy-done = bf16[256,128]{1,0:T(8,128)(2,1)S(1)} copy-done((bf16[256,128]{1,0:T(8,128)(2,1)S(1)}, bf16[256,128]{1,0:T(8,128)(2,1)}, u32[]{:S(2)}) %copy-start) | copy-done | bytes 65560
  1.5 5.1 %collective-permute-start.2 = (bf16[128,128]{1,0:T(8,128)(2,1)S(1)}, bf16[128,128]{1,0:T(8,128)(2,1)S(1)}, u32[]{:S(2)}, u32[]{:S(2)}) collective-permute-start(bf16[128,128]{1,0:T(8,128)(2,1)S(1)} %copy.15), channel_id=1, source_target_pairs={{0,24},{1,25},{2,26},{3,27},{4,28},{5,29},{6,30},{7,31},{8,16},{9,... | collective-permute-start | bytes 98312 | tf_op jit(solution)/shard_map/ppermute | solution.py:29
  6.6 0.0 collective-permute-start.1
  6.6 0.6 %collective-permute-start = (bf16[128,128]{1,0:T(8,128)(2,1)S(1)}, bf16[128,128]{1,0:T(8,128)(2,1)S(1)}, u32[]{:S(2)}, u32[]{:S(2)}) collective-permute-start(bf16[128,128]{1,0:T(8,128)(2,1)S(1)} %constant_dynamic-slice_fusion.value), channel_id=1, source_target_pairs={{0,8},{1,9},{2,10},{3,11},{4,12},{5,13},{6,14},{7,15},{8,0},{9,1},... | collective-permute-start | bytes 98312 | tf_op jit(solution)/shard_map/ppermute | solution.py:29
  7.2 1.3 %collective-permute-done.2 = bf16[128,128]{1,0:T(8,128)(2,1)S(1)} collective-permute-done((bf16[128,128]{1,0:T(8,128)(2,1)S(1)}, bf16[128,128]{1,0:T(8,128)(2,1)S(1)}, u32[]{:S(2)}, u32[]{:S(2)}) %collective-permute-start.2) | collective-permute-done | bytes 32800 | tf_op jit(solution)/shard_map/ppermute | solution.py:29
  8.5 2.9 %collective-permute-done.1 = bf16[128,128]{1,0:T(8,128)(2,1)S(1)} collective-permute-done((bf16[128,128]{1,0:T(8,128)(2,1)S(1)}, bf16[128,128]{1,0:T(8,128)(2,1)S(1)}, u32[]{:S(2)}, u32[]{:S(2)}) %collective-permute-start.1) | collective-permute-done | bytes 32800 | tf_op jit(solution)/shard_map/ppermute | solution.py:29
  11.4 0.0 collective-permute-done
  11.5 0.0 copy-start.3
  11.5 0.0 copy-start.2
  11.5 0.0 copy-start.5
  11.5 2.5 %collective-permute-start.4 = (bf16[512,128]{1,0:T(8,128)(2,1)S(1)}, bf16[512,128]{1,0:T(8,128)(2,1)S(1)}, u32[]{:S(2)}, u32[]{:S(2)}) collective-permute-start(bf16[512,128]{1,0:T(8,128)(2,1)S(1)} %copy.17), channel_id=1, source_target_pairs={{0,6},{1,7},{2,4},{3,5},{4,2},{5,3},{6,0},{7,1},{8,14},{9,15},{10,... | collective-permute-start | bytes 393224 | tf_op jit(solution)/shard_map/ppermute | solution.py:29
  14.0 0.5 %collective-permute-start.6 = (bf16[512,128]{1,0:T(8,128)(2,1)S(1)}, bf16[512,128]{1,0:T(8,128)(2,1)S(1)}, u32[]{:S(2)}, u32[]{:S(2)}) collective-permute-start(bf16[512,128]{1,0:T(8,128)(2,1)S(1)} %copy.16.value), channel_id=1, source_target_pairs={{0,4},{1,5},{2,6},{3,7},{4,0},{5,1},{6,2},{7,3},{8,12},{9,13},{10,... | collective-permute-start | bytes 393224 | tf_op jit(solution)/shard_map/ppermute | solution.py:29
  14.5 0.5 %collective-permute-start.5 = (bf16[512,128]{1,0:T(8,128)(2,1)S(1)}, bf16[512,128]{1,0:T(8,128)(2,1)S(1)}, u32[]{:S(2)}, u32[]{:S(2)}) collective-permute-start(bf16[512,128]{1,0:T(8,128)(2,1)S(1)} %pad_maximum_fusion.value.refs_0_), channel_id=1, source_target_pairs={{0,2},{1,3},{2,0},{3,1},{4,6},{5,7},{6,4},{7,5},{8,10},{9,11},{10,... | collective-permute-start | bytes 393224 | tf_op jit(solution)/shard_map/ppermute | solution.py:29
  15.1 0.0 copy-done.3
  15.1 0.0 collective-permute-start.3
  15.1 0.0 copy-start.4
  15.1 0.0 copy-start.6
  15.1 0.0 copy-done.1
  15.1 0.0 copy-done.2
  15.1 0.0 copy-done.5
  15.1 0.6 %copy-done.4 = f32[256]{0:T(256)S(1)} copy-done((f32[256]{0:T(256)S(1)}, f32[256]{0:T(256)}, u32[]{:S(2)}) %copy-start.4) | copy-done | bytes 1048
  15.8 0.0 copy-done.6
  15.8 1.4 %place.1 = (bf16[16,256,128]{2,1,0:T(8,128)(2,1)S(1)}, bf16[256,128]{1,0:T(8,128)(2,1)S(1)}, f32[256,128]{1,0:T(8,128)S(1)}) custom-call(s32[1,4]{1,0:T(1,128)S(1)} %copy-done.6, s32[4,16]{1,0:T(4,128)S(1)} %bitcast.8, bf16[4,16,4096]{2,1,0:T(8,128)(2,1)S(1)} %bitcast.5, bf16[128,256]{1,0:T(8,128)(2,1)S(1)} %copy-done.2, f32[1,256]{1,0:T(1,128)S(1)} %bitcast.6), custom_call_target="tpu_custom_call" | custom-call | tf_op jit(solution)/shard_map/place/pallas_call | solution.py:115
  17.1 0.0 collective-permute-done.3.other
  17.1 0.3 turn.1.cot_t
  17.4 1.4 %collective-permute-done.4.refs_1_ = bf16[512,128]{1,0:T(8,128)(2,1)S(1)} collective-permute-done((bf16[512,128]{1,0:T(8,128)(2,1)S(1)}, bf16[512,128]{1,0:T(8,128)(2,1)S(1)}, u32[]{:S(2)}, u32[]{:S(2)}) %collective-permute-start.4) | collective-permute-done | bytes 131104 | tf_op jit(solution)/shard_map/ppermute | solution.py:29
  18.8 0.3 block_sum.2.refs_0_
  19.1 0.5 %collective-permute-done.6.refs_2_ = bf16[512,128]{1,0:T(8,128)(2,1)S(1)} collective-permute-done((bf16[512,128]{1,0:T(8,128)(2,1)S(1)}, bf16[512,128]{1,0:T(8,128)(2,1)S(1)}, u32[]{:S(2)}, u32[]{:S(2)}) %collective-permute-start.6) | collective-permute-done | bytes 131104 | tf_op jit(solution)/shard_map/ppermute | solution.py:29
  19.6 0.0 collective-permute-done.5.refs_1_
  19.6 0.3 block_sum.3.mine
  19.9 0.1 collective-permute-start.7
  20.0 1.3 %collective-permute-done.7.other = f32[256,128]{1,0:T(8,128)S(1)} collective-permute-done((f32[256,128]{1,0:T(8,128)S(1)}, f32[256,128]{1,0:T(8,128)S(1)}, u32[]{:S(2)}, u32[]{:S(2)}) %collective-permute-start.7) | collective-permute-done | bytes 131104 | tf_op jit(solution)/shard_map/ppermute | solution.py:29
  21.3 0.4 %layer.1 = (bf16[16,32,128]{2,1,0:T(8,128)(2,1)S(1)}, bf16[128,256]{1,0:T(8,128)(2,1)S(1)}) custom-call(f32[256,128]{1,0:T(8,128)S(1)} %block_sum.3.mine, f32[256,128]{1,0:T(8,128)S(1)} %collective-permute-done.7.other, bf16[128,256]{1,0:T(8,128)(2,1)S(1)} %copy-done.2, f32[1,256]{1,0:T(1,128)S(1)} %bitcast.7, ...), custom_call_target="tpu_custom_call" | custom-call | tf_op jit(solution)/shard_map/layer/pallas_call | solution.py:221
  21.7 11.8 %all_to_all.5.got = bf16[16,32,128]{2,1,0:T(8,128)(2,1)S(1)} all-to-all(bf16[16,32,128]{2,1,0:T(8,128)(2,1)S(1)} %get-tuple-element.25), channel_id=1, replica_groups=mesh['rows'=16,'rep'=2] {'rows'}, dimensions={0} | all-to-all | bytes 262144 | tf_op jit(solution)/shard_map/all_to_all | solution.py:293
  33.6 1.2 %finish.1 = (bf16[128,256]{1,0:T(8,128)(2,1)}, f32[16,128]{1,0:T(8,128)}, f32[1,16]{1,0:T(1,128)}) custom-call(bf16[128,256]{1,0:T(8,128)(2,1)S(1)} %get-tuple-element.24.act_in, bf16[16,32,128]{2,1,0:T(8,128)(2,1)S(1)} %all_to_all.5.got), custom_call_target="tpu_custom_call" | custom-call | tf_op jit(solution)/shard_map/finish/pallas_call | solution.py:250
  (6 shorter events, 0.0 us)
Async XLA Ops:
  0.6 0.8 %copy-start = (bf16[256,128]{1,0:T(8,128)(2,1)S(1)}, bf16[256,128]{1,0:T(8,128)(2,1)}, u32[]{:S(2)}) copy-start(bf16[256,128]{1,0:T(8,128)(2,1)} %param.7) | copy-start | bytes 196612
  0.6 14.4 %copy-start.1 = (bf16[1,4,16,4096]{3,2,1,0:T(8,128)(2,1)S(1)}, bf16[1,4,16,4096]{3,2,1,0:T(8,128)(2,1)}, u32[]{:S(2)}) copy-start(bf16[1,4,16,4096]{3,2,1,0:T(8,128)(2,1)} %param.12) | copy-start | bytes 1572868
  1.5 7.0 %collective-permute-start.2 = (bf16[128,128]{1,0:T(8,128)(2,1)S(1)}, bf16[128,128]{1,0:T(8,128)(2,1)S(1)}, u32[]{:S(2)}, u32[]{:S(2)}) collective-permute-start(bf16[128,128]{1,0:T(8,128)(2,1)S(1)} %copy.15), channel_id=1, source_target_pairs={{0,24},{1,25},{2,26},{3,27},{4,28},{5,29},{6,30},{7,31},{8,16},{9,... | collective-permute-start | bytes 98312 | tf_op jit(solution)/shard_map/ppermute | solution.py:29
  6.6 4.8 %collective-permute-start.1 = (bf16[128,128]{1,0:T(8,128)(2,1)S(1)}, bf16[128,128]{1,0:T(8,128)(2,1)S(1)}, u32[]{:S(2)}, u32[]{:S(2)}) collective-permute-start(bf16[128,128]{1,0:T(8,128)(2,1)S(1)} %copy.14.value), channel_id=1, source_target_pairs={{0,16},{1,17},{2,18},{3,19},{4,20},{5,21},{6,22},{7,23},{8,24},{9,... | collective-permute-start | bytes 98312 | tf_op jit(solution)/shard_map/ppermute | solution.py:29
  6.6 4.8 %collective-permute-start = (bf16[128,128]{1,0:T(8,128)(2,1)S(1)}, bf16[128,128]{1,0:T(8,128)(2,1)S(1)}, u32[]{:S(2)}, u32[]{:S(2)}) collective-permute-start(bf16[128,128]{1,0:T(8,128)(2,1)S(1)} %constant_dynamic-slice_fusion.value), channel_id=1, source_target_pairs={{0,8},{1,9},{2,10},{3,11},{4,12},{5,13},{6,14},{7,15},{8,0},{9,1},... | collective-permute-start | bytes 98312 | tf_op jit(solution)/shard_map/ppermute | solution.py:29
  11.5 3.6 %copy-start.3 = (bf16[128,256]{1,0:T(8,128)(2,1)S(1)}, bf16[128,256]{1,0:T(8,128)(2,1)}, u32[]{:S(2)}) copy-start(bf16[128,256]{1,0:T(8,128)(2,1)} %mine) | copy-start | bytes 196612
  11.5 3.6 %copy-start.2 = (bf16[128,256]{1,0:T(8,128)(2,1)S(1)}, bf16[128,256]{1,0:T(8,128)(2,1)}, u32[]{:S(2)}) copy-start(bf16[128,256]{1,0:T(8,128)(2,1)} %weight.3) | copy-start | bytes 196612
  11.5 3.6 %copy-start.5 = (s32[1,4,16]{2,1,0:T(4,128)S(1)}, s32[1,4,16]{2,1,0:T(4,128)}, u32[]{:S(2)}) copy-start(s32[1,4,16]{2,1,0:T(4,128)} %param.11) | copy-start | bytes 772
  11.5 7.3 %collective-permute-start.4 = (bf16[512,128]{1,0:T(8,128)(2,1)S(1)}, bf16[512,128]{1,0:T(8,128)(2,1)S(1)}, u32[]{:S(2)}, u32[]{:S(2)}) collective-permute-start(bf16[512,128]{1,0:T(8,128)(2,1)S(1)} %copy.17), channel_id=1, source_target_pairs={{0,6},{1,7},{2,4},{3,5},{4,2},{5,3},{6,0},{7,1},{8,14},{9,15},{10,... | collective-permute-start | bytes 393224 | tf_op jit(solution)/shard_map/ppermute | solution.py:29
  14.0 5.6 %collective-permute-start.6 = (bf16[512,128]{1,0:T(8,128)(2,1)S(1)}, bf16[512,128]{1,0:T(8,128)(2,1)S(1)}, u32[]{:S(2)}, u32[]{:S(2)}) collective-permute-start(bf16[512,128]{1,0:T(8,128)(2,1)S(1)} %copy.16.value), channel_id=1, source_target_pairs={{0,4},{1,5},{2,6},{3,7},{4,0},{5,1},{6,2},{7,3},{8,12},{9,13},{10,... | collective-permute-start | bytes 393224 | tf_op jit(solution)/shard_map/ppermute | solution.py:29
  14.5 5.1 %collective-permute-start.5 = (bf16[512,128]{1,0:T(8,128)(2,1)S(1)}, bf16[512,128]{1,0:T(8,128)(2,1)S(1)}, u32[]{:S(2)}, u32[]{:S(2)}) collective-permute-start(bf16[512,128]{1,0:T(8,128)(2,1)S(1)} %pad_maximum_fusion.value.refs_0_), channel_id=1, source_target_pairs={{0,2},{1,3},{2,0},{3,1},{4,6},{5,7},{6,4},{7,5},{8,10},{9,11},{10,... | collective-permute-start | bytes 393224 | tf_op jit(solution)/shard_map/ppermute | solution.py:29
  15.1 2.1 %collective-permute-start.3 = (bf16[128,256]{1,0:T(8,128)(2,1)S(1)}, bf16[128,256]{1,0:T(8,128)(2,1)S(1)}, u32[]{:S(2)}, u32[]{:S(2)}) collective-permute-start(bf16[128,256]{1,0:T(8,128)(2,1)S(1)} %copy-done.3), channel_id=1, source_target_pairs={{0,1},{1,0},{2,3},{3,2},{4,5},{5,4},{6,7},{7,6},{8,9},{9,8},{10,11... | collective-permute-start | bytes 196616 | tf_op jit(solution)/shard_map/ppermute | solution.py:29
  15.1 0.7 %copy-start.4 = (f32[256]{0:T(256)S(1)}, f32[256]{0:T(256)}, u32[]{:S(2)}) copy-start(f32[256]{0:T(256)} %param.9) | copy-start | bytes 3076
  15.1 0.7 %copy-start.6 = (s32[1,4]{1,0:T(1,128)S(1)}, s32[1,4]{1,0:T(1,128)}, u32[]{:S(2)}) copy-start(s32[1,4]{1,0:T(1,128)} %counts.1) | copy-start | bytes 52
  19.9 1.4 %collective-permute-start.7 = (f32[256,128]{1,0:T(8,128)S(1)}, f32[256,128]{1,0:T(8,128)S(1)}, u32[]{:S(2)}, u32[]{:S(2)}) collective-permute-start(f32[256,128]{1,0:T(8,128)S(1)} %block_sum.3.mine), channel_id=1, source_target_pairs={{0,1},{1,0},{2,3},{3,2},{4,5},{5,4},{6,7},{7,6},{8,9},{9,8},{10,11... | collective-permute-start | bytes 393224 | tf_op jit(solution)/shard_map/ppermute | solution.py:29

commit v11 on v9

--- a/solution.py
+++ b/solution.py
@@ -231,15 +231,21 @@
     )(mine, other, weight, bias, weight_t, bias_t, cot_t)
 
 
-def finish_kernel(act_in, got, act, weight_grad, bias_grad):
-    act[...] = act_in[...]
+def finish_kernel(act_in, got, act, weight_out, bias_out, weight_grad, bias_grad, sems):
+    pairs = ((act_in, act), (weight_grad, weight_out), (bias_grad, bias_out))
+    copies_out = [pltpu.make_async_copy(a, b, sems.at[i]) for i, (a, b) in enumerate(pairs)]
+    copies_out[0].start()
     share = weight_grad.shape[0]
     total = jnp.sum(got[...].astype(jnp.float32), axis=0)
     weight_grad[...] = total[:share]
+    copies_out[1].start()
     flat = jnp.concatenate([total[share : share + 1], total[share + 1 : share + 2]], axis=1)
     flat = jnp.broadcast_to(flat, (8, 256))
     flat = pltpu.roll(flat, lax.rem(256 - lax.axis_index("rows") * share, 256), 1)
     bias_grad[...] = flat[:1, :share]
+    copies_out[2].start()
+    for copy in copies_out:
+        copy.wait()
 
 
 def finish(act, got):
@@ -253,7 +259,12 @@
             jax.ShapeDtypeStruct((1, share), jnp.float32),
         ),
         in_specs=[VMEM] * 2,
-        out_specs=(VMEM,) * 3,
+        out_specs=(pl.BlockSpec(memory_space=pltpu.HBM),) * 3,
+        scratch_shapes=[
+            pltpu.VMEM((share, 128), jnp.float32),
+            pltpu.VMEM((1, share), jnp.float32),
+            pltpu.SemaphoreType.DMA((3,)),
+        ],
         compiler_params=limit(owners),
         name="finish",
     )(act, got)

time: 34.4 us -> 34.4 us (level)
  no operation moved by 1% of the time
where the time goes in v11:
time: 34.4 us; the launch traced here: 34.2 us
  blocking collectives  11.8 us (34%)
  starting transfers between devices  9.38 us (27%)
  waiting for transfers between devices  7.41 us (22%)
  Pallas kernels  3.32 us (10%)
  local copies, waits for them, and re-layouts  1.5 us (4%)
  between operations  0.79 us (2%)
    all_to_all x1, blocking collectives, body(): got = lax.all_to_all(parts, 'rows', split_axis=0, concat_axis=0, tiled=True)  11.8 us
    ppermute x8, starting transfers between devices, across(): return lax.ppermute(value, BOTH, pairs)  9.38 us
    ppermute x8, waiting for transfers between devices, across(): return lax.ppermute(value, BOTH, pairs)  7.41 us
    unnamed x14, local copies, waits for them, and re-layouts  1.49 us
    pallas_call x1, Pallas kernels, place_blocks(): pl.pallas_call(functools.partial(place_kernel, digit_groups(owners)), out...  1.36 us
  transfers between devices with their start and end apart: 8, of which 5 were waited for; matrix products, arithmetic and copies ran while one was open for 0% of the time, Pallas kernels for 6%

profile of v11, /device:TPU:0, one launch (start us, length us, event | category | flops | bytes accessed | tf_op | source)
XLA Modules:
  0.0 34.2 jit_solution(2527178018724727067)
XLA Ops:
  0.6 0.0 copy-start
  0.6 0.0 copy-start.1
  0.7 0.8 %copy-done = bf16[256,128]{1,0:T(8,128)(2,1)S(1)} copy-done((bf16[256,128]{1,0:T(8,128)(2,1)S(1)}, bf16[256,128]{1,0:T(8,128)(2,1)}, u32[]{:S(2)}) %copy-start) | copy-done | bytes 65560
  1.5 5.1 %collective-permute-start.2 = (bf16[128,128]{1,0:T(8,128)(2,1)S(1)}, bf16[128,128]{1,0:T(8,128)(2,1)S(1)}, u32[]{:S(2)}, u32[]{:S(2)}) collective-permute-start(bf16[128,128]{1,0:T(8,128)(2,1)S(1)} %copy.15), channel_id=1, source_target_pairs={{0,24},{1,25},{2,26},{3,27},{4,28},{5,29},{6,30},{7,31},{8,16},{9,... | collective-permute-start | bytes 98312 | tf_op jit(solution)/shard_map/ppermute | solution.py:29
  6.6 0.0 collective-permute-start.1
  6.6 0.6 %collective-permute-start = (bf16[128,128]{1,0:T(8,128)(2,1)S(1)}, bf16[128,128]{1,0:T(8,128)(2,1)S(1)}, u32[]{:S(2)}, u32[]{:S(2)}) collective-permute-start(bf16[128,128]{1,0:T(8,128)(2,1)S(1)} %constant_dynamic-slice_fusion.value), channel_id=1, source_target_pairs={{0,8},{1,9},{2,10},{3,11},{4,12},{5,13},{6,14},{7,15},{8,0},{9,1},... | collective-permute-start | bytes 98312 | tf_op jit(solution)/shard_map/ppermute | solution.py:29
  7.2 1.3 %collective-permute-done.2 = bf16[128,128]{1,0:T(8,128)(2,1)S(1)} collective-permute-done((bf16[128,128]{1,0:T(8,128)(2,1)S(1)}, bf16[128,128]{1,0:T(8,128)(2,1)S(1)}, u32[]{:S(2)}, u32[]{:S(2)}) %collective-permute-start.2) | collective-permute-done | bytes 32800 | tf_op jit(solution)/shard_map/ppermute | solution.py:29
  8.5 2.9 %collective-permute-done.1 = bf16[128,128]{1,0:T(8,128)(2,1)S(1)} collective-permute-done((bf16[128,128]{1,0:T(8,128)(2,1)S(1)}, bf16[128,128]{1,0:T(8,128)(2,1)S(1)}, u32[]{:S(2)}, u32[]{:S(2)}) %collective-permute-start.1) | collective-permute-done | bytes 32800 | tf_op jit(solution)/shard_map/ppermute | solution.py:29
  11.4 0.0 collective-permute-done
  11.5 0.0 copy-start.3
  11.5 0.0 copy-start.2
  11.5 0.0 copy-start.5
  11.5 2.5 %collective-permute-start.4 = (bf16[512,128]{1,0:T(8,128)(2,1)S(1)}, bf16[512,128]{1,0:T(8,128)(2,1)S(1)}, u32[]{:S(2)}, u32[]{:S(2)}) collective-permute-start(bf16[512,128]{1,0:T(8,128)(2,1)S(1)} %copy.17), channel_id=1, source_target_pairs={{0,6},{1,7},{2,4},{3,5},{4,2},{5,3},{6,0},{7,1},{8,14},{9,15},{10,... | collective-permute-start | bytes 393224 | tf_op jit(solution)/shard_map/ppermute | solution.py:29
  14.0 0.5 %collective-permute-start.6 = (bf16[512,128]{1,0:T(8,128)(2,1)S(1)}, bf16[512,128]{1,0:T(8,128)(2,1)S(1)}, u32[]{:S(2)}, u32[]{:S(2)}) collective-permute-start(bf16[512,128]{1,0:T(8,128)(2,1)S(1)} %copy.16.value), channel_id=1, source_target_pairs={{0,4},{1,5},{2,6},{3,7},{4,0},{5,1},{6,2},{7,3},{8,12},{9,13},{10,... | collective-permute-start | bytes 393224 | tf_op jit(solution)/shard_map/ppermute | solution.py:29
  14.5 0.5 %collective-permute-start.5 = (bf16[512,128]{1,0:T(8,128)(2,1)S(1)}, bf16[512,128]{1,0:T(8,128)(2,1)S(1)}, u32[]{:S(2)}, u32[]{:S(2)}) collective-permute-start(bf16[512,128]{1,0:T(8,128)(2,1)S(1)} %pad_maximum_fusion.value.refs_0_), channel_id=1, source_target_pairs={{0,2},{1,3},{2,0},{3,1},{4,6},{5,7},{6,4},{7,5},{8,10},{9,11},{10,... | collective-permute-start | bytes 393224 | tf_op jit(solution)/shard_map/ppermute | solution.py:29
  15.1 0.0 copy-done.3
  15.1 0.0 collective-permute-start.3
  15.1 0.0 copy-start.4
  15.1 0.0 copy-start.6
  15.1 0.0 copy-done.1
  15.1 0.0 copy-done.2
  15.1 0.0 copy-done.5
  15.1 0.6 %copy-done.4 = f32[256]{0:T(256)S(1)} copy-done((f32[256]{0:T(256)S(1)}, f32[256]{0:T(256)}, u32[]{:S(2)}) %copy-start.4) | copy-done | bytes 1048
  15.8 0.0 copy-done.6
  15.8 1.4 %place.1 = (bf16[16,256,128]{2,1,0:T(8,128)(2,1)S(1)}, bf16[256,128]{1,0:T(8,128)(2,1)S(1)}, f32[256,128]{1,0:T(8,128)S(1)}) custom-call(s32[1,4]{1,0:T(1,128)S(1)} %copy-done.6, s32[4,16]{1,0:T(4,128)S(1)} %bitcast.8, bf16[4,16,4096]{2,1,0:T(8,128)(2,1)S(1)} %bitcast.5, bf16[128,256]{1,0:T(8,128)(2,1)S(1)} %copy-done.2, f32[1,256]{1,0:T(1,128)S(1)} %bitcast.6), custom_call_target="tpu_custom_call" | custom-call | tf_op jit(solution)/shard_map/place/pallas_call | solution.py:115
  17.1 0.0 collective-permute-done.3.other
  17.1 0.3 turn.1.cot_t
  17.4 1.4 %collective-permute-done.4.refs_1_ = bf16[512,128]{1,0:T(8,128)(2,1)S(1)} collective-permute-done((bf16[512,128]{1,0:T(8,128)(2,1)S(1)}, bf16[512,128]{1,0:T(8,128)(2,1)S(1)}, u32[]{:S(2)}, u32[]{:S(2)}) %collective-permute-start.4) | collective-permute-done | bytes 131104 | tf_op jit(solution)/shard_map/ppermute | solution.py:29
  18.8 0.3 block_sum.2.refs_0_
  19.1 0.5 %collective-permute-done.6.refs_2_ = bf16[512,128]{1,0:T(8,128)(2,1)S(1)} collective-permute-done((bf16[512,128]{1,0:T(8,128)(2,1)S(1)}, bf16[512,128]{1,0:T(8,128)(2,1)S(1)}, u32[]{:S(2)}, u32[]{:S(2)}) %collective-permute-start.6) | collective-permute-done | bytes 131104 | tf_op jit(solution)/shard_map/ppermute | solution.py:29
  19.6 0.0 collective-permute-done.5.refs_1_
  19.6 0.3 block_sum.3.mine
  19.9 0.1 collective-permute-start.7
  20.0 1.3 %collective-permute-done.7.other = f32[256,128]{1,0:T(8,128)S(1)} collective-permute-done((f32[256,128]{1,0:T(8,128)S(1)}, f32[256,128]{1,0:T(8,128)S(1)}, u32[]{:S(2)}, u32[]{:S(2)}) %collective-permute-start.7) | collective-permute-done | bytes 131104 | tf_op jit(solution)/shard_map/ppermute | solution.py:29
  21.3 0.4 %layer.1 = (bf16[16,32,128]{2,1,0:T(8,128)(2,1)S(1)}, bf16[128,256]{1,0:T(8,128)(2,1)S(1)}) custom-call(f32[256,128]{1,0:T(8,128)S(1)} %block_sum.3.mine, f32[256,128]{1,0:T(8,128)S(1)} %collective-permute-done.7.other, bf16[128,256]{1,0:T(8,128)(2,1)S(1)} %copy-done.2, f32[1,256]{1,0:T(1,128)S(1)} %bitcast.7, ...), custom_call_target="tpu_custom_call" | custom-call | tf_op jit(solution)/shard_map/layer/pallas_call | solution.py:221
  21.7 11.8 %all_to_all.5.got = bf16[16,32,128]{2,1,0:T(8,128)(2,1)S(1)} all-to-all(bf16[16,32,128]{2,1,0:T(8,128)(2,1)S(1)} %get-tuple-element.25), channel_id=1, replica_groups=mesh['rows'=16,'rep'=2] {'rows'}, dimensions={0} | all-to-all | bytes 262144 | tf_op jit(solution)/shard_map/all_to_all | solution.py:301
  33.6 0.7 %finish.1 = (bf16[128,256]{1,0:T(8,128)(2,1)}, f32[16,128]{1,0:T(8,128)}, f32[1,16]{1,0:T(1,128)}) custom-call(bf16[128,256]{1,0:T(8,128)(2,1)S(1)} %get-tuple-element.24.act_in, bf16[16,32,128]{2,1,0:T(8,128)(2,1)S(1)} %all_to_all.5.got), custom_call_target="tpu_custom_call" | custom-call | tf_op jit(solution)/shard_map/finish/pallas_call | solution.py:254
  (6 shorter events, 0.0 us)
Async XLA Ops:
  0.6 0.8 %copy-start = (bf16[256,128]{1,0:T(8,128)(2,1)S(1)}, bf16[256,128]{1,0:T(8,128)(2,1)}, u32[]{:S(2)}) copy-start(bf16[256,128]{1,0:T(8,128)(2,1)} %param.7) | copy-start | bytes 196612
  0.6 14.4 %copy-start.1 = (bf16[1,4,16,4096]{3,2,1,0:T(8,128)(2,1)S(1)}, bf16[1,4,16,4096]{3,2,1,0:T(8,128)(2,1)}, u32[]{:S(2)}) copy-start(bf16[1,4,16,4096]{3,2,1,0:T(8,128)(2,1)} %param.12) | copy-start | bytes 1572868
  1.5 7.0 %collective-permute-start.2 = (bf16[128,128]{1,0:T(8,128)(2,1)S(1)}, bf16[128,128]{1,0:T(8,128)(2,1)S(1)}, u32[]{:S(2)}, u32[]{:S(2)}) collective-permute-start(bf16[128,128]{1,0:T(8,128)(2,1)S(1)} %copy.15), channel_id=1, source_target_pairs={{0,24},{1,25},{2,26},{3,27},{4,28},{5,29},{6,30},{7,31},{8,16},{9,... | collective-permute-start | bytes 98312 | tf_op jit(solution)/shard_map/ppermute | solution.py:29
  6.6 4.8 %collective-permute-start.1 = (bf16[128,128]{1,0:T(8,128)(2,1)S(1)}, bf16[128,128]{1,0:T(8,128)(2,1)S(1)}, u32[]{:S(2)}, u32[]{:S(2)}) collective-permute-start(bf16[128,128]{1,0:T(8,128)(2,1)S(1)} %copy.14.value), channel_id=1, source_target_pairs={{0,16},{1,17},{2,18},{3,19},{4,20},{5,21},{6,22},{7,23},{8,24},{9,... | collective-permute-start | bytes 98312 | tf_op jit(solution)/shard_map/ppermute | solution.py:29
  6.6 4.8 %collective-permute-start = (bf16[128,128]{1,0:T(8,128)(2,1)S(1)}, bf16[128,128]{1,0:T(8,128)(2,1)S(1)}, u32[]{:S(2)}, u32[]{:S(2)}) collective-permute-start(bf16[128,128]{1,0:T(8,128)(2,1)S(1)} %constant_dynamic-slice_fusion.value), channel_id=1, source_target_pairs={{0,8},{1,9},{2,10},{3,11},{4,12},{5,13},{6,14},{7,15},{8,0},{9,1},... | collective-permute-start | bytes 98312 | tf_op jit(solution)/shard_map/ppermute | solution.py:29
  11.5 3.6 %copy-start.3 = (bf16[128,256]{1,0:T(8,128)(2,1)S(1)}, bf16[128,256]{1,0:T(8,128)(2,1)}, u32[]{:S(2)}) copy-start(bf16[128,256]{1,0:T(8,128)(2,1)} %mine) | copy-start | bytes 196612
  11.5 3.6 %copy-start.2 = (bf16[128,256]{1,0:T(8,128)(2,1)S(1)}, bf16[128,256]{1,0:T(8,128)(2,1)}, u32[]{:S(2)}) copy-start(bf16[128,256]{1,0:T(8,128)(2,1)} %weight.3) | copy-start | bytes 196612
  11.5 3.6 %copy-start.5 = (s32[1,4,16]{2,1,0:T(4,128)S(1)}, s32[1,4,16]{2,1,0:T(4,128)}, u32[]{:S(2)}) copy-start(s32[1,4,16]{2,1,0:T(4,128)} %param.11) | copy-start | bytes 772
  11.5 7.3 %collective-permute-start.4 = (bf16[512,128]{1,0:T(8,128)(2,1)S(1)}, bf16[512,128]{1,0:T(8,128)(2,1)S(1)}, u32[]{:S(2)}, u32[]{:S(2)}) collective-permute-start(bf16[512,128]{1,0:T(8,128)(2,1)S(1)} %copy.17), channel_id=1, source_target_pairs={{0,6},{1,7},{2,4},{3,5},{4,2},{5,3},{6,0},{7,1},{8,14},{9,15},{10,... | collective-permute-start | bytes 393224 | tf_op jit(solution)/shard_map/ppermute | solution.py:29
  14.0 5.6 %collective-permute-start.6 = (bf16[512,128]{1,0:T(8,128)(2,1)S(1)}, bf16[512,128]{1,0:T(8,128)(2,1)S(1)}, u32[]{:S(2)}, u32[]{:S(2)}) collective-permute-start(bf16[512,128]{1,0:T(8,128)(2,1)S(1)} %copy.16.value), channel_id=1, source_target_pairs={{0,4},{1,5},{2,6},{3,7},{4,0},{5,1},{6,2},{7,3},{8,12},{9,13},{10,... | collective-permute-start | bytes 393224 | tf_op jit(solution)/shard_map/ppermute | solution.py:29
  14.5 5.1 %collective-permute-start.5 = (bf16[512,128]{1,0:T(8,128)(2,1)S(1)}, bf16[512,128]{1,0:T(8,128)(2,1)S(1)}, u32[]{:S(2)}, u32[]{:S(2)}) collective-permute-start(bf16[512,128]{1,0:T(8,128)(2,1)S(1)} %pad_maximum_fusion.value.refs_0_), channel_id=1, source_target_pairs={{0,2},{1,3},{2,0},{3,1},{4,6},{5,7},{6,4},{7,5},{8,10},{9,11},{10,... | collective-permute-start | bytes 393224 | tf_op jit(solution)/shard_map/ppermute | solution.py:29
  15.1 2.1 %collective-permute-start.3 = (bf16[128,256]{1,0:T(8,128)(2,1)S(1)}, bf16[128,256]{1,0:T(8,128)(2,1)S(1)}, u32[]{:S(2)}, u32[]{:S(2)}) collective-permute-start(bf16[128,256]{1,0:T(8,128)(2,1)S(1)} %copy-done.3), channel_id=1, source_target_pairs={{0,1},{1,0},{2,3},{3,2},{4,5},{5,4},{6,7},{7,6},{8,9},{9,8},{10,11... | collective-permute-start | bytes 196616 | tf_op jit(solution)/shard_map/ppermute | solution.py:29
  15.1 0.7 %copy-start.4 = (f32[256]{0:T(256)S(1)}, f32[256]{0:T(256)}, u32[]{:S(2)}) copy-start(f32[256]{0:T(256)} %param.9) | copy-start | bytes 3076
  15.1 0.7 %copy-start.6 = (s32[1,4]{1,0:T(1,128)S(1)}, s32[1,4]{1,0:T(1,128)}, u32[]{:S(2)}) copy-start(s32[1,4]{1,0:T(1,128)} %counts.1) | copy-start | bytes 52
  19.9 1.4 %collective-permute-start.7 = (f32[256,128]{1,0:T(8,128)S(1)}, f32[256,128]{1,0:T(8,128)S(1)}, u32[]{:S(2)}, u32[]{:S(2)}) collective-permute-start(f32[256,128]{1,0:T(8,128)S(1)} %block_sum.3.mine), channel_id=1, source_target_pairs={{0,1},{1,0},{2,3},{3,2},{4,5},{5,4},{6,7},{7,6},{8,9},{9,8},{10,11... | collective-permute-start | bytes 393224 | tf_op jit(solution)/shard_map/ppermute | solution.py:29

commit v12 on v9

--- a/solution.py
+++ b/solution.py
@@ -27,6 +27,26 @@
 def across(value, mask, owners, swap):
     pairs = [(i, i ^ (2 * mask + swap)) for i in range(2 * owners)]
     return lax.ppermute(value, BOTH, pairs)
+
+
+def half_kernel(features, keep, sem):
+    half, _ = keep.shape
+    side = lax.axis_index("rep")
+    copy = pltpu.make_async_copy(features.at[pl.ds(pl.multiple_of(side * half, half), half), :], keep, sem)
+    copy.start()
+    copy.wait()
+
+
+def own_half(features):
+    return pl.pallas_call(
+        half_kernel,
+        out_shape=jax.ShapeDtypeStruct((features.shape[0] // 2, features.shape[1]), features.dtype),
+        in_specs=[pl.BlockSpec(memory_space=pltpu.HBM)],
+        out_specs=VMEM,
+        scratch_shapes=[pltpu.SemaphoreType.DMA],
+        compiler_params=pltpu.CompilerParams(vmem_limit_bytes=8 << 20),
+        name="own_half",
+    )(pltpu.with_memory_space_constraint(features, pltpu.HBM))
 
 
 def copy_kernel(value, out):
@@ -260,12 +280,10 @@
 
 
 def body(features, weight, bias, block_count, block_cols, block_vals, cotangent):
-    side = lax.axis_index("rep")
     owners = lax.axis_size("rows")
     groups = digit_groups(owners)
-    half_rows = features.shape[0] // 2
-
-    keep = lax.dynamic_slice_in_dim(features, side * half_rows, half_rows, 0)
+
+    keep = own_half(features)
     shift, radix = groups[0]
     sent = zip(range(1, radix), copies(keep, radix - 1))
     pieces = [keep] + [across(value, s << shift, owners, 0) for s, value in sent]

time: 34.4 us -> 34.4 us (level)
  local copies, waits for them, and re-layouts: 1.5 us -> 0.67 us
  Pallas kernels: 3.31 us -> 4.13 us
    pallas_call x0 -> x1, Pallas kernels: none -> 0.83 us  [own_half(): pl.pallas_call(half_kernel, out_shape=jax.ShapeDtypeStruct((features.shap...]
    unnamed x14 -> x12, local copies, waits for them, and re-layouts: 1.49 us -> 0.67 us
where the time goes in v12:
time: 34.4 us; the launch traced here: 34.2 us
  blocking collectives  11.8 us (34%)
  starting transfers between devices  9.38 us (27%)
  waiting for transfers between devices  7.41 us (22%)
  Pallas kernels  4.13 us (12%)
  between operations  0.8 us (2%)
  local copies, waits for them, and re-layouts  0.67 us (2%)
    all_to_all x1, blocking collectives, body(): got = lax.all_to_all(parts, 'rows', split_axis=0, concat_axis=0, tiled=True)  11.8 us
    ppermute x8, starting transfers between devices, across(): return lax.ppermute(value, BOTH, pairs)  9.38 us
    ppermute x8, waiting for transfers between devices, across(): return lax.ppermute(value, BOTH, pairs)  7.41 us
    pallas_call x1, Pallas kernels, place_blocks(): pl.pallas_call(functools.partial(place_kernel, digit_groups(owners)), out...  1.36 us
    pallas_call x1, Pallas kernels, own_half(): pl.pallas_call(half_kernel, out_shape=jax.ShapeDtypeStruct((features.shap...  0.83 us
  transfers between devices with their start and end apart: 8, of which 5 were waited for; matrix products, arithmetic and copies ran while one was open for 0% of the time, Pallas kernels for 6%

profile of v12, /device:TPU:0, one launch (start us, length us, event | category | flops | bytes accessed | tf_op | source)
XLA Modules:
  0.0 34.2 jit_solution(337868173529849581)
XLA Ops:
  0.6 0.0 copy-start
  0.6 0.8 %own_half.1.value = bf16[128,128]{1,0:T(8,128)(2,1)S(1)} custom-call(bf16[256,128]{1,0:T(8,128)(2,1)} %features.1), custom_call_target="tpu_custom_call" | custom-call | tf_op jit(solution)/shard_map/own_half/pallas_call | solution.py:41
  1.5 5.1 %collective-permute-start.2 = (bf16[128,128]{1,0:T(8,128)(2,1)S(1)}, bf16[128,128]{1,0:T(8,128)(2,1)S(1)}, u32[]{:S(2)}, u32[]{:S(2)}) collective-permute-start(bf16[128,128]{1,0:T(8,128)(2,1)S(1)} %copy.15), channel_id=1, source_target_pairs={{0,24},{1,25},{2,26},{3,27},{4,28},{5,29},{6,30},{7,31},{8,16},{9,... | collective-permute-start | bytes 98312 | tf_op jit(solution)/shard_map/ppermute | solution.py:29
  6.6 0.0 collective-permute-start.1
  6.6 0.6 %collective-permute-start = (bf16[128,128]{1,0:T(8,128)(2,1)S(1)}, bf16[128,128]{1,0:T(8,128)(2,1)S(1)}, u32[]{:S(2)}, u32[]{:S(2)}) collective-permute-start(bf16[128,128]{1,0:T(8,128)(2,1)S(1)} %own_half.1.value), channel_id=1, source_target_pairs={{0,8},{1,9},{2,10},{3,11},{4,12},{5,13},{6,14},{7,15},{8,0},{9,1},... | collective-permute-start | bytes 98312 | tf_op jit(solution)/shard_map/ppermute | solution.py:29
  7.3 1.3 %collective-permute-done.2 = bf16[128,128]{1,0:T(8,128)(2,1)S(1)} collective-permute-done((bf16[128,128]{1,0:T(8,128)(2,1)S(1)}, bf16[128,128]{1,0:T(8,128)(2,1)S(1)}, u32[]{:S(2)}, u32[]{:S(2)}) %collective-permute-start.2) | collective-permute-done | bytes 32800 | tf_op jit(solution)/shard_map/ppermute | solution.py:29
  8.5 2.9 %collective-permute-done.1 = bf16[128,128]{1,0:T(8,128)(2,1)S(1)} collective-permute-done((bf16[128,128]{1,0:T(8,128)(2,1)S(1)}, bf16[128,128]{1,0:T(8,128)(2,1)S(1)}, u32[]{:S(2)}, u32[]{:S(2)}) %collective-permute-start.1) | collective-permute-done | bytes 32800 | tf_op jit(solution)/shard_map/ppermute | solution.py:29
  11.4 0.0 collective-permute-done
  11.5 0.0 copy-start.2
  11.5 0.0 copy-start.1
  11.5 0.0 copy-start.4
  11.5 2.5 %collective-permute-start.4 = (bf16[512,128]{1,0:T(8,128)(2,1)S(1)}, bf16[512,128]{1,0:T(8,128)(2,1)S(1)}, u32[]{:S(2)}, u32[]{:S(2)}) collective-permute-start(bf16[512,128]{1,0:T(8,128)(2,1)S(1)} %copy.17), channel_id=1, source_target_pairs={{0,6},{1,7},{2,4},{3,5},{4,2},{5,3},{6,0},{7,1},{8,14},{9,15},{10,... | collective-permute-start | bytes 393224 | tf_op jit(solution)/shard_map/ppermute | solution.py:29
  14.0 0.5 %collective-permute-start.6 = (bf16[512,128]{1,0:T(8,128)(2,1)S(1)}, bf16[512,128]{1,0:T(8,128)(2,1)S(1)}, u32[]{:S(2)}, u32[]{:S(2)}) collective-permute-start(bf16[512,128]{1,0:T(8,128)(2,1)S(1)} %copy.16.value), channel_id=1, source_target_pairs={{0,4},{1,5},{2,6},{3,7},{4,0},{5,1},{6,2},{7,3},{8,12},{9,13},{10,... | collective-permute-start | bytes 393224 | tf_op jit(solution)/shard_map/ppermute | solution.py:29
  14.5 0.5 %collective-permute-start.5 = (bf16[512,128]{1,0:T(8,128)(2,1)S(1)}, bf16[512,128]{1,0:T(8,128)(2,1)S(1)}, u32[]{:S(2)}, u32[]{:S(2)}) collective-permute-start(bf16[512,128]{1,0:T(8,128)(2,1)S(1)} %pad_maximum_fusion.value.refs_0_), channel_id=1, source_target_pairs={{0,2},{1,3},{2,0},{3,1},{4,6},{5,7},{6,4},{7,5},{8,10},{9,11},{10,... | collective-permute-start | bytes 393224 | tf_op jit(solution)/shard_map/ppermute | solution.py:29
  15.1 0.0 copy-done.2
  15.1 0.0 collective-permute-start.3
  15.1 0.0 copy-start.3
  15.1 0.0 copy-start.5
  15.1 0.0 copy-done
  15.1 0.0 copy-done.1
  15.1 0.0 copy-done.4
  15.1 0.6 %copy-done.3 = f32[256]{0:T(256)S(1)} copy-done((f32[256]{0:T(256)S(1)}, f32[256]{0:T(256)}, u32[]{:S(2)}) %copy-start.3) | copy-done | bytes 1048
  15.8 0.0 copy-done.5
  15.8 1.4 %place.1 = (bf16[16,256,128]{2,1,0:T(8,128)(2,1)S(1)}, bf16[256,128]{1,0:T(8,128)(2,1)S(1)}, f32[256,128]{1,0:T(8,128)S(1)}) custom-call(s32[1,4]{1,0:T(1,128)S(1)} %copy-done.5, s32[4,16]{1,0:T(4,128)S(1)} %bitcast.8, bf16[4,16,4096]{2,1,0:T(8,128)(2,1)S(1)} %bitcast.5, bf16[128,256]{1,0:T(8,128)(2,1)S(1)} %copy-done.1, f32[1,256]{1,0:T(1,128)S(1)} %bitcast.6), custom_call_target="tpu_custom_call" | custom-call | tf_op jit(solution)/shard_map/place/pallas_call | solution.py:135
  17.1 0.0 collective-permute-done.3.other
  17.1 0.3 turn.1.cot_t
  17.4 1.4 %collective-permute-done.4.refs_1_ = bf16[512,128]{1,0:T(8,128)(2,1)S(1)} collective-permute-done((bf16[512,128]{1,0:T(8,128)(2,1)S(1)}, bf16[512,128]{1,0:T(8,128)(2,1)S(1)}, u32[]{:S(2)}, u32[]{:S(2)}) %collective-permute-start.4) | collective-permute-done | bytes 131104 | tf_op jit(solution)/shard_map/ppermute | solution.py:29
  18.9 0.3 block_sum.2.refs_0_
  19.2 0.5 %collective-permute-done.6.refs_2_ = bf16[512,128]{1,0:T(8,128)(2,1)S(1)} collective-permute-done((bf16[512,128]{1,0:T(8,128)(2,1)S(1)}, bf16[512,128]{1,0:T(8,128)(2,1)S(1)}, u32[]{:S(2)}, u32[]{:S(2)}) %collective-permute-start.6) | collective-permute-done | bytes 131104 | tf_op jit(solution)/shard_map/ppermute | solution.py:29
  19.6 0.0 collective-permute-done.5.refs_1_
  19.6 0.3 block_sum.3.mine
  19.9 0.1 collective-permute-start.7
  20.0 1.3 %collective-permute-done.7.other = f32[256,128]{1,0:T(8,128)S(1)} collective-permute-done((f32[256,128]{1,0:T(8,128)S(1)}, f32[256,128]{1,0:T(8,128)S(1)}, u32[]{:S(2)}, u32[]{:S(2)}) %collective-permute-start.7) | collective-permute-done | bytes 131104 | tf_op jit(solution)/shard_map/ppermute | solution.py:29
  21.3 0.4 %layer.1 = (bf16[16,32,128]{2,1,0:T(8,128)(2,1)S(1)}, bf16[128,256]{1,0:T(8,128)(2,1)S(1)}) custom-call(f32[256,128]{1,0:T(8,128)S(1)} %block_sum.3.mine, f32[256,128]{1,0:T(8,128)S(1)} %collective-permute-done.7.other, bf16[128,256]{1,0:T(8,128)(2,1)S(1)} %copy-done.1, f32[1,256]{1,0:T(1,128)S(1)} %bitcast.7, ...), custom_call_target="tpu_custom_call" | custom-call | tf_op jit(solution)/shard_map/layer/pallas_call | solution.py:241
  21.8 11.8 %all_to_all.5.got = bf16[16,32,128]{2,1,0:T(8,128)(2,1)S(1)} all-to-all(bf16[16,32,128]{2,1,0:T(8,128)(2,1)S(1)} %get-tuple-element.25), channel_id=1, replica_groups=mesh['rows'=16,'rep'=2] {'rows'}, dimensions={0} | all-to-all | bytes 262144 | tf_op jit(solution)/shard_map/all_to_all | solution.py:308
  33.6 0.6 %finish.1 = (bf16[128,256]{1,0:T(8,128)(2,1)}, f32[16,128]{1,0:T(8,128)}, f32[1,16]{1,0:T(1,128)}) custom-call(bf16[128,256]{1,0:T(8,128)(2,1)S(1)} %get-tuple-element.24.act_in, bf16[16,32,128]{2,1,0:T(8,128)(2,1)S(1)} %all_to_all.5.got), custom_call_target="tpu_custom_call" | custom-call | tf_op jit(solution)/shard_map/finish/pallas_call | solution.py:268
  (5 shorter events, 0.0 us)
Async XLA Ops:
  0.6 14.5 %copy-start = (bf16[1,4,16,4096]{3,2,1,0:T(8,128)(2,1)S(1)}, bf16[1,4,16,4096]{3,2,1,0:T(8,128)(2,1)}, u32[]{:S(2)}) copy-start(bf16[1,4,16,4096]{3,2,1,0:T(8,128)(2,1)} %param.12) | copy-start | bytes 1572868
  1.5 7.0 %collective-permute-start.2 = (bf16[128,128]{1,0:T(8,128)(2,1)S(1)}, bf16[128,128]{1,0:T(8,128)(2,1)S(1)}, u32[]{:S(2)}, u32[]{:S(2)}) collective-permute-start(bf16[128,128]{1,0:T(8,128)(2,1)S(1)} %copy.15), channel_id=1, source_target_pairs={{0,24},{1,25},{2,26},{3,27},{4,28},{5,29},{6,30},{7,31},{8,16},{9,... | collective-permute-start | bytes 98312 | tf_op jit(solution)/shard_map/ppermute | solution.py:29
  6.6 4.8 %collective-permute-start.1 = (bf16[128,128]{1,0:T(8,128)(2,1)S(1)}, bf16[128,128]{1,0:T(8,128)(2,1)S(1)}, u32[]{:S(2)}, u32[]{:S(2)}) collective-permute-start(bf16[128,128]{1,0:T(8,128)(2,1)S(1)} %copy.14.value), channel_id=1, source_target_pairs={{0,16},{1,17},{2,18},{3,19},{4,20},{5,21},{6,22},{7,23},{8,24},{9,... | collective-permute-start | bytes 98312 | tf_op jit(solution)/shard_map/ppermute | solution.py:29
  6.6 4.8 %collective-permute-start = (bf16[128,128]{1,0:T(8,128)(2,1)S(1)}, bf16[128,128]{1,0:T(8,128)(2,1)S(1)}, u32[]{:S(2)}, u32[]{:S(2)}) collective-permute-start(bf16[128,128]{1,0:T(8,128)(2,1)S(1)} %own_half.1.value), channel_id=1, source_target_pairs={{0,8},{1,9},{2,10},{3,11},{4,12},{5,13},{6,14},{7,15},{8,0},{9,1},... | collective-permute-start | bytes 98312 | tf_op jit(solution)/shard_map/ppermute | solution.py:29
  11.5 3.6 %copy-start.2 = (bf16[128,256]{1,0:T(8,128)(2,1)S(1)}, bf16[128,256]{1,0:T(8,128)(2,1)}, u32[]{:S(2)}) copy-start(bf16[128,256]{1,0:T(8,128)(2,1)} %mine) | copy-start | bytes 196612
  11.5 3.6 %copy-start.1 = (bf16[128,256]{1,0:T(8,128)(2,1)S(1)}, bf16[128,256]{1,0:T(8,128)(2,1)}, u32[]{:S(2)}) copy-start(bf16[128,256]{1,0:T(8,128)(2,1)} %weight.3) | copy-start | bytes 196612
  11.5 3.6 %copy-start.4 = (s32[1,4,16]{2,1,0:T(4,128)S(1)}, s32[1,4,16]{2,1,0:T(4,128)}, u32[]{:S(2)}) copy-start(s32[1,4,16]{2,1,0:T(4,128)} %param.11) | copy-start | bytes 772
  11.5 7.3 %collective-permute-start.4 = (bf16[512,128]{1,0:T(8,128)(2,1)S(1)}, bf16[512,128]{1,0:T(8,128)(2,1)S(1)}, u32[]{:S(2)}, u32[]{:S(2)}) collective-permute-start(bf16[512,128]{1,0:T(8,128)(2,1)S(1)} %copy.17), channel_id=1, source_target_pairs={{0,6},{1,7},{2,4},{3,5},{4,2},{5,3},{6,0},{7,1},{8,14},{9,15},{10,... | collective-permute-start | bytes 393224 | tf_op jit(solution)/shard_map/ppermute | solution.py:29
  14.0 5.6 %collective-permute-start.6 = (bf16[512,128]{1,0:T(8,128)(2,1)S(1)}, bf16[512,128]{1,0:T(8,128)(2,1)S(1)}, u32[]{:S(2)}, u32[]{:S(2)}) collective-permute-start(bf16[512,128]{1,0:T(8,128)(2,1)S(1)} %copy.16.value), channel_id=1, source_target_pairs={{0,4},{1,5},{2,6},{3,7},{4,0},{5,1},{6,2},{7,3},{8,12},{9,13},{10,... | collective-permute-start | bytes 393224 | tf_op jit(solution)/shard_map/ppermute | solution.py:29
  14.5 5.1 %collective-permute-start.5 = (bf16[512,128]{1,0:T(8,128)(2,1)S(1)}, bf16[512,128]{1,0:T(8,128)(2,1)S(1)}, u32[]{:S(2)}, u32[]{:S(2)}) collective-permute-start(bf16[512,128]{1,0:T(8,128)(2,1)S(1)} %pad_maximum_fusion.value.refs_0_), channel_id=1, source_target_pairs={{0,2},{1,3},{2,0},{3,1},{4,6},{5,7},{6,4},{7,5},{8,10},{9,11},{10,... | collective-permute-start | bytes 393224 | tf_op jit(solution)/shard_map/ppermute | solution.py:29
  15.1 2.1 %collective-permute-start.3 = (bf16[128,256]{1,0:T(8,128)(2,1)S(1)}, bf16[128,256]{1,0:T(8,128)(2,1)S(1)}, u32[]{:S(2)}, u32[]{:S(2)}) collective-permute-start(bf16[128,256]{1,0:T(8,128)(2,1)S(1)} %copy-done.2), channel_id=1, source_target_pairs={{0,1},{1,0},{2,3},{3,2},{4,5},{5,4},{6,7},{7,6},{8,9},{9,8},{10,11... | collective-permute-start | bytes 196616 | tf_op jit(solution)/shard_map/ppermute | solution.py:29
  15.1 0.7 %copy-start.3 = (f32[256]{0:T(256)S(1)}, f32[256]{0:T(256)}, u32[]{:S(2)}) copy-start(f32[256]{0:T(256)} %param.9) | copy-start | bytes 3076
  15.1 0.7 %copy-start.5 = (s32[1,4]{1,0:T(1,128)S(1)}, s32[1,4]{1,0:T(1,128)}, u32[]{:S(2)}) copy-start(s32[1,4]{1,0:T(1,128)} %counts.1) | copy-start | bytes 52
  19.9 1.4 %collective-permute-start.7 = (f32[256,128]{1,0:T(8,128)S(1)}, f32[256,128]{1,0:T(8,128)S(1)}, u32[]{:S(2)}, u32[]{:S(2)}) collective-permute-start(f32[256,128]{1,0:T(8,128)S(1)} %block_sum.3.mine), channel_id=1, source_target_pairs={{0,1},{1,0},{2,3},{3,2},{4,5},{5,4},{6,7},{7,6},{8,9},{9,8},{10,11... | collective-permute-start | bytes 393224 | tf_op jit(solution)/shard_map/ppermute | solution.py:29
